TPU v7x, 512 devices: a whole 4x4x16 slice. The times are simulated.
512 devices in a mesh: freq: 128 (over z, x, core), rcv: 4 (over y).
Axes of the slice: x: 4, y: 4, z: 16, core: 2. Of those that a mesh axis runs over, the one named last changes fastest.
Arguments:
- recorded: float32 [1024, 64, 1024], P(('rcv', 'freq')), may hold values from -32 to 32
- kernel: bfloat16 [256, 1024, 2, 1024], P('freq', None, None, 'rcv'), may hold values from -0.125 to 0.125
- freq_index: int32 [256], replicated, may hold values from 1 to 511, as said below
Outputs:
- solution: float32 [1024, 64, 1024], P(('rcv', 'freq'))
- normal_residual: float32 [1024, 64, 1024], P(('rcv', 'freq'))
Inputs may be any that keep to these rules, and one draw needn't show every extreme that they name: `freq_index`: 256 distinct values; both 1 and 511 appear.
All inputs are finite; a program needn't handle non-finite values.
Results may differ from a plain program's by a relative error of at most 0.017.
Values may be sent and summed in bfloat16 or wider, within the bound.
No kernel may reach another device: no remote copies, remote signals or barrier semaphores. Data moves between devices by JAX's collectives and lax.ppermute only.
A program may use at most 64 MiB of HBM per device.

v0:
```python
import jax
import jax.numpy as jnp
from jax import lax
from jax.sharding import PartitionSpec as P

ITERS = 2


HIGH = lax.Precision.HIGHEST


def dft_table(freq_index, samples):
    times = jnp.arange(samples, dtype=jnp.int32)
    phase = freq_index[:, None] * times[None, :] % samples
    angle = 2.0 * jnp.pi / samples * phase.astype(jnp.float32)
    factor = 1.0 / jnp.sqrt(jnp.float32(samples))
    return jnp.stack([jnp.cos(angle) * factor, -jnp.sin(angle) * factor])


def to_spectrum(table, field):
    spectrum = jnp.einsum("pkt,rvt->krpv", table, field, precision=HIGH)
    return spectrum.reshape(spectrum.shape[0], spectrum.shape[1], -1)


def to_traces(table, spectrum):
    rows, kept, width = spectrum.shape
    split = spectrum.reshape(rows, kept, 2, width // 2)
    return jnp.einsum("rkpv,pkt->rvt", split, table, precision=HIGH)


def global_norm(field):
    return jnp.sqrt(lax.psum(jnp.sum(field * field), ("freq", "rcv")))


def rotate(solution, direction, right_vec, diag_est, residual_est, beta_norm, alpha_norm):
    rotation_norm = jnp.sqrt(diag_est * diag_est + beta_norm * beta_norm)
    cos_term = diag_est / rotation_norm
    sin_term = beta_norm / rotation_norm
    coupling = sin_term * alpha_norm
    diag_next = -cos_term * alpha_norm
    step_weight = cos_term * residual_est
    residual_next = sin_term * residual_est
    solution = solution + step_weight / rotation_norm * direction
    direction = right_vec - coupling / rotation_norm * direction
    return (solution, direction, diag_next, residual_next)


def body(recorded, kernel, freq_index):
    table = dft_table(freq_index, recorded.shape[2])
    freq_share, sources, _, recv_share = kernel.shape
    kernel_flat = kernel.reshape(freq_share, sources, 2 * recv_share)

    def forward_rest(rounded):
        half = rounded.shape[2] // 2
        turned = jnp.concatenate([-rounded[:, :, half:], rounded[:, :, :half]], axis=2)
        stacked = jnp.concatenate([rounded, turned], axis=1)
        summed = lax.psum_scatter(
            jnp.einsum("fsq,fqw->sfw", kernel_flat, stacked, preferred_element_type=jnp.float32),
            "rcv",
            scatter_dimension=0,
            tiled=True,
        )
        back = lax.all_to_all(summed, "freq", split_axis=0, concat_axis=1, tiled=True)
        return to_traces(table, back)

    def adjoint_rest(rounded):
        half = rounded.shape[2] // 2
        product = jnp.einsum(
            "fsq,fsw->qfw",
            kernel_flat,
            lax.all_gather(rounded, "rcv", axis=1, tiled=True),
            preferred_element_type=jnp.float32,
        )
        real_part = product[:recv_share, :, :half] + product[recv_share:, :, half:]
        imag_part = product[:recv_share, :, half:] - product[recv_share:, :, :half]
        combined = jnp.concatenate([real_part, imag_part], axis=2)
        back = lax.all_to_all(combined, "freq", split_axis=0, concat_axis=1, tiled=True)
        return to_traces(table, back)

    def normalized_apply(raw, operator):
        length = global_norm(raw)
        scaled = to_spectrum(table, raw / length).astype(jnp.bfloat16)
        spectrum = lax.all_to_all(scaled, "freq", split_axis=0, concat_axis=1, tiled=True)
        return (operator(spectrum), length, raw / length)

    right_raw, beta_norm, left_vec = normalized_apply(recorded, adjoint_rest)
    residual_est = beta_norm
    solution = jnp.zeros_like(right_raw)
    direction = solution
    diag_est = beta_norm
    for step in range(ITERS):
        image, alpha_norm, right_vec = normalized_apply(right_raw, forward_rest)
        if step == 0:
            diag_est = alpha_norm
            direction = right_vec
        else:
            solution, direction, diag_est, residual_est = rotate(
                solution, direction, right_vec, diag_est, residual_est, beta_norm, alpha_norm
            )
        left_raw = image - alpha_norm * left_vec
        back_image, beta_norm, left_vec = normalized_apply(left_raw, adjoint_rest)
        right_raw = back_image - beta_norm * right_vec
    alpha_norm = global_norm(right_raw)
    right_vec = right_raw / alpha_norm
    solution, direction, diag_est, residual_est = rotate(
        solution, direction, right_vec, diag_est, residual_est, beta_norm, alpha_norm
    )
    return (solution, residual_est * diag_est * right_vec)


def solution(mesh):
    in_specs = (P(("rcv", "freq"), None, None), P("freq", None, None, "rcv"), P())
    out_specs = (P(("rcv", "freq"), None, None), P(("rcv", "freq"), None, None))
    return jax.shard_map(body, mesh=mesh, in_specs=in_specs, out_specs=out_specs, check_vma=False)
```

profile of v0, /device:TPU:1, one launch (start us, length us, event | category | flops | bytes accessed | tf_op | source)
XLA Modules:
  0.0 1065.6 jit_solution(3370125316620646361)
XLA Ops:
  7.2 1.8 multiply_reduce_fusion.5
  9.0 4.9 cosine_multiply_fusion
  14.0 111.0 %psum.42 = f32[]{:T(128)} all-reduce(f32[]{:T(128)} %multiply_reduce_fusion.5), channel_id=1, replica_groups=mesh['freq'=128,'rcv'=4] {'freq','rcv'}, use_global_device_ids=true, to_apply=%region_1.2 | all-reduce | flops 1 | bytes 8 | tf_op jit(solution)/shard_map/psum | solution.py:32
  125.7 2.2 convolution_convert_fusion.4
  128.7 10.3 all-to-all-start
  139.1 3.2 reshape.139
  142.2 12.8 %all-to-all-done = bf16[256,2,128]{2,1,0:T(2,128)(2,1)S(1)} async-done(((bf16[256,2,128]{2,1,0:T(2,128)(2,1)}), bf16[256,2,128]{2,1,0:T(2,128)(2,1)S(1)}, u32[]{:S(2)}, u32[]{:S(2)}) %all-to-all-start) | async-done | bytes 131104 | tf_op jit(solution)/shard_map/all_to_all | solution.py:83
  155.4 9.9 all_gather.9
  165.8 0.8 copy.53
  166.6 31.1 %all_to_all.165 = f32[256,2,128]{2,1,0:T(2,128)S(1)} all-to-all(f32[256,2,128]{2,1,0:T(2,128)} %copy.53), channel_id=1, replica_groups=mesh['freq'=128,'rcv'=4] {'freq'}, dimensions={0} | all-to-all | bytes 524288 | tf_op jit(solution)/shard_map/all_to_all | solution.py:77
  197.9 1.3 reshape.140
  199.2 4.2 multiply_reduce_fusion.4
  203.4 101.3 %psum.43 = f32[]{:T(128)} all-reduce(f32[]{:T(128)} %get-tuple-element.14), channel_id=1, replica_groups=mesh['freq'=128,'rcv'=4] {'freq','rcv'}, use_global_device_ids=true, to_apply=%region_3.4 | all-reduce | flops 1 | bytes 8 | tf_op jit(solution)/shard_map/psum | solution.py:32
  305.3 3.6 convolution_convert_fusion.3
  309.1 25.2 %all_to_all.166 = bf16[256,2,128]{2,1,0:T(2,128)(2,1)S(1)} all-to-all(bf16[256,2,128]{2,1,0:T(2,128)(2,1)S(1)} %copy.57), channel_id=1, replica_groups=mesh['freq'=128,'rcv'=4] {'freq'}, dimensions={0} | all-to-all | bytes 262144 | tf_op jit(solution)/shard_map/all_to_all | solution.py:83
  334.6 1.8 convolution_bitcast_fusion.1
  336.5 19.4 %reduce-scatter.3.cloned.1.call-done = f32[256,2,128]{0,2,1:T(8,128)} async-done(((f32[1024,2,128]{0,2,1:T(8,128)}), f32[256,2,128]{0,2,1:T(8,128)}) %reduce-scatter.3.cloned.1.call-update) | async-done | bytes 262160 | tf_op jit(solution)/shard_map/reduce_scatter | solution.py:57
  355.9 1.1 copy.63
  357.0 38.4 %all_to_all.167 = f32[256,2,128]{2,1,0:T(2,128)S(1)} all-to-all(f32[256,2,128]{2,1,0:T(2,128)S(1)} %copy.63), channel_id=1, replica_groups=mesh['freq'=128,'rcv'=4] {'freq'}, dimensions={0} | all-to-all | bytes 524288 | tf_op jit(solution)/shard_map/all_to_all | solution.py:63
  395.6 1.3 reshape.141
  396.9 4.3 multiply_reduce_fusion.3
  401.2 101.3 %psum.44 = f32[]{:T(128)} all-reduce(f32[]{:T(128)} %get-tuple-element.16), channel_id=1, replica_groups=mesh['freq'=128,'rcv'=4] {'freq','rcv'}, use_global_device_ids=true, to_apply=%region_6.7 | all-reduce | flops 1 | bytes 8 | tf_op jit(solution)/shard_map/psum | solution.py:32
  503.3 3.6 convolution_convert_fusion.2
  507.0 25.2 %all_to_all.168 = bf16[256,2,128]{2,1,0:T(2,128)(2,1)S(1)} all-to-all(bf16[256,2,128]{2,1,0:T(2,128)(2,1)S(1)} %copy.67), channel_id=1, replica_groups=mesh['freq'=128,'rcv'=4] {'freq'}, dimensions={0} | all-to-all | bytes 262144 | tf_op jit(solution)/shard_map/all_to_all | solution.py:83
  532.4 9.9 all_gather.10
  542.9 0.8 copy.71
  543.7 30.8 %all_to_all.169 = f32[256,2,128]{2,1,0:T(2,128)S(1)} all-to-all(f32[256,2,128]{2,1,0:T(2,128)} %copy.71), channel_id=1, replica_groups=mesh['freq'=128,'rcv'=4] {'freq'}, dimensions={0} | all-to-all | bytes 524288 | tf_op jit(solution)/shard_map/all_to_all | solution.py:77
  574.7 1.3 reshape.142
  576.0 4.3 multiply_reduce_fusion.2
  580.3 101.7 %psum.45 = f32[]{:T(128)} all-reduce(f32[]{:T(128)} %get-tuple-element.18), channel_id=1, replica_groups=mesh['freq'=128,'rcv'=4] {'freq','rcv'}, use_global_device_ids=true, to_apply=%region_8.9 | all-reduce | flops 1 | bytes 8 | tf_op jit(solution)/shard_map/psum | solution.py:32
  682.7 3.6 convolution_convert_fusion.1
  686.4 25.2 %all_to_all.170 = bf16[256,2,128]{2,1,0:T(2,128)(2,1)S(1)} all-to-all(bf16[256,2,128]{2,1,0:T(2,128)(2,1)S(1)} %copy.75), channel_id=1, replica_groups=mesh['freq'=128,'rcv'=4] {'freq'}, dimensions={0} | all-to-all | bytes 262144 | tf_op jit(solution)/shard_map/all_to_all | solution.py:83
  711.9 1.8 convolution_bitcast_fusion
  713.8 19.5 %reduce-scatter.5.cloned.1.call-done = f32[256,2,128]{0,2,1:T(8,128)} async-done(((f32[1024,2,128]{0,2,1:T(8,128)}), f32[256,2,128]{0,2,1:T(8,128)}) %reduce-scatter.5.cloned.1.call-update) | async-done | bytes 262160 | tf_op jit(solution)/shard_map/reduce_scatter | solution.py:57
  733.3 1.1 copy.81
  734.4 38.2 %all_to_all.171 = f32[256,2,128]{2,1,0:T(2,128)S(1)} all-to-all(f32[256,2,128]{2,1,0:T(2,128)S(1)} %copy.81), channel_id=1, replica_groups=mesh['freq'=128,'rcv'=4] {'freq'}, dimensions={0} | all-to-all | bytes 524288 | tf_op jit(solution)/shard_map/all_to_all | solution.py:63
  772.9 1.3 reshape.143
  774.1 4.3 multiply_reduce_fusion.1
  778.4 101.3 %psum.46 = f32[]{:T(128)} all-reduce(f32[]{:T(128)} %get-tuple-element.20), channel_id=1, replica_groups=mesh['freq'=128,'rcv'=4] {'freq','rcv'}, use_global_device_ids=true, to_apply=%region_11.12 | all-reduce | flops 1 | bytes 8 | tf_op jit(solution)/shard_map/psum | solution.py:32
  880.4 3.6 convolution_convert_fusion
  884.1 25.4 %all_to_all.172 = bf16[256,2,128]{2,1,0:T(2,128)(2,1)S(1)} all-to-all(bf16[256,2,128]{2,1,0:T(2,128)(2,1)S(1)} %copy.85), channel_id=1, replica_groups=mesh['freq'=128,'rcv'=4] {'freq'}, dimensions={0} | all-to-all | bytes 262144 | tf_op jit(solution)/shard_map/all_to_all | solution.py:83
  909.8 9.9 all_gather.11
  921.1 10.5 all-to-all-start.9
  931.9 2.0 multiply_add_fusion
  933.9 18.1 %all-to-all-done.9 = f32[256,2,128]{2,1,0:T(2,128)S(1)} async-done(((f32[256,2,128]{2,1,0:T(2,128)}), f32[256,2,128]{2,1,0:T(2,128)S(1)}, u32[]{:S(2)}, u32[]{:S(2)}) %all-to-all-start.9) | async-done | bytes 262176 | tf_op jit(solution)/shard_map/all_to_all | solution.py:77
  952.7 3.1 multiply_reduce_fusion
  955.8 101.3 %psum.47 = f32[]{:T(128)} all-reduce(f32[]{:T(128)} %get-tuple-element.22), channel_id=1, replica_groups=mesh['freq'=128,'rcv'=4] {'freq','rcv'}, use_global_device_ids=true, to_apply=%region_13.14 | all-reduce | flops 1 | bytes 8 | tf_op jit(solution)/shard_map/psum | solution.py:32
  1057.7 0.9 divide_multiply_fusion
  (55 shorter events, 6.7 us)
Async XLA Ops:
  7.2 118.5 %copy-start.3 = (f32[2,64,1024]{2,1,0:T(8,128)S(1)}, f32[2,64,1024]{2,1,0:T(8,128)}, u32[]{:S(2)}) copy-start(f32[2,64,1024]{2,1,0:T(8,128)} %param.3) | copy-start | bytes 1572868
  13.9 114.8 %copy-start = (f32[1,256,1024]{2,1,0:T(8,128)}, f32[1,256,1024]{2,1,0:T(8,128)S(1)}, u32[]{:S(2)}) copy-start(f32[1,256,1024]{2,1,0:T(8,128)S(1)} %get-tuple-element.13) | copy-start | bytes 3145732
  128.7 26.3 %all-to-all-start = ((bf16[256,2,128]{2,1,0:T(2,128)(2,1)}), bf16[256,2,128]{2,1,0:T(2,128)(2,1)S(1)}, u32[]{:S(2)}, u32[]{:S(2)}) async-start(bf16[256,2,128]{2,1,0:T(2,128)(2,1)} %copy.49), calls=%async_computation | async-start | bytes 262144 | tf_op jit(solution)/shard_map/all_to_all | solution.py:83
  139.0 216.9 %reduce-scatter.3.cloned.1.call-start = ((), (), s32[]{:S(2)}) async-start(), calls=%async_computation.12 | async-start | bytes 1310720 | tf_op jit(solution)/shard_map/reduce_scatter | solution.py:57
  336.4 396.9 %reduce-scatter.5.cloned.1.call-start = ((), (), s32[]{:S(2)}) async-start(), calls=%async_computation.13 | async-start | bytes 1310720 | tf_op jit(solution)/shard_map/reduce_scatter | solution.py:57
  920.1 11.8 %copy-start.2 = (f32[2,64,1024]{2,1,0:T(8,128)S(1)}, f32[2,64,1024]{2,1,0:T(8,128)}, u32[]{:S(2)}) copy-start(f32[2,64,1024]{2,1,0:T(8,128)} %get-tuple-element.15) | copy-start | bytes 1572868
  921.0 31.6 %copy-start.1 = (f32[1,256,1024]{2,1,0:T(8,128)S(1)}, f32[1,256,1024]{2,1,0:T(8,128)}, u32[]{:S(2)}) copy-start(f32[1,256,1024]{2,1,0:T(8,128)} %copy-done) | copy-start | bytes 3145732
  921.1 30.9 %all-to-all-start.9 = ((f32[256,2,128]{2,1,0:T(2,128)}), f32[256,2,128]{2,1,0:T(2,128)S(1)}, u32[]{:S(2)}, u32[]{:S(2)}) async-start(f32[256,2,128]{2,1,0:T(2,128)} %copy.89), calls=%async_computation.11 | async-start | bytes 524288 | tf_op jit(solution)/shard_map/all_to_all | solution.py:77
Sparse Core Ops, SparseCore 0:
  336.5 19.3 reduce-scatter.2
  713.9 19.3 reduce-scatter.4
where the time goes:
time: 1080 us; the launch traced here: 1070 us
  blocking collectives  887 us (82%)
  waiting for transfers between devices  70 us (6%)
  matrix products  42 us (4%)
  starting transfers between devices  20.8 us (2%)
  between operations  19.2 us (2%)
  local copies, waits for them, and re-layouts  17.1 us (2%)
    psum x6, blocking collectives, global_norm(): return jnp.sqrt(lax.psum(jnp.sum(field * field), ('freq', 'rcv')))  618 us
    all_to_all x4, blocking collectives, normalized_apply(): lax.all_to_all(scaled, 'freq', split_axis=0, concat_axis=1, tiled=True)  101 us
    all_to_all x2, blocking collectives, forward_rest(): lax.all_to_all(summed, 'freq', split_axis=0, concat_axis=1, tiled=True)  76.6 us
    all_to_all x2, blocking collectives, adjoint_rest(): lax.all_to_all(combined, 'freq', split_axis=0, concat_axis=1, tiled=True)  61.9 us
    reduce_scatter x2, waiting for transfers between devices, forward_rest(): lax.psum_scatter(jnp.einsum('fsq,fqw->sfw', kernel_flat, stacked, preferr...  39 us
    all_gather x3, blocking collectives, adjoint_rest(): lax.all_gather(rounded, 'rcv', axis=1, tiled=True)  29.7 us
  transfers between devices with their start and end apart: 4, of which 4 were waited for; matrix products, arithmetic and copies ran while one was open for 0% of the time, Pallas kernels for 0%

commit v1 on v0

v1 whole, which is shorter than its diff:
```python
import functools
import math

import jax
import jax.numpy as jnp
from jax import lax
from jax.experimental import pallas as pl
from jax.experimental.pallas import tpu as pltpu
from jax.sharding import PartitionSpec as P

Y = 4
HV = 32
HIGH = lax.Precision.HIGHEST
MIB = 1024 * 1024


def dft_kernel(fr_ref, rec_ref, tab_ref, out_ref, norm_ref):
    kept = fr_ref.shape[0]
    samples = rec_ref.shape[1]
    chunks = samples // 128
    unit = 2.0 * math.pi / samples
    fr = fr_ref[...]
    lane = lax.broadcasted_iota(jnp.int32, (kept, 128), 1)
    fine = (fr * lane & (samples - 1)).astype(jnp.float32) * unit
    coarse = (fr * (lane * 128) & (samples - 1)).astype(jnp.float32) * unit
    cos_f, sin_f = jnp.cos(fine), jnp.sin(fine)
    factor = 1.0 / math.sqrt(samples)
    cos_c, sin_c = jnp.cos(coarse) * factor, jnp.sin(coarse) * factor
    for a in range(chunks):
        ca, sa = cos_c[:, a : a + 1], sin_c[:, a : a + 1]
        tab_ref[0, :, a * 128 : (a + 1) * 128] = ca * cos_f - sa * sin_f
        tab_ref[1, :, a * 128 : (a + 1) * 128] = -(sa * cos_f + ca * sin_f)
    rec = rec_ref[...]
    norm_ref[...] = jnp.sum(rec * rec, axis=(0, 1), keepdims=True)
    spec = [
        lax.dot_general(
            tab_ref[p], rec, (((1,), (1,)), ((), ())), precision=HIGH, preferred_element_type=jnp.float32
        )
        for p in range(2)
    ]
    for c in range(2):
        parts = [spec[p][:, (2 * src + c) * HV : (2 * src + c + 1) * HV] for src in range(2) for p in range(2)]
        out_ref[c] = jnp.concatenate(parts, axis=1).astype(jnp.bfloat16)


def quarter_turn(x):
    width = x.shape[1]
    even = lax.broadcasted_iota(jnp.int32, x.shape, 1) % 2 == 0
    return jnp.where(even, pltpu.roll(x, width - 1, 1), -pltpu.roll(x, 1, 1))


def length_of(x):
    return jnp.sqrt(jnp.sum(x * x, axis=(0, 1), keepdims=True))


def inverse_of(x):
    return jnp.where(x > 1e-30, 1.0 / jnp.maximum(x, 1e-30), 0.0)


def krylov_kernel(idx_ref, norm_ref, *refs):
    u_refs, k_refs, g_refs = refs[:4], refs[4:12], refs[12:16]
    kmat, u_rows, u_all, q_rows, g_rows, sems = refs[16:]
    devices = u_refs[0].shape[0]
    half = devices // 2
    y, core = idx_ref[0], idx_ref[1]

    copies = []
    for j in range(8):
        side = core if j < 4 else 1 - core
        start = pl.multiple_of(side * (4 * devices) + (j % 4) * devices, devices)
        copies.append(pltpu.make_async_copy(k_refs[j], kmat.at[:, pl.ds(start, devices)], sems.at[j]))
    for copy in copies:
        copy.start()

    for o in range(4):
        block = u_refs[o][...].astype(jnp.float32)
        for g in range(4):
            u_rows[pl.ds(g, devices, stride=4), 0:HV] = block[:, g * HV : (g + 1) * HV]
        turned = u_rows[...].T[0:HV]
        start = pl.multiple_of(lax.rem(y + 4 - o, 4) * (4 * devices), 4 * devices)
        u_all[:, pl.ds(start, 4 * devices)] = turned

    for copy in copies:
        copy.wait()

    def adjoint(p):
        both = jnp.concatenate([p, quarter_turn(p)], axis=0).astype(jnp.bfloat16)
        return 0.5 * jnp.dot(both, kmat[...], preferred_element_type=jnp.float32)

    def forward(q):
        w = lax.dot_general(
            q.astype(jnp.bfloat16), kmat[...], (((1,), (1,)), ((), ())), preferred_element_type=jnp.float32
        )
        return 0.5 * (w[:HV] - quarter_turn(w[HV:]))

    u = u_all[...]
    length = length_of(u)
    scale = inverse_of(length)
    g1 = adjoint(u) * scale
    a1 = length_of(g1)
    q1 = g1 * inverse_of(a1)
    h2 = forward(q1) - (a1 * scale) * u
    b2 = length_of(h2)
    p2 = h2 * inverse_of(b2)
    g2 = adjoint(p2) - b2 * q1
    a2 = length_of(g2)
    q2 = g2 * inverse_of(a2)
    h3 = forward(q2) - a2 * p2
    b3 = length_of(h3)
    p3 = h3 * inverse_of(b3)
    g3 = adjoint(p3) - b3 * q2
    a3 = length_of(g3)
    q3 = g3 * inverse_of(a3)

    lane = lax.broadcasted_iota(jnp.int32, (1, 128), 1)
    slot = lane % 8
    values = jnp.zeros((1, 128), jnp.float32)
    for n, value in enumerate((math.sqrt(2.0) * length, a1, b2, a2, b3, a3, norm_ref[...])):
        values = jnp.where(slot == n, value, values)
    hi = values.astype(jnp.bfloat16).astype(jnp.float32)
    rest = values - hi
    mid = rest.astype(jnp.bfloat16).astype(jnp.float32)
    low = rest - mid
    scalars = jnp.where(lane < 8, hi, jnp.where(lane < 16, mid, jnp.where(lane < 24, low, 0.0)))

    for o in range(4):
        g_rows[o, pl.ds(3, devices, stride=4), :] = jnp.broadcast_to(scalars, (devices, 128))
    for pair in range(2):
        first, second = ((q1, q2), (q3, q3))[pair]
        q_rows[...] = jnp.concatenate([first, second], axis=0).T
        even = q_rows[pl.ds(0, 4 * devices, stride=2), :]
        odd = q_rows[pl.ds(1, 4 * devices, stride=2), :]
        for inner in range(2 - pair):
            lanes = slice(inner * 64, (inner + 1) * 64)
            both = jnp.concatenate([even[:, lanes], odd[:, lanes]], axis=1)
            vec = 2 * pair + inner
            for side in range(2):
                for o in range(4):
                    j = side * 4 + o
                    g_rows[o, pl.ds(side * half * 4 + vec, half, stride=4), :] = both[j * half : (j + 1) * half]
    for o in range(4):
        g_refs[o][...] = g_rows[o].astype(jnp.bfloat16)


def total(x):
    return jnp.sum(x)


def reduced_lsqr(scal):
    s, a1, b2, a2, b3, a3, rec = [scal[..., n] for n in range(7)]
    beta = jnp.sqrt(total(rec))
    y11 = s / beta
    w1 = jnp.sqrt(jnp.maximum(1.0 - total(y11 * y11), 0.0))
    x = a1 * y11
    alpha = jnp.sqrt(total(x * x))
    x11 = x / alpha
    res, diag = beta, alpha
    y21, y22, w2 = a1 * x11 - alpha * y11, b2 * x11, -alpha * w1
    beta = jnp.sqrt(total(y21 * y21 + y22 * y22) + w2 * w2)
    y21, y22, w2 = y21 / beta, y22 / beta, w2 / beta
    x21, x22 = a1 * y21 + b2 * y22 - beta * x11, a2 * y22
    alpha = jnp.sqrt(total(x21 * x21 + x22 * x22))
    x21, x22 = x21 / alpha, x22 / alpha

    def rotate(res, diag, beta, alpha):
        rho = jnp.sqrt(diag * diag + beta * beta)
        c, sn = diag / rho, beta / rho
        return c * res / rho, sn * alpha / rho, sn * res, -c * alpha

    step, couple, res, diag = rotate(res, diag, beta, alpha)
    sol1 = step * x11
    dir1, dir2 = x21 - couple * x11, x22
    y31, y32, y33 = a1 * x21 - alpha * y21, b2 * x21 + a2 * x22 - alpha * y22, b3 * x22
    w3 = -alpha * w2
    beta = jnp.sqrt(total(y31 * y31 + y32 * y32 + y33 * y33) + w3 * w3)
    y31, y32, y33 = y31 / beta, y32 / beta, y33 / beta
    x31 = a1 * y31 + b2 * y32 - beta * x21
    x32 = a2 * y32 + b3 * y33 - beta * x22
    x33 = a3 * y33
    alpha = jnp.sqrt(total(x31 * x31 + x32 * x32 + x33 * x33))
    step, couple, res, diag = rotate(res, diag, beta, alpha)
    last = res * diag / alpha
    return (sol1 + step * dir1, step * dir2), (last * x31, last * x32, last * x33)


def body(devices, recorded, kernel, freq_index):
    share, virtual, samples = recorded.shape
    f = lax.axis_index("freq")
    y = lax.axis_index("rcv")
    core = f % 2
    columns = devices // 2
    kept = freq_index.shape[0]
    sources = kernel.shape[1]
    swap = [(i, i ^ 1) for i in range(devices)]

    def shift(o):
        return [(i, (i + o) % Y) for i in range(Y)]

    low, high = kernel[..., :devices], kernel[..., devices:]
    own = jnp.where(core == 0, low, high).reshape(2, 2 * sources, devices)
    send = jnp.where(core == 0, high, low).reshape(2, 2 * sources, devices)
    other = lax.ppermute(send, "freq", swap)

    def block(phi):
        mine = lax.dynamic_index_in_dim(own, phi % 2, 0, keepdims=False)
        theirs = lax.dynamic_index_in_dim(other, phi % 2, 0, keepdims=False)
        return jnp.where(phi // 2 == core, mine, theirs)

    blocks = [block(y)] + [lax.ppermute(block((y + o) % Y), "rcv", shift(o)) for o in range(1, Y)]
    blocks = blocks + [lax.ppermute(b, "freq", swap) for b in blocks]

    fr = freq_index.reshape(columns, Y)
    fr = lax.dynamic_slice_in_dim(jnp.concatenate([fr, fr], axis=1), y, Y, axis=1)
    table, spec, rec_norm = pl.pallas_call(
        dft_kernel,
        out_shape=(
            jax.ShapeDtypeStruct((2, kept, samples), jnp.float32),
            jax.ShapeDtypeStruct((2, kept, 128), jnp.bfloat16),
            jax.ShapeDtypeStruct((1, 1), jnp.float32),
        ),
        compiler_params=pltpu.CompilerParams(vmem_limit_bytes=32 * MIB),
        name="dft",
    )(fr.reshape(kept, 1), recorded.reshape(share * virtual, samples))
    spec = spec.reshape(2, columns, Y, 128).transpose(1, 0, 2, 3).reshape(devices, Y, 128)
    spec = lax.all_to_all(spec, "freq", split_axis=0, concat_axis=0, tiled=True)
    parts = [spec[:, 0]] + [lax.ppermute(spec[:, o], "rcv", shift(o)) for o in range(1, Y)]

    position = jnp.stack([y, core]).astype(jnp.int32)
    vectors = pl.pallas_call(
        krylov_kernel,
        out_shape=tuple(jax.ShapeDtypeStruct((4 * devices, 128), jnp.bfloat16) for _ in range(Y)),
        in_specs=[pl.BlockSpec(memory_space=pltpu.SMEM), pl.BlockSpec(memory_space=pltpu.VMEM)]
        + [pl.BlockSpec(memory_space=pltpu.VMEM)] * 4
        + [pl.BlockSpec(memory_space=pl.ANY)] * 8,
        out_specs=tuple(pl.BlockSpec(memory_space=pltpu.VMEM) for _ in range(Y)),
        scratch_shapes=[
            pltpu.VMEM((2 * sources, 8 * devices), jnp.bfloat16),
            pltpu.VMEM((4 * devices, 128), jnp.float32),
            pltpu.VMEM((HV, 2 * sources), jnp.float32),
            pltpu.VMEM((8 * devices, 128), jnp.float32),
            pltpu.VMEM((Y, 4 * devices, 128), jnp.float32),
            pltpu.SemaphoreType.DMA((8,)),
        ],
        compiler_params=pltpu.CompilerParams(vmem_limit_bytes=32 * MIB),
        name="krylov",
    )(position, rec_norm, *parts, *blocks)
    back = [vectors[0]] + [lax.ppermute(vectors[o], "rcv", shift(Y - o)) for o in range(1, Y)]
    back = jnp.stack([b.reshape(devices, 4, 128) for b in back], axis=1)
    back = lax.all_to_all(back, "freq", split_axis=0, concat_axis=0, tiled=True)

    scal = back[:, :, 3, :24].astype(jnp.float32)
    scal = scal[..., :8] + scal[..., 8:16] + scal[..., 16:24]
    sol_c, res_c = reduced_lsqr(scal)
    vecs = [back[:, :, n].astype(jnp.float32) for n in range(3)]
    root = math.sqrt(2.0)
    sol = sum((root * w)[..., None] * v for w, v in zip(sol_c, vecs))
    res = sum((root * w)[..., None] * v for w, v in zip(res_c, vecs))
    table = table.reshape(2, columns, Y, samples)

    def to_time(x):
        x = x.reshape(columns, 2, Y, share, 2, HV)
        return jnp.einsum("zcorqv,qzot->rcvt", x, table, precision=HIGH).reshape(share, virtual, samples)

    return to_time(sol), to_time(res)


def solution(mesh):
    in_specs = (P(("rcv", "freq"), None, None), P("freq", None, None, "rcv"), P())
    out_specs = (P(("rcv", "freq"), None, None), P(("rcv", "freq"), None, None))
    run = functools.partial(body, mesh.shape["freq"])
    return jax.shard_map(run, mesh=mesh, in_specs=in_specs, out_specs=out_specs, check_vma=False)
```

time: 1080 us -> 188 us (0.17)
  the two profiles are of different devices: /device:TPU:1 before, /device:TPU:33 now
where the time goes in v1:
time: 188 us; the launch traced here: 187 us
  starting transfers between devices  69.2 us (37%)
  waiting for transfers between devices  55.9 us (30%)
  local copies, waits for them, and re-layouts  19.5 us (10%)
  other arithmetic  15.1 us (8%)
  Pallas kernels  14 us (7%)
  matrix products  6.62 us (4%)
  between operations  6.55 us (3%)
    all_to_all x1, waiting for transfers between devices, body(): back = lax.all_to_all(back, 'freq', split_axis=0, concat_axis=0, tiled=True)  31.9 us
    all_to_all x1, starting transfers between devices, body(): spec = lax.all_to_all(spec, 'freq', split_axis=0, concat_axis=0, tiled=True)  19.9 us
    all_to_all x1, starting transfers between devices, body(): back = lax.all_to_all(back, 'freq', split_axis=0, concat_axis=0, tiled=True)  12.6 us
    ppermute x3, starting transfers between devices, body(): lax.ppermute(block((y + o) % Y), 'rcv', shift(o))  10.7 us
    pallas_call x1, Pallas kernels, body(): pl.pallas_call(krylov_kernel, out_shape=tuple((jax.ShapeDtypeStruct((4 *...  10.4 us
    ppermute x3, waiting for transfers between devices, body(): lax.ppermute(spec[:, o], 'rcv', shift(o))  10.2 us
    ppermute x4, starting transfers between devices, body(): blocks = blocks + [lax.ppermute(b, 'freq', swap) for b in blocks]  8.66 us
    ppermute x3, starting transfers between devices, body(): lax.ppermute(vectors[o], 'rcv', shift(Y - o))  8.41 us
  transfers between devices with their start and end apart: 16, of which 8 were waited for; matrix products, arithmetic and copies ran while one was open for 2% of the time, Pallas kernels for 2%

profile of v1, /device:TPU:33, one launch (start us, length us, event | category | flops | bytes accessed | tf_op | source)
XLA Modules:
  0.0 186.8 jit_solution(4918326371160921805)
XLA Ops:
  0.7 3.0 %broadcast_select_fusion.1 = (bf16[2,1024,2,128]{3,2,1,0:T(2,128)(2,1)S(1)}, bf16[2,1024,2,128]{3,2,1,0:T(2,128)(2,1)S(1)}) fusion(pred[]{:T(512)S(6)} %eq.30, bf16[2,1024,2,256]{3,2,1,0:T(2,128)(2,1)} %param.4), kind=kLoop, calls=%fused_computation.1 | loop fusion | flops 1048576 | bytes 4194305 | tf_op jit(solution)/shard_map/jit(_where)/select_n | solution.py:200
  3.7 2.6 %collective-permute-start.3 = (bf16[2,2048,128]{2,1,0:T(8,128)(2,1)S(1)}, bf16[2,2048,128]{2,1,0:T(8,128)(2,1)S(1)}, u32[]{:S(2)}, u32[]{:S(2)}) collective-permute-start(bf16[2,2048,128]{2,1,0:T(8,128)(2,1)S(1)} %bitcast.238), channel_id=1, source_target_pairs={{0,4},{4,0},{8,12},{12,8},{16,20},{20,16},{24,28},{28,24},{32,36},... | collective-permute-start | bytes 3145736 | tf_op jit(solution)/shard_map/ppermute | solution.py:202
  6.6 1.9 %collective-permute-done.3 = bf16[2,2048,128]{2,1,0:T(8,128)(2,1)S(1)} collective-permute-done((bf16[2,2048,128]{2,1,0:T(8,128)(2,1)S(1)}, bf16[2,2048,128]{2,1,0:T(8,128)(2,1)S(1)}, u32[]{:S(2)}, u32[]{:S(2)}) %collective-permute-start.3) | collective-permute-done | bytes 1048608 | tf_op jit(solution)/shard_map/ppermute | solution.py:202
  8.5 1.2 select_bitcast_fusion
  9.7 3.2 %collective-permute-start.4 = (bf16[2048,128]{1,0:T(8,128)(2,1)}, bf16[2048,128]{1,0:T(8,128)(2,1)S(1)}, u32[]{:S(2)}, u32[]{:S(2)}) collective-permute-start(bf16[2048,128]{1,0:T(8,128)(2,1)} %get-tuple-element.28), channel_id=1, source_target_pairs={{0,1},{1,2},{2,3},{3,0},{4,5},{5,6},{6,7},{7,4},{8,9},{9,10},{10,1... | collective-permute-start | bytes 1572872 | tf_op jit(solution)/shard_map/ppermute | solution.py:209
  12.9 4.5 %collective-permute-start.5 = (bf16[2048,128]{1,0:T(8,128)(2,1)}, bf16[2048,128]{1,0:T(8,128)(2,1)}, u32[]{:S(2)}, u32[]{:S(2)}) collective-permute-start(bf16[2048,128]{1,0:T(8,128)(2,1)} %get-tuple-element.27), channel_id=1, source_target_pairs={{0,2},{1,3},{2,0},{3,1},{4,6},{5,7},{6,4},{7,5},{8,10},{9,11},{10,... | collective-permute-start | bytes 1572872 | tf_op jit(solution)/shard_map/ppermute | solution.py:209
  17.5 3.0 %collective-permute-start.6 = (bf16[2048,128]{1,0:T(8,128)(2,1)}, bf16[2048,128]{1,0:T(8,128)(2,1)}, u32[]{:S(2)}, u32[]{:S(2)}) collective-permute-start(bf16[2048,128]{1,0:T(8,128)(2,1)} %get-tuple-element.26), channel_id=1, source_target_pairs={{0,3},{1,0},{2,1},{3,2},{4,7},{5,4},{6,5},{7,6},{8,11},{9,8},{10,9... | collective-permute-start | bytes 1572872 | tf_op jit(solution)/shard_map/ppermute | solution.py:209
  20.7 1.0 copy-done
  21.7 3.5 %dft.1 = (f32[2,256,1024]{2,1,0:T(8,128)S(1)}, bf16[2,256,128]{2,1,0:T(8,128)(2,1)S(1)}, f32[1,1]{1,0:T(1,128)}) custom-call(s32[256,1]{1,0:T(8,128)S(1)} %reshape.87.fr_ref, f32[128,1024]{1,0:T(8,128)S(1)} %bitcast.231), custom_call_target="tpu_custom_call" | custom-call | tf_op jit(solution)/shard_map/dft/pallas_call | solution.py:214
  25.3 0.7 copy.165
  26.0 19.9 %all-to-all-start = ((bf16[128,4,128]{2,1,0:T(4,128)(2,1)}), bf16[128,4,128]{2,1,0:T(4,128)(2,1)S(1)}, u32[]{:S(2)}, u32[]{:S(2)}) async-start(bf16[128,4,128]{2,1,0:T(4,128)(2,1)} %bitcast.6), calls=%async_computation | async-start | bytes 262144 | tf_op jit(solution)/shard_map/all_to_all | solution.py:225
  45.8 2.3 %collective-permute-start.7 = (bf16[2048,128]{1,0:T(8,128)(2,1)S(1)}, bf16[2048,128]{1,0:T(8,128)(2,1)}, u32[]{:S(2)}, u32[]{:S(2)}) collective-permute-start(bf16[2048,128]{1,0:T(8,128)(2,1)S(1)} %get-tuple-element.29.refs_4_), channel_id=1, source_target_pairs={{0,4},{4,0},{8,12},{12,8},{16,20},{20,16},{24,28},{28,24},{32,36},... | collective-permute-start | bytes 1572872 | tf_op jit(solution)/shard_map/ppermute | solution.py:210
  48.1 2.1 %collective-permute-start.8 = (bf16[2048,128]{1,0:T(8,128)(2,1)S(1)}, bf16[2048,128]{1,0:T(8,128)(2,1)}, u32[]{:S(2)}, u32[]{:S(2)}) collective-permute-start(bf16[2048,128]{1,0:T(8,128)(2,1)S(1)} %collective-permute-done.4.refs_5_), channel_id=1, source_target_pairs={{0,4},{4,0},{8,12},{12,8},{16,20},{20,16},{24,28},{28,24},{32,36},... | collective-permute-start | bytes 1572872 | tf_op jit(solution)/shard_map/ppermute | solution.py:210
  50.2 2.3 %collective-permute-start.9 = (bf16[2048,128]{1,0:T(8,128)(2,1)}, bf16[2048,128]{1,0:T(8,128)(2,1)}, u32[]{:S(2)}, u32[]{:S(2)}) collective-permute-start(bf16[2048,128]{1,0:T(8,128)(2,1)} %collective-permute-done.5.refs_6_), channel_id=1, source_target_pairs={{0,4},{4,0},{8,12},{12,8},{16,20},{20,16},{24,28},{28,24},{32,36},... | collective-permute-start | bytes 1572872 | tf_op jit(solution)/shard_map/ppermute | solution.py:210
  52.5 2.1 %collective-permute-start.10 = (bf16[2048,128]{1,0:T(8,128)(2,1)}, bf16[2048,128]{1,0:T(8,128)(2,1)}, u32[]{:S(2)}, u32[]{:S(2)}) collective-permute-start(bf16[2048,128]{1,0:T(8,128)(2,1)} %collective-permute-done.6.refs_7_), channel_id=1, source_target_pairs={{0,4},{4,0},{8,12},{12,8},{16,20},{20,16},{24,28},{28,24},{32,36},... | collective-permute-start | bytes 1572872 | tf_op jit(solution)/shard_map/ppermute | solution.py:210
  54.5 8.4 %all-to-all-done = bf16[128,4,128]{2,1,0:T(4,128)(2,1)S(1)} async-done(((bf16[128,4,128]{2,1,0:T(4,128)(2,1)}), bf16[128,4,128]{2,1,0:T(4,128)(2,1)S(1)}, u32[]{:S(2)}, u32[]{:S(2)}) %all-to-all-start) | async-done | bytes 131104 | tf_op jit(solution)/shard_map/all_to_all | solution.py:225
  63.1 2.3 %collective-permute-start = (bf16[128,128]{1,0:T(8,128)(2,1)S(1)}, bf16[128,128]{1,0:T(8,128)(2,1)S(1)}, u32[]{:S(2)}, u32[]{:S(2)}) collective-permute-start(bf16[128,128]{1,0:T(8,128)(2,1)S(1)} %bitcast.251), channel_id=1, source_target_pairs={{0,1},{1,2},{2,3},{3,0},{4,5},{5,6},{6,7},{7,4},{8,9},{9,10},{10,1... | collective-permute-start | bytes 98312 | tf_op jit(solution)/shard_map/ppermute | solution.py:226
  65.4 3.5 %collective-permute-done.refs_1_ = bf16[128,128]{1,0:T(8,128)(2,1)S(1)} collective-permute-done((bf16[128,128]{1,0:T(8,128)(2,1)S(1)}, bf16[128,128]{1,0:T(8,128)(2,1)S(1)}, u32[]{:S(2)}, u32[]{:S(2)}) %collective-permute-start) | collective-permute-done | bytes 32800 | tf_op jit(solution)/shard_map/ppermute | solution.py:226
  69.0 1.9 %collective-permute-start.1 = (bf16[128,128]{1,0:T(8,128)(2,1)S(1)}, bf16[128,128]{1,0:T(8,128)(2,1)S(1)}, u32[]{:S(2)}, u32[]{:S(2)}) collective-permute-start(bf16[128,128]{1,0:T(8,128)(2,1)S(1)} %bitcast.250), channel_id=1, source_target_pairs={{0,2},{1,3},{2,0},{3,1},{4,6},{5,7},{6,4},{7,5},{8,10},{9,11},{10,... | collective-permute-start | bytes 98312 | tf_op jit(solution)/shard_map/ppermute | solution.py:226
  70.9 4.2 %collective-permute-done.1.refs_2_ = bf16[128,128]{1,0:T(8,128)(2,1)S(1)} collective-permute-done((bf16[128,128]{1,0:T(8,128)(2,1)S(1)}, bf16[128,128]{1,0:T(8,128)(2,1)S(1)}, u32[]{:S(2)}, u32[]{:S(2)}) %collective-permute-start.1) | collective-permute-done | bytes 32800 | tf_op jit(solution)/shard_map/ppermute | solution.py:226
  75.1 2.1 %collective-permute-start.2 = (bf16[128,128]{1,0:T(8,128)(2,1)S(1)}, bf16[128,128]{1,0:T(8,128)(2,1)S(1)}, u32[]{:S(2)}, u32[]{:S(2)}) collective-permute-start(bf16[128,128]{1,0:T(8,128)(2,1)S(1)} %bitcast.249), channel_id=1, source_target_pairs={{0,3},{1,0},{2,1},{3,2},{4,7},{5,4},{6,5},{7,6},{8,11},{9,8},{10,9... | collective-permute-start | bytes 98312 | tf_op jit(solution)/shard_map/ppermute | solution.py:226
  77.3 2.5 %collective-permute-done.2.refs_3_ = bf16[128,128]{1,0:T(8,128)(2,1)S(1)} collective-permute-done((bf16[128,128]{1,0:T(8,128)(2,1)S(1)}, bf16[128,128]{1,0:T(8,128)(2,1)S(1)}, u32[]{:S(2)}, u32[]{:S(2)}) %collective-permute-start.2) | collective-permute-done | bytes 32800 | tf_op jit(solution)/shard_map/ppermute | solution.py:226
  79.8 10.4 %krylov.1 = (bf16[512,128]{1,0:T(8,128)(2,1)S(1)}, bf16[512,128]{1,0:T(8,128)(2,1)S(1)}, bf16[512,128]{1,0:T(8,128)(2,1)S(1)}, bf16[512,128]{1,0:T(8,128)(2,1)S(1)}) custom-call(s32[2]{0:T(128)S(1)} %pad_add_fusion.1.idx_ref, f32[1,1]{1,0:T(1,128)} %get-tuple-element.10.norm_ref, bf16[128,128]{1,0:T(8,128)(2,1)S(1)} %bitcast.232, ...), custom_call_target="tpu_custom_call" | custom-call | tf_op jit(solution)/shard_map/krylov/pallas_call | solution.py:229
  90.2 1.9 %collective-permute-start.13 = (bf16[512,128]{1,0:T(8,128)(2,1)S(1)}, bf16[512,128]{1,0:T(8,128)(2,1)S(1)}, u32[]{:S(2)}, u32[]{:S(2)}) collective-permute-start(bf16[512,128]{1,0:T(8,128)(2,1)S(1)} %get-tuple-element.15), channel_id=1, source_target_pairs={{0,1},{1,2},{2,3},{3,0},{4,5},{5,6},{6,7},{7,4},{8,9},{9,10},{10,1... | collective-permute-start | bytes 393224 | tf_op jit(solution)/shard_map/ppermute | solution.py:247
  92.2 4.3 %collective-permute-start.12 = (bf16[512,128]{1,0:T(8,128)(2,1)S(1)}, bf16[512,128]{1,0:T(8,128)(2,1)S(1)}, u32[]{:S(2)}, u32[]{:S(2)}) collective-permute-start(bf16[512,128]{1,0:T(8,128)(2,1)S(1)} %get-tuple-element.14), channel_id=1, source_target_pairs={{0,2},{1,3},{2,0},{3,1},{4,6},{5,7},{6,4},{7,5},{8,10},{9,11},{10,... | collective-permute-start | bytes 393224 | tf_op jit(solution)/shard_map/ppermute | solution.py:247
  96.5 2.2 %collective-permute-start.11 = (bf16[512,128]{1,0:T(8,128)(2,1)S(1)}, bf16[512,128]{1,0:T(8,128)(2,1)S(1)}, u32[]{:S(2)}, u32[]{:S(2)}) collective-permute-start(bf16[512,128]{1,0:T(8,128)(2,1)S(1)} %get-tuple-element.13), channel_id=1, source_target_pairs={{0,3},{1,0},{2,1},{3,2},{4,7},{5,4},{6,5},{7,6},{8,11},{9,8},{10,9... | collective-permute-start | bytes 393224 | tf_op jit(solution)/shard_map/ppermute | solution.py:247
  98.7 0.8 collective-permute-done.12
  99.5 2.7 %collective-permute-done.11 = bf16[512,128]{1,0:T(8,128)(2,1)S(1)} collective-permute-done((bf16[512,128]{1,0:T(8,128)(2,1)S(1)}, bf16[512,128]{1,0:T(8,128)(2,1)S(1)}, u32[]{:S(2)}, u32[]{:S(2)}) %collective-permute-start.11) | collective-permute-done | bytes 131104 | tf_op jit(solution)/shard_map/ppermute | solution.py:247
  102.2 1.2 pad_maximum_fusion
  103.4 12.6 %all-to-all-start.1 = ((bf16[128,4,4,128]{3,2,1,0:T(4,128)(2,1)}), bf16[128,4,4,128]{3,2,1,0:T(4,128)(2,1)S(1)}, u32[]{:S(2)}, u32[]{:S(2)}) async-start(bf16[128,4,4,128]{3,2,1,0:T(4,128)(2,1)} %pad_maximum_fusion), calls=%async_computation.1 | async-start | bytes 1048576 | tf_op jit(solution)/shard_map/all_to_all | solution.py:249
  116.1 1.7 reshape.72
  117.7 31.9 %all-to-all-done.1 = bf16[128,4,4,128]{3,2,1,0:T(4,128)(2,1)S(1)} async-done(((bf16[128,4,4,128]{3,2,1,0:T(4,128)(2,1)}), bf16[128,4,4,128]{3,2,1,0:T(4,128)(2,1)S(1)}, u32[]{:S(2)}, u32[]{:S(2)}) %all-to-all-start.1) | async-done | bytes 524320 | tf_op jit(solution)/shard_map/all_to_all | solution.py:249
  156.0 0.6 add_reduce_fusion
  157.6 0.6 fusion.19
  158.8 0.8 reshape.82
  159.7 0.8 reshape.81
  160.5 0.8 reshape.80
  164.2 0.8 copy.184
  165.0 1.4 copy.185
  166.4 1.4 copy.178
  167.8 2.0 %copy.179 = f32[64,2,4]{1,0,2:T(8,128)} copy(f32[64,2,4]{2,1,0:T(2,128)} %bitcast.244) | data formatting | bytes 4096 | tf_op jit(solution)/shard_map/mul | solution.py:256
  169.9 1.4 copy.175
  171.3 2.0 %copy.176 = f32[64,2,4]{1,0,2:T(8,128)} copy(f32[64,2,4]{2,1,0:T(2,128)} %bitcast.245) | data formatting | bytes 4096 | tf_op jit(solution)/shard_map/mul | solution.py:256
  173.3 5.2 %multiply_add_fusion = (f32[64,2,4,2,2,32]{5,4,3,1,0,2:T(2,128)S(1)}, f32[64,2,4,2,2,32]{5,4,3,1,0,2:T(2,128)S(1)}) fusion(f32[64,2,4,2,2,32]{5,4,3,1,0,2:T(2,128)S(1)} %reshape.82, f32[64,2,4,2,2,32]{5,4,3,1,0,2:T(2,128)S(1)} %reshape.81, f32[64,2,4,2,2,32]{5,4,3,1,0,2:T(2,128)S(1)} %reshape.80, f32[64,2,4]{1,0,2:T(8,128)S(1)} %copy.189, ...), kind=kLoop, calls=%fused_computation.10 | loop fusion | flops 524288 | bytes 1320960 | tf_op jit(solution)/shard_map/add | solution.py:257
  178.5 3.3 %fusion.4 = f32[2,2,32,1024]{3,2,0,1:T(8,128)S(1)} fusion(f32[2,64,4,1024,1,1]{3,2,1,0,5,4:T(4,128)S(1)} %bitcast.235, f32[64,2,4,2,2,32]{5,4,3,1,0,2:T(2,128)S(1)} %get-tuple-element.25), kind=kOutput, calls=%fused_computation.6 | convolution fusion | flops 805306368 | bytes 2883584 | tf_op jit(solution)/shard_map/zcorqv,qzot->rcvt/dot_general | solution.py:262
  181.8 0.8 copy.183
  182.7 3.3 %fusion.7 = f32[2,2,32,1024]{3,2,0,1:T(8,128)S(1)} fusion(f32[2,64,4,1024,1,1]{3,2,1,0,5,4:T(4,128)S(1)} %bitcast.236, f32[64,2,4,2,2,32]{5,4,3,1,0,2:T(2,128)S(1)} %get-tuple-element.24), kind=kOutput, calls=%fused_computation.7 | convolution fusion | flops 805306368 | bytes 2883584 | tf_op jit(solution)/shard_map/zcorqv,qzot->rcvt/dot_general | solution.py:262
  186.0 0.8 copy.193
  (42 shorter events, 6.1 us)
Async XLA Ops:
  0.6 5.7 %copy-start.2 = (s32[256]{0:T(256)S(1)}, s32[256]{0:T(256)}, u32[]{:S(2)}) copy-start(s32[256]{0:T(256)} %param.5) | copy-start | bytes 3076
  3.7 4.9 %collective-permute-start.3 = (bf16[2,2048,128]{2,1,0:T(8,128)(2,1)S(1)}, bf16[2,2048,128]{2,1,0:T(8,128)(2,1)S(1)}, u32[]{:S(2)}, u32[]{:S(2)}) collective-permute-start(bf16[2,2048,128]{2,1,0:T(8,128)(2,1)S(1)} %bitcast.238), channel_id=1, source_target_pairs={{0,4},{4,0},{8,12},{12,8},{16,20},{20,16},{24,28},{28,24},{32,36},... | collective-permute-start | bytes 3145736 | tf_op jit(solution)/shard_map/ppermute | solution.py:202
  9.7 38.4 %collective-permute-start.4 = (bf16[2048,128]{1,0:T(8,128)(2,1)}, bf16[2048,128]{1,0:T(8,128)(2,1)S(1)}, u32[]{:S(2)}, u32[]{:S(2)}) collective-permute-start(bf16[2048,128]{1,0:T(8,128)(2,1)} %get-tuple-element.28), channel_id=1, source_target_pairs={{0,1},{1,2},{2,3},{3,0},{4,5},{5,6},{6,7},{7,4},{8,9},{9,10},{10,1... | collective-permute-start | bytes 1572872 | tf_op jit(solution)/shard_map/ppermute | solution.py:209
  12.9 37.2 %collective-permute-start.5 = (bf16[2048,128]{1,0:T(8,128)(2,1)}, bf16[2048,128]{1,0:T(8,128)(2,1)}, u32[]{:S(2)}, u32[]{:S(2)}) collective-permute-start(bf16[2048,128]{1,0:T(8,128)(2,1)} %get-tuple-element.27), channel_id=1, source_target_pairs={{0,2},{1,3},{2,0},{3,1},{4,6},{5,7},{6,4},{7,5},{8,10},{9,11},{10,... | collective-permute-start | bytes 1572872 | tf_op jit(solution)/shard_map/ppermute | solution.py:209
  17.5 35.0 %collective-permute-start.6 = (bf16[2048,128]{1,0:T(8,128)(2,1)}, bf16[2048,128]{1,0:T(8,128)(2,1)}, u32[]{:S(2)}, u32[]{:S(2)}) collective-permute-start(bf16[2048,128]{1,0:T(8,128)(2,1)} %get-tuple-element.26), channel_id=1, source_target_pairs={{0,3},{1,0},{2,1},{3,2},{4,7},{5,4},{6,5},{7,6},{8,11},{9,8},{10,9... | collective-permute-start | bytes 1572872 | tf_op jit(solution)/shard_map/ppermute | solution.py:209
  20.7 1.0 copy-start
  26.0 36.9 %all-to-all-start = ((bf16[128,4,128]{2,1,0:T(4,128)(2,1)}), bf16[128,4,128]{2,1,0:T(4,128)(2,1)S(1)}, u32[]{:S(2)}, u32[]{:S(2)}) async-start(bf16[128,4,128]{2,1,0:T(4,128)(2,1)} %bitcast.6), calls=%async_computation | async-start | bytes 262144 | tf_op jit(solution)/shard_map/all_to_all | solution.py:225
  45.8 34.0 %collective-permute-start.7 = (bf16[2048,128]{1,0:T(8,128)(2,1)S(1)}, bf16[2048,128]{1,0:T(8,128)(2,1)}, u32[]{:S(2)}, u32[]{:S(2)}) collective-permute-start(bf16[2048,128]{1,0:T(8,128)(2,1)S(1)} %get-tuple-element.29.refs_4_), channel_id=1, source_target_pairs={{0,4},{4,0},{8,12},{12,8},{16,20},{20,16},{24,28},{28,24},{32,36},... | collective-permute-start | bytes 1572872 | tf_op jit(solution)/shard_map/ppermute | solution.py:210
  48.1 31.7 %collective-permute-start.8 = (bf16[2048,128]{1,0:T(8,128)(2,1)S(1)}, bf16[2048,128]{1,0:T(8,128)(2,1)}, u32[]{:S(2)}, u32[]{:S(2)}) collective-permute-start(bf16[2048,128]{1,0:T(8,128)(2,1)S(1)} %collective-permute-done.4.refs_5_), channel_id=1, source_target_pairs={{0,4},{4,0},{8,12},{12,8},{16,20},{20,16},{24,28},{28,24},{32,36},... | collective-permute-start | bytes 1572872 | tf_op jit(solution)/shard_map/ppermute | solution.py:210
  50.2 29.6 %collective-permute-start.9 = (bf16[2048,128]{1,0:T(8,128)(2,1)}, bf16[2048,128]{1,0:T(8,128)(2,1)}, u32[]{:S(2)}, u32[]{:S(2)}) collective-permute-start(bf16[2048,128]{1,0:T(8,128)(2,1)} %collective-permute-done.5.refs_6_), channel_id=1, source_target_pairs={{0,4},{4,0},{8,12},{12,8},{16,20},{20,16},{24,28},{28,24},{32,36},... | collective-permute-start | bytes 1572872 | tf_op jit(solution)/shard_map/ppermute | solution.py:210
  52.5 27.3 %collective-permute-start.10 = (bf16[2048,128]{1,0:T(8,128)(2,1)}, bf16[2048,128]{1,0:T(8,128)(2,1)}, u32[]{:S(2)}, u32[]{:S(2)}) collective-permute-start(bf16[2048,128]{1,0:T(8,128)(2,1)} %collective-permute-done.6.refs_7_), channel_id=1, source_target_pairs={{0,4},{4,0},{8,12},{12,8},{16,20},{20,16},{24,28},{28,24},{32,36},... | collective-permute-start | bytes 1572872 | tf_op jit(solution)/shard_map/ppermute | solution.py:210
  63.1 5.9 %collective-permute-start = (bf16[128,128]{1,0:T(8,128)(2,1)S(1)}, bf16[128,128]{1,0:T(8,128)(2,1)S(1)}, u32[]{:S(2)}, u32[]{:S(2)}) collective-permute-start(bf16[128,128]{1,0:T(8,128)(2,1)S(1)} %bitcast.251), channel_id=1, source_target_pairs={{0,1},{1,2},{2,3},{3,0},{4,5},{5,6},{6,7},{7,4},{8,9},{9,10},{10,1... | collective-permute-start | bytes 98312 | tf_op jit(solution)/shard_map/ppermute | solution.py:226
  69.0 6.2 %collective-permute-start.1 = (bf16[128,128]{1,0:T(8,128)(2,1)S(1)}, bf16[128,128]{1,0:T(8,128)(2,1)S(1)}, u32[]{:S(2)}, u32[]{:S(2)}) collective-permute-start(bf16[128,128]{1,0:T(8,128)(2,1)S(1)} %bitcast.250), channel_id=1, source_target_pairs={{0,2},{1,3},{2,0},{3,1},{4,6},{5,7},{6,4},{7,5},{8,10},{9,11},{10,... | collective-permute-start | bytes 98312 | tf_op jit(solution)/shard_map/ppermute | solution.py:226
  75.1 4.6 %collective-permute-start.2 = (bf16[128,128]{1,0:T(8,128)(2,1)S(1)}, bf16[128,128]{1,0:T(8,128)(2,1)S(1)}, u32[]{:S(2)}, u32[]{:S(2)}) collective-permute-start(bf16[128,128]{1,0:T(8,128)(2,1)S(1)} %bitcast.249), channel_id=1, source_target_pairs={{0,3},{1,0},{2,1},{3,2},{4,7},{5,4},{6,5},{7,6},{8,11},{9,8},{10,9... | collective-permute-start | bytes 98312 | tf_op jit(solution)/shard_map/ppermute | solution.py:226
  90.2 8.4 %collective-permute-start.13 = (bf16[512,128]{1,0:T(8,128)(2,1)S(1)}, bf16[512,128]{1,0:T(8,128)(2,1)S(1)}, u32[]{:S(2)}, u32[]{:S(2)}) collective-permute-start(bf16[512,128]{1,0:T(8,128)(2,1)S(1)} %get-tuple-element.15), channel_id=1, source_target_pairs={{0,1},{1,2},{2,3},{3,0},{4,5},{5,6},{6,7},{7,4},{8,9},{9,10},{10,1... | collective-permute-start | bytes 393224 | tf_op jit(solution)/shard_map/ppermute | solution.py:247
  92.2 7.3 %collective-permute-start.12 = (bf16[512,128]{1,0:T(8,128)(2,1)S(1)}, bf16[512,128]{1,0:T(8,128)(2,1)S(1)}, u32[]{:S(2)}, u32[]{:S(2)}) collective-permute-start(bf16[512,128]{1,0:T(8,128)(2,1)S(1)} %get-tuple-element.14), channel_id=1, source_target_pairs={{0,2},{1,3},{2,0},{3,1},{4,6},{5,7},{6,4},{7,5},{8,10},{9,11},{10,... | collective-permute-start | bytes 393224 | tf_op jit(solution)/shard_map/ppermute | solution.py:247
  96.5 5.7 %collective-permute-start.11 = (bf16[512,128]{1,0:T(8,128)(2,1)S(1)}, bf16[512,128]{1,0:T(8,128)(2,1)S(1)}, u32[]{:S(2)}, u32[]{:S(2)}) collective-permute-start(bf16[512,128]{1,0:T(8,128)(2,1)S(1)} %get-tuple-element.13), channel_id=1, source_target_pairs={{0,3},{1,0},{2,1},{3,2},{4,7},{5,4},{6,5},{7,6},{8,11},{9,8},{10,9... | collective-permute-start | bytes 393224 | tf_op jit(solution)/shard_map/ppermute | solution.py:247
  103.4 46.2 %all-to-all-start.1 = ((bf16[128,4,4,128]{3,2,1,0:T(4,128)(2,1)}), bf16[128,4,4,128]{3,2,1,0:T(4,128)(2,1)S(1)}, u32[]{:S(2)}, u32[]{:S(2)}) async-start(bf16[128,4,4,128]{3,2,1,0:T(4,128)(2,1)} %pad_maximum_fusion), calls=%async_computation.1 | async-start | bytes 1048576 | tf_op jit(solution)/shard_map/all_to_all | solution.py:249
  173.3 5.2 %copy-start.1 = (f32[2,64,4,1024]{3,2,1,0:T(4,128)S(1)}, f32[2,64,4,1024]{3,2,1,0:T(4,128)}, u32[]{:S(2)}) copy-start(f32[2,64,4,1024]{3,2,1,0:T(4,128)} %reshape.72) | copy-start | bytes 6291460

commit v2 on v1

v2 whole, which is shorter than its diff:
```python
import functools
import math

import jax
import jax.numpy as jnp
from jax import lax
from jax.experimental import pallas as pl
from jax.experimental.pallas import tpu as pltpu
from jax.sharding import Mesh, PartitionSpec as P

Y = 4
GROUP = 8
HV = 32
EXTRA = 16
HIGH = lax.Precision.HIGHEST
MIB = 1024 * 1024
COLUMN = ("core", "rcv")


def dft_kernel(fr_ref, rec_ref, thi_ref, tlo_ref, out_ref, norm_ref, table, rows):
    columns = fr_ref.shape[0]
    kept = Y * columns
    samples = rec_ref.shape[1]
    unit = 2.0 * math.pi / samples
    fr = jnp.concatenate([fr_ref[:, phi : phi + 1] for phi in range(Y)], axis=0)
    lane = lax.broadcasted_iota(jnp.int32, (kept, 128), 1)
    fine = (fr * lane & (samples - 1)).astype(jnp.float32) * unit
    coarse = (fr * (lane * 128) & (samples - 1)).astype(jnp.float32) * unit
    cos_f, sin_f = jnp.cos(fine), jnp.sin(fine)
    factor = 1.0 / math.sqrt(samples)
    cos_c, sin_c = jnp.cos(coarse) * factor, jnp.sin(coarse) * factor
    for a in range(samples // 128):
        ca, sa = cos_c[:, a : a + 1], sin_c[:, a : a + 1]
        part = slice(a * 128, (a + 1) * 128)
        for p, value in enumerate((ca * cos_f - sa * sin_f, -(sa * cos_f + ca * sin_f))):
            table[p, :, part] = value
            top = value.astype(jnp.bfloat16)
            thi_ref[p, :, part] = top
            tlo_ref[p, :, part] = (value - top.astype(jnp.float32)).astype(jnp.bfloat16)
    rec = rec_ref[...]
    norm_ref[...] = jnp.sum(rec * rec, axis=(0, 1), keepdims=True)
    spec = [
        lax.dot_general(table[p], rec, (((1,), (1,)), ((), ())), precision=HIGH, preferred_element_type=jnp.float32)
        for p in range(2)
    ]
    for c in range(2):
        parts = [spec[p][:, (2 * src + c) * HV : (2 * src + c + 1) * HV] for src in range(2) for p in range(2)]
        both = jnp.concatenate(parts, axis=1)
        for phi in range(Y):
            rows[pl.ds(c * Y + phi, columns, stride=GROUP), :] = both[phi * columns : (phi + 1) * columns]
    out_ref[...] = rows[...].astype(jnp.bfloat16)


def quarter_turn(x):
    width = x.shape[1]
    even = lax.broadcasted_iota(jnp.int32, x.shape, 1) % 2 == 0
    return jnp.where(even, pltpu.roll(x, width - 1, 1), -pltpu.roll(x, 1, 1))


def total(x):
    return jnp.sum(x, axis=(0, 1), keepdims=True)


def length_of(x):
    return jnp.sqrt(total(x * x))


def inverse_of(x):
    return jnp.where(x > 1e-30, 1.0 / jnp.maximum(x, 1e-30), 0.0)


def krylov_kernel(idx_ref, norm_ref, u_ref, *refs):
    k_refs, g_ref = refs[:8], refs[8]
    kmat, u_rows, q_rows, sems = refs[9:]
    columns = u_ref.shape[1]
    width = 2 * columns
    half = columns // 2
    y, core = idx_ref[0], idx_ref[1]

    copies = []
    for j in range(8):
        side = core if j < 4 else 1 - core
        quarter = lax.rem(y + 8 - j % 4 - 2 * side, Y)
        start = pl.multiple_of((side * Y + quarter) * width, width)
        copies.append(pltpu.make_async_copy(k_refs[j], kmat.at[:, pl.ds(start, width)], sems.at[j]))
    for copy in copies:
        copy.start()

    for c in range(2):
        fields = [u_ref[c * Y + ys].astype(jnp.float32) for ys in range(Y)]
        for g in range(4):
            both = jnp.concatenate([block[:, g * HV : (g + 1) * HV] for block in fields], axis=1)
            u_rows[pl.ds(c * 4 + g, columns, stride=8), :] = both
    turned = u_rows[...].T
    u = jnp.concatenate([turned[ys * HV : (ys + 1) * HV] for ys in range(Y)], axis=1)

    for copy in copies:
        copy.wait()

    def adjoint(p):
        both = jnp.concatenate([p, quarter_turn(p)], axis=0).astype(jnp.bfloat16)
        return 0.5 * jnp.dot(both, kmat[...], preferred_element_type=jnp.float32)

    def forward(q):
        w = lax.dot_general(
            q.astype(jnp.bfloat16), kmat[...], (((1,), (1,)), ((), ())), preferred_element_type=jnp.float32
        )
        return 0.5 * (w[:HV] - quarter_turn(w[HV:]))

    length = length_of(u)
    scale = inverse_of(length)
    g1 = adjoint(u) * scale
    a1 = length_of(g1)
    q1 = g1 * inverse_of(a1)
    h2 = forward(q1) - (a1 * scale) * u
    b2 = length_of(h2)
    p2 = h2 * inverse_of(b2)
    g2 = adjoint(p2) - b2 * q1
    a2 = length_of(g2)
    q2 = g2 * inverse_of(a2)
    h3 = forward(q2) - a2 * p2
    b3 = length_of(h3)
    p3 = h3 * inverse_of(b3)
    g3 = adjoint(p3) - b3 * q2
    a3 = length_of(g3)
    q3 = g3 * inverse_of(a3)

    lane = lax.broadcasted_iota(jnp.int32, (EXTRA, 128), 1)
    slot = lax.rem(lane, 64) // GROUP
    values = jnp.zeros((EXTRA, 128), jnp.float32)
    for n, value in enumerate((math.sqrt(2.0) * length, a1, b2, a2, b3, a3, norm_ref[...])):
        values = jnp.where(slot == n, value, values)
    hi = values.astype(jnp.bfloat16).astype(jnp.float32)
    scalars = jnp.where(lane < 64, hi, values - hi)
    scalars = jnp.where(lax.rem(lane, GROUP) == core * Y + y, scalars, 0.0).astype(jnp.bfloat16)

    for pair in range(2):
        first, second = ((q1, q2), (q3, q3))[pair]
        q_rows[...] = jnp.concatenate([first, second], axis=0).T
        for c in range(2):
            for quarter in range(Y):
                for side in range(2):
                    base = (side * Y + quarter) * width + 2 * c
                    even = q_rows[pl.ds(base, half, stride=4), :]
                    odd = q_rows[pl.ds(base + 1, half, stride=4), :]
                    for inner in range(2 - pair):
                        lanes = slice(inner * 64, (inner + 1) * 64)
                        both = jnp.concatenate([even[:, lanes], odd[:, lanes]], axis=1)
                        row = (2 * pair + inner) * columns + side * half
                        g_ref[c * Y + quarter, row : row + half, :] = both.astype(jnp.bfloat16)
    for e in range(GROUP):
        g_ref[e, 3 * columns : 3 * columns + EXTRA, :] = scalars


def reduced_lsqr(s, a1, b2, a2, b3, a3, rec):
    def norm(*parts):
        return jnp.sqrt(total(sum(part * part for part in parts)))

    beta = jnp.sqrt(total(rec))
    y11 = s / beta
    w1 = jnp.sqrt(jnp.maximum(1.0 - total(y11 * y11), 0.0))
    x = a1 * y11
    alpha = norm(x)
    x11 = x / alpha
    res, diag = beta, alpha
    y21, y22, w2 = a1 * x11 - alpha * y11, b2 * x11, -alpha * w1
    beta = jnp.sqrt(total(y21 * y21 + y22 * y22) + w2 * w2)
    y21, y22, w2 = y21 / beta, y22 / beta, w2 / beta
    x21, x22 = a1 * y21 + b2 * y22 - beta * x11, a2 * y22
    alpha = norm(x21, x22)
    x21, x22 = x21 / alpha, x22 / alpha

    def rotate(res, diag, beta, alpha):
        rho = jnp.sqrt(diag * diag + beta * beta)
        c, sn = diag / rho, beta / rho
        return c * res / rho, sn * alpha / rho, sn * res, -c * alpha

    step, couple, res, diag = rotate(res, diag, beta, alpha)
    sol1 = step * x11
    dir1, dir2 = x21 - couple * x11, x22
    y31, y32, y33 = a1 * x21 - alpha * y21, b2 * x21 + a2 * x22 - alpha * y22, b3 * x22
    w3 = -alpha * w2
    beta = jnp.sqrt(total(y31 * y31 + y32 * y32 + y33 * y33) + w3 * w3)
    y31, y32, y33 = y31 / beta, y32 / beta, y33 / beta
    x31 = a1 * y31 + b2 * y32 - beta * x21
    x32 = a2 * y32 + b3 * y33 - beta * x22
    x33 = a3 * y33
    alpha = norm(x31, x32, x33)
    step, couple, res, diag = rotate(res, diag, beta, alpha)
    last = res * diag / alpha
    return (sol1 + step * dir1, step * dir2), (last * x31, last * x32, last * x33)


def traces_kernel(m_ref, thi_ref, tlo_ref, sol_ref, res_ref):
    kept = thi_ref.shape[1]
    samples = thi_ref.shape[2]
    scal = m_ref[3 * GROUP].astype(jnp.float32)
    parts = [
        scal[:, n * GROUP : (n + 1) * GROUP] + scal[:, 64 + n * GROUP : 64 + (n + 1) * GROUP] for n in range(7)
    ]
    sol_c, res_c = reduced_lsqr(*parts)
    root = math.sqrt(2.0)
    sol_c, res_c = [root * w for w in sol_c], [root * w for w in res_c]
    lines = []
    for weights in (sol_c, res_c):
        for c in range(2):
            blocks = []
            for phi in range(Y):
                e = c * Y + phi
                blocks.append(
                    sum(w[:, e : e + 1] * m_ref[3 * e + n].astype(jnp.float32) for n, w in enumerate(weights))
                )
            turned = jnp.concatenate(blocks, axis=0).T
            for rr in range(2):
                lines.append(
                    jnp.concatenate([turned[(2 * rr + q) * HV : (2 * rr + q + 1) * HV] for q in range(2)], axis=1)
                )
    x = jnp.concatenate(lines, axis=0)
    hi = x.astype(jnp.bfloat16)
    lo = (x - hi.astype(jnp.float32)).astype(jnp.bfloat16)
    thi = thi_ref[...].reshape(2 * kept, samples)
    tlo = tlo_ref[...].reshape(2 * kept, samples)

    def dot(a, b):
        return jnp.dot(a, b, preferred_element_type=jnp.float32)

    out = dot(hi, thi) + (dot(hi, tlo) + dot(lo, thi))
    for n, ref in enumerate((sol_ref, res_ref)):
        for c in range(2):
            for rr in range(2):
                row = ((n * 2 + c) * 2 + rr) * HV
                ref[rr, c * HV : (c + 1) * HV, :] = out[row : row + HV]


def body(recorded, kernel, freq_index):
    share, virtual, samples = recorded.shape
    columns = freq_index.shape[0] // Y
    kept = freq_index.shape[0]
    sources = kernel.shape[1]
    width = kernel.shape[3] // 2
    core = lax.axis_index("core")
    y = lax.axis_index("rcv")

    def route(o):
        pairs = []
        for c in range(2):
            for here in range(Y):
                if (here + o) % Y // 2 == c:
                    pairs.append((c * Y + here, (here + o) % Y))
                else:
                    pairs.append((c * Y + here, Y + (here + o + 2) % Y))
        return pairs

    def payload(o):
        mine = lax.dynamic_index_in_dim(kernel, (y + o) % 2, 0, keepdims=False)
        low = (y + o) % Y // 2 == core
        return jnp.where(low, mine[..., :width], mine[..., width:]).reshape(2 * sources, width)

    blocks = [lax.ppermute(payload(o), COLUMN, route(o)) for o in range(Y)]
    blocks = blocks + [lax.ppermute(b, "core", [(0, 1), (1, 0)]) for b in blocks]

    table_hi, table_lo, spec, rec_norm = pl.pallas_call(
        dft_kernel,
        out_shape=(
            jax.ShapeDtypeStruct((2, kept, samples), jnp.bfloat16),
            jax.ShapeDtypeStruct((2, kept, samples), jnp.bfloat16),
            jax.ShapeDtypeStruct((GROUP * columns, 128), jnp.bfloat16),
            jax.ShapeDtypeStruct((1, 1), jnp.float32),
        ),
        scratch_shapes=[
            pltpu.VMEM((2, kept, samples), jnp.float32),
            pltpu.VMEM((GROUP * columns, 128), jnp.float32),
        ],
        compiler_params=pltpu.CompilerParams(vmem_limit_bytes=32 * MIB),
        name="dft",
    )(freq_index.reshape(columns, Y), recorded.reshape(share * virtual, samples))
    spec = spec.reshape(columns, GROUP, 128)
    spec = lax.all_to_all(spec, "zx", split_axis=0, concat_axis=0, tiled=True)
    spec = lax.all_to_all(spec.transpose(1, 0, 2), COLUMN, split_axis=0, concat_axis=0, tiled=True)

    position = jnp.stack([y, core]).astype(jnp.int32)
    lines = 3 * columns + EXTRA
    vectors = pl.pallas_call(
        krylov_kernel,
        out_shape=jax.ShapeDtypeStruct((GROUP, lines, 128), jnp.bfloat16),
        in_specs=[pl.BlockSpec(memory_space=pltpu.SMEM)]
        + [pl.BlockSpec(memory_space=pltpu.VMEM)] * 2
        + [pl.BlockSpec(memory_space=pl.ANY)] * 8,
        out_specs=pl.BlockSpec(memory_space=pltpu.VMEM),
        scratch_shapes=[
            pltpu.VMEM((2 * sources, 8 * width), jnp.bfloat16),
            pltpu.VMEM((8 * columns, 128), jnp.float32),
            pltpu.VMEM((8 * width, 128), jnp.float32),
            pltpu.SemaphoreType.DMA((8,)),
        ],
        compiler_params=pltpu.CompilerParams(vmem_limit_bytes=32 * MIB),
        name="krylov",
    )(position, rec_norm, spec, *blocks)
    back = lax.all_to_all(vectors, COLUMN, split_axis=0, concat_axis=0, tiled=True)
    data = back[:, : 3 * columns].reshape(GROUP, 3, columns, 128).transpose(2, 0, 1, 3).reshape(columns, 24, 128)
    scal = jnp.sum(back[:, 3 * columns].astype(jnp.float32), axis=0).astype(jnp.bfloat16)
    scal = jnp.broadcast_to(scal, (columns, 2, 128))
    send = jnp.concatenate([data, scal], axis=1).reshape(columns, 13, 2, 128)
    got = lax.all_to_all(send, "zx", split_axis=0, concat_axis=0, tiled=True)
    got = got.reshape(columns, 26, 128).transpose(1, 0, 2)

    return pl.pallas_call(
        traces_kernel,
        out_shape=tuple(jax.ShapeDtypeStruct((share, virtual, samples), jnp.float32) for _ in range(2)),
        compiler_params=pltpu.CompilerParams(vmem_limit_bytes=32 * MIB),
        name="traces",
    )(got, table_hi, table_lo)


def solution(mesh):
    devices = mesh.devices
    fine = Mesh(devices.reshape(devices.shape[0] // 2, 2, devices.shape[1]), ("zx", "core", "rcv"))
    traces = P(("rcv", "zx", "core"), None, None)
    in_specs = (traces, P(("zx", "core"), None, None, "rcv"), P())
    return jax.shard_map(body, mesh=fine, in_specs=in_specs, out_specs=(traces, traces), check_vma=False)
```

time: 188 us -> 141 us (0.75)
  the two profiles are of different devices: /device:TPU:33 before, /device:TPU:2 now
where the time goes in v2:
time: 141 us; the launch traced here: 140 us
  blocking collectives  47.3 us (34%)
  starting transfers between devices  45.7 us (32%)
  Pallas kernels  18.3 us (13%)
  waiting for transfers between devices  13.8 us (10%)
  local copies, waits for them, and re-layouts  7.14 us (5%)
  other arithmetic  6.76 us (5%)
    all_to_all x1, blocking collectives, body(): got = lax.all_to_all(send, 'zx', split_axis=0, concat_axis=0, tiled=True)  35.9 us
    all_to_all x1, starting transfers between devices, body(): spec = lax.all_to_all(spec, 'zx', split_axis=0, concat_axis=0, tiled=True)  18.6 us
    ppermute x4, starting transfers between devices, body(): blocks = [lax.ppermute(payload(o), COLUMN, route(o)) for o in range(Y)]  14.8 us
    all_to_all x1, blocking collectives, body(): lax.all_to_all(vectors, COLUMN, split_axis=0, concat_axis=0, tiled=True)  11.5 us
    pallas_call x1, Pallas kernels, body(): pl.pallas_call(krylov_kernel, out_shape=jax.ShapeDtypeStruct((GROUP, line...  9.86 us
    ppermute x4, starting transfers between devices, body(): lax.ppermute(b, 'core', [(0, 1), (1, 0)])  8.66 us
    all_to_all x1, waiting for transfers between devices, body(): spec = lax.all_to_all(spec, 'zx', split_axis=0, concat_axis=0, tiled=True)  8.59 us
    select_n x4, other arithmetic, payload(): jnp.where(low, mine[..., :width], mine[..., width:])  6.62 us
  transfers between devices with their start and end apart: 10, of which 2 were waited for; matrix products, arithmetic and copies ran while one was open for 4% of the time, Pallas kernels for 3%

profile of v2, /device:TPU:2, one launch (start us, length us, event | category | flops | bytes accessed | tf_op | source)
XLA Modules:
  0.0 140.1 jit_solution(4009731937101148964)
XLA Ops:
  0.7 5.8 %dynamic-slice_bitcast_fusion = (bf16[1024,2,256]{2,1,0:T(2,128)(2,1)S(1)}, bf16[1024,2,256]{2,1,0:T(2,128)(2,1)S(1)}, bf16[1024,2,256]{2,1,0:T(2,128)(2,1)S(1)}, bf16[1024,2,256]{2,1,0:T(2,128)(2,1)}) fusion(bf16[2,1024,2,256]{3,2,1,0:T(2,128)(2,1)} %param.4, s32[]{:T(128)S(6)} %select_n.109, s32[]{:T(128)S(6)} %select_n.97, s32[]{:T(128)S(6)} %select_n.91, ...), kind=kLoop, calls=%fused_computation | loop fusion | bytes 8388624 | tf_op jit(solution)/shard_map/jit(dynamic_index_in_dim)/squeeze | solution.py:255
  6.5 1.3 broadcast_select_fusion.2
  7.8 3.5 %collective-permute-start.1 = (bf16[2048,128]{1,0:T(8,128)(2,1)}, bf16[2048,128]{1,0:T(8,128)(2,1)S(1)}, u32[]{:S(2)}, u32[]{:S(2)}) collective-permute-start(bf16[2048,128]{1,0:T(8,128)(2,1)} %bitcast.8), channel_id=1, source_target_pairs={{0,1},{1,4},{2,5},{3,0},{4,7},{5,2},{6,3},{7,6},{8,9},{9,12},{10,1... | collective-permute-start | bytes 1572872 | tf_op jit(solution)/shard_map/ppermute | solution.py:259
  11.4 0.0 copy-start.1
  11.4 0.0 copy-start
  11.4 2.6 %broadcast_select_fusion.1 = bf16[1024,2,128]{2,1,0:T(2,128)(2,1)} fusion(pred[]{:T(512)S(6)} %eq.23, bf16[1024,2,256]{2,1,0:T(2,128)(2,1)} %get-tuple-element.13), kind=kLoop, calls=%fused_computation.5 | loop fusion | flops 262144 | bytes 1572865 | tf_op jit(solution)/shard_map/jit(_where)/select_n | solution.py:257
  14.0 2.9 %collective-permute-start.2 = (bf16[2048,128]{1,0:T(8,128)(2,1)}, bf16[2048,128]{1,0:T(8,128)(2,1)}, u32[]{:S(2)}, u32[]{:S(2)}) collective-permute-start(bf16[2048,128]{1,0:T(8,128)(2,1)} %bitcast.10), channel_id=1, source_target_pairs={{0,4},{1,5},{2,0},{3,1},{4,2},{5,3},{6,6},{7,7},{8,12},{9,13},{10,... | collective-permute-start | bytes 1572872 | tf_op jit(solution)/shard_map/ppermute | solution.py:259
  16.9 1.3 broadcast_select_fusion
  18.3 3.1 %collective-permute-start.3 = (bf16[2048,128]{1,0:T(8,128)(2,1)}, bf16[2048,128]{1,0:T(8,128)(2,1)}, u32[]{:S(2)}, u32[]{:S(2)}) collective-permute-start(bf16[2048,128]{1,0:T(8,128)(2,1)} %bitcast.12), channel_id=1, source_target_pairs={{0,5},{1,0},{2,1},{3,4},{4,3},{5,6},{6,7},{7,2},{8,13},{9,8},{10,9... | collective-permute-start | bytes 1572872 | tf_op jit(solution)/shard_map/ppermute | solution.py:259
  21.4 1.3 broadcast_select_fusion.3
  22.8 5.3 %collective-permute-start = (bf16[2048,128]{1,0:T(8,128)(2,1)}, bf16[2048,128]{1,0:T(8,128)(2,1)}, u32[]{:S(2)}, u32[]{:S(2)}) collective-permute-start(bf16[2048,128]{1,0:T(8,128)(2,1)} %bitcast.6), channel_id=1, source_target_pairs={{0,0},{1,1},{2,4},{3,5},{4,6},{5,7},{6,2},{7,3},{8,8},{9,9},{10,12... | collective-permute-start | bytes 1572872 | tf_op jit(solution)/shard_map/ppermute | solution.py:259
  28.1 0.0 copy-done.1
  28.1 0.1 reshape.37.fr_ref
  28.2 0.0 copy-done
  28.2 3.9 %dft.1 = (bf16[2,256,1024]{2,1,0:T(8,128)(2,1)S(1)}, bf16[2,256,1024]{2,1,0:T(8,128)(2,1)S(1)}, bf16[512,128]{1,0:T(8,128)(2,1)}, f32[1,1]{1,0:T(1,128)}) custom-call(s32[64,4]{1,0:T(8,128)S(1)} %reshape.37.fr_ref, f32[128,1024]{1,0:T(8,128)S(1)} %bitcast.29), custom_call_target="tpu_custom_call" | custom-call | tf_op jit(solution)/shard_map/dft/pallas_call | solution.py:262
  32.1 18.6 %all-to-all-start = ((bf16[64,8,128]{2,1,0:T(8,128)(2,1)}), bf16[64,8,128]{2,1,0:T(8,128)(2,1)S(1)}, u32[]{:S(2)}, u32[]{:S(2)}) async-start(bf16[64,8,128]{2,1,0:T(8,128)(2,1)} %bitcast.3), calls=%async_computation | async-start | bytes 262144 | tf_op jit(solution)/shard_map/all_to_all | solution.py:278
  50.8 0.0 collective-permute-done.1.refs_1_
  50.8 1.9 %collective-permute-start.5 = (bf16[2048,128]{1,0:T(8,128)(2,1)S(1)}, bf16[2048,128]{1,0:T(8,128)(2,1)S(1)}, u32[]{:S(2)}, u32[]{:S(2)}) collective-permute-start(bf16[2048,128]{1,0:T(8,128)(2,1)S(1)} %collective-permute-done.1.refs_1_), channel_id=1, source_target_pairs={{0,4},{4,0},{1,5},{5,1},{2,6},{6,2},{3,7},{7,3},{8,12},{12,8},{9,1... | collective-permute-start | bytes 1572872 | tf_op jit(solution)/shard_map/ppermute | solution.py:260
  52.7 0.0 collective-permute-done.2.refs_2_
  52.7 2.4 %collective-permute-start.6 = (bf16[2048,128]{1,0:T(8,128)(2,1)}, bf16[2048,128]{1,0:T(8,128)(2,1)}, u32[]{:S(2)}, u32[]{:S(2)}) collective-permute-start(bf16[2048,128]{1,0:T(8,128)(2,1)} %collective-permute-done.2.refs_2_), channel_id=1, source_target_pairs={{0,4},{4,0},{1,5},{5,1},{2,6},{6,2},{3,7},{7,3},{8,12},{12,8},{9,1... | collective-permute-start | bytes 1572872 | tf_op jit(solution)/shard_map/ppermute | solution.py:260
  55.2 0.0 collective-permute-done.3.refs_3_
  55.2 1.9 %collective-permute-start.7 = (bf16[2048,128]{1,0:T(8,128)(2,1)}, bf16[2048,128]{1,0:T(8,128)(2,1)}, u32[]{:S(2)}, u32[]{:S(2)}) collective-permute-start(bf16[2048,128]{1,0:T(8,128)(2,1)} %collective-permute-done.3.refs_3_), channel_id=1, source_target_pairs={{0,4},{4,0},{1,5},{5,1},{2,6},{6,2},{3,7},{7,3},{8,12},{12,8},{9,1... | collective-permute-start | bytes 1572872 | tf_op jit(solution)/shard_map/ppermute | solution.py:260
  57.1 0.0 collective-permute-done.refs_0_
  57.1 2.4 %collective-permute-start.4 = (bf16[2048,128]{1,0:T(8,128)(2,1)}, bf16[2048,128]{1,0:T(8,128)(2,1)}, u32[]{:S(2)}, u32[]{:S(2)}) collective-permute-start(bf16[2048,128]{1,0:T(8,128)(2,1)} %collective-permute-done.refs_0_), channel_id=1, source_target_pairs={{0,4},{4,0},{1,5},{5,1},{2,6},{6,2},{3,7},{7,3},{8,12},{12,8},{9,1... | collective-permute-start | bytes 1572872 | tf_op jit(solution)/shard_map/ppermute | solution.py:260
  59.5 8.6 %all-to-all-done = bf16[64,8,128]{2,1,0:T(8,128)(2,1)S(1)} async-done(((bf16[64,8,128]{2,1,0:T(8,128)(2,1)}), bf16[64,8,128]{2,1,0:T(8,128)(2,1)S(1)}, u32[]{:S(2)}, u32[]{:S(2)}) %all-to-all-start) | async-done | bytes 131104 | tf_op jit(solution)/shard_map/all_to_all | solution.py:278
  68.1 0.7 copy.13
  68.8 3.6 %all-to-all-start.1 = ((bf16[8,64,128]{2,1,0:T(8,128)(2,1)}), bf16[8,64,128]{2,1,0:T(8,128)(2,1)S(1)}, u32[]{:S(2)}, u32[]{:S(2)}) async-start(bf16[8,64,128]{2,1,0:T(8,128)(2,1)} %bitcast.27), calls=%async_computation.1 | async-start | bytes 262144 | tf_op jit(solution)/shard_map/all_to_all | solution.py:279
  72.4 0.1 pad_add_fusion.idx_ref
  72.4 5.2 %all-to-all-done.1.u_ref = bf16[8,64,128]{2,1,0:T(8,128)(2,1)S(1)} async-done(((bf16[8,64,128]{2,1,0:T(8,128)(2,1)}), bf16[8,64,128]{2,1,0:T(8,128)(2,1)S(1)}, u32[]{:S(2)}, u32[]{:S(2)}) %all-to-all-start.1) | async-done | bytes 131104 | tf_op jit(solution)/shard_map/all_to_all | solution.py:279
  77.6 0.0 collective-permute-done.5.refs_5_
  77.6 0.0 collective-permute-done.6.refs_6_
  77.7 0.0 collective-permute-done.7.refs_7_
  77.7 0.0 collective-permute-done.4.refs_4_
  77.7 9.9 %krylov.1 = bf16[8,208,128]{2,1,0:T(8,128)(2,1)S(1)} custom-call(s32[2]{0:T(128)S(1)} %pad_add_fusion.idx_ref, f32[1,1]{1,0:T(1,128)} %get-tuple-element.6.norm_ref, bf16[8,64,128]{2,1,0:T(8,128)(2,1)S(1)} %all-to-all-done.1.u_ref, bf16[2048,128]{1,0:T(8,128)(2,1)} %collective-permute-done.refs_0_, bf16[2048,128]{1,0:T(8,128)(2,1)S(1)} %collective-permute-done.1.refs_1_, ...), custom_call_target="tpu_custom_call" | custom-call | tf_op jit(solution)/shard_map/krylov/pallas_call | solution.py:283
  87.5 11.5 %all_to_all.20 = bf16[8,208,128]{2,1,0:T(8,128)(2,1)S(1)} all-to-all(bf16[8,208,128]{2,1,0:T(8,128)(2,1)S(1)} %krylov.1), channel_id=1, replica_groups=mesh['zx'=64,'core'=2,'rcv'=4] {'core','rcv'}, dimensions={0} | all-to-all | bytes 851968 | tf_op jit(solution)/shard_map/all_to_all | solution.py:299
  99.1 0.4 copy.10
  99.6 35.9 %all_to_all.21 = bf16[64,13,2,128]{3,2,1,0:T(2,128)(2,1)S(1)} all-to-all(bf16[64,13,2,128]{3,2,1,0:T(2,128)(2,1)S(1)} %copy.10), channel_id=1, replica_groups=mesh['zx'=64,'core'=2,'rcv'=4] {'zx'}, dimensions={0} | all-to-all | bytes 851968 | tf_op jit(solution)/shard_map/all_to_all | solution.py:304
  135.4 0.1 copy.11
  135.5 4.5 %traces.1 = (f32[2,64,1024]{2,1,0:T(8,128)}, f32[2,64,1024]{2,1,0:T(8,128)}) custom-call(bf16[26,64,128]{2,1,0:T(8,128)(2,1)S(1)} %bitcast.28, bf16[2,256,1024]{2,1,0:T(8,128)(2,1)S(1)} %get-tuple-element.8.thi_ref, bf16[2,256,1024]{2,1,0:T(8,128)(2,1)S(1)} %get-tuple-element.9.tlo_ref), custom_call_target="tpu_custom_call" | custom-call | tf_op jit(solution)/shard_map/traces/pallas_call | solution.py:307
  (4 shorter events, 0.1 us)
Async XLA Ops:
  7.8 43.0 %collective-permute-start.1 = (bf16[2048,128]{1,0:T(8,128)(2,1)}, bf16[2048,128]{1,0:T(8,128)(2,1)S(1)}, u32[]{:S(2)}, u32[]{:S(2)}) collective-permute-start(bf16[2048,128]{1,0:T(8,128)(2,1)} %bitcast.8), channel_id=1, source_target_pairs={{0,1},{1,4},{2,5},{3,0},{4,7},{5,2},{6,3},{7,6},{8,9},{9,12},{10,1... | collective-permute-start | bytes 1572872 | tf_op jit(solution)/shard_map/ppermute | solution.py:259
  11.4 16.8 %copy-start.1 = (s32[256]{0:T(256)S(1)}, s32[256]{0:T(256)}, u32[]{:S(2)}) copy-start(s32[256]{0:T(256)} %param.5) | copy-start | bytes 3076
  11.4 16.9 %copy-start = (f32[2,64,1024]{2,1,0:T(8,128)S(1)}, f32[2,64,1024]{2,1,0:T(8,128)}, u32[]{:S(2)}) copy-start(f32[2,64,1024]{2,1,0:T(8,128)} %param.3) | copy-start | bytes 1572868
  14.0 38.8 %collective-permute-start.2 = (bf16[2048,128]{1,0:T(8,128)(2,1)}, bf16[2048,128]{1,0:T(8,128)(2,1)}, u32[]{:S(2)}, u32[]{:S(2)}) collective-permute-start(bf16[2048,128]{1,0:T(8,128)(2,1)} %bitcast.10), channel_id=1, source_target_pairs={{0,4},{1,5},{2,0},{3,1},{4,2},{5,3},{6,6},{7,7},{8,12},{9,13},{10,... | collective-permute-start | bytes 1572872 | tf_op jit(solution)/shard_map/ppermute | solution.py:259
  18.3 36.9 %collective-permute-start.3 = (bf16[2048,128]{1,0:T(8,128)(2,1)}, bf16[2048,128]{1,0:T(8,128)(2,1)}, u32[]{:S(2)}, u32[]{:S(2)}) collective-permute-start(bf16[2048,128]{1,0:T(8,128)(2,1)} %bitcast.12), channel_id=1, source_target_pairs={{0,5},{1,0},{2,1},{3,4},{4,3},{5,6},{6,7},{7,2},{8,13},{9,8},{10,9... | collective-permute-start | bytes 1572872 | tf_op jit(solution)/shard_map/ppermute | solution.py:259
  22.8 34.3 %collective-permute-start = (bf16[2048,128]{1,0:T(8,128)(2,1)}, bf16[2048,128]{1,0:T(8,128)(2,1)}, u32[]{:S(2)}, u32[]{:S(2)}) collective-permute-start(bf16[2048,128]{1,0:T(8,128)(2,1)} %bitcast.6), channel_id=1, source_target_pairs={{0,0},{1,1},{2,4},{3,5},{4,6},{5,7},{6,2},{7,3},{8,8},{9,9},{10,12... | collective-permute-start | bytes 1572872 | tf_op jit(solution)/shard_map/ppermute | solution.py:259
  32.1 36.0 %all-to-all-start = ((bf16[64,8,128]{2,1,0:T(8,128)(2,1)}), bf16[64,8,128]{2,1,0:T(8,128)(2,1)S(1)}, u32[]{:S(2)}, u32[]{:S(2)}) async-start(bf16[64,8,128]{2,1,0:T(8,128)(2,1)} %bitcast.3), calls=%async_computation | async-start | bytes 262144 | tf_op jit(solution)/shard_map/all_to_all | solution.py:278
  50.8 26.8 %collective-permute-start.5 = (bf16[2048,128]{1,0:T(8,128)(2,1)S(1)}, bf16[2048,128]{1,0:T(8,128)(2,1)S(1)}, u32[]{:S(2)}, u32[]{:S(2)}) collective-permute-start(bf16[2048,128]{1,0:T(8,128)(2,1)S(1)} %collective-permute-done.1.refs_1_), channel_id=1, source_target_pairs={{0,4},{4,0},{1,5},{5,1},{2,6},{6,2},{3,7},{7,3},{8,12},{12,8},{9,1... | collective-permute-start | bytes 1572872 | tf_op jit(solution)/shard_map/ppermute | solution.py:260
  52.7 24.9 %collective-permute-start.6 = (bf16[2048,128]{1,0:T(8,128)(2,1)}, bf16[2048,128]{1,0:T(8,128)(2,1)}, u32[]{:S(2)}, u32[]{:S(2)}) collective-permute-start(bf16[2048,128]{1,0:T(8,128)(2,1)} %collective-permute-done.2.refs_2_), channel_id=1, source_target_pairs={{0,4},{4,0},{1,5},{5,1},{2,6},{6,2},{3,7},{7,3},{8,12},{12,8},{9,1... | collective-permute-start | bytes 1572872 | tf_op jit(solution)/shard_map/ppermute | solution.py:260
  55.2 22.5 %collective-permute-start.7 = (bf16[2048,128]{1,0:T(8,128)(2,1)}, bf16[2048,128]{1,0:T(8,128)(2,1)}, u32[]{:S(2)}, u32[]{:S(2)}) collective-permute-start(bf16[2048,128]{1,0:T(8,128)(2,1)} %collective-permute-done.3.refs_3_), channel_id=1, source_target_pairs={{0,4},{4,0},{1,5},{5,1},{2,6},{6,2},{3,7},{7,3},{8,12},{12,8},{9,1... | collective-permute-start | bytes 1572872 | tf_op jit(solution)/shard_map/ppermute | solution.py:260
  57.1 20.5 %collective-permute-start.4 = (bf16[2048,128]{1,0:T(8,128)(2,1)}, bf16[2048,128]{1,0:T(8,128)(2,1)}, u32[]{:S(2)}, u32[]{:S(2)}) collective-permute-start(bf16[2048,128]{1,0:T(8,128)(2,1)} %collective-permute-done.refs_0_), channel_id=1, source_target_pairs={{0,4},{4,0},{1,5},{5,1},{2,6},{6,2},{3,7},{7,3},{8,12},{12,8},{9,1... | collective-permute-start | bytes 1572872 | tf_op jit(solution)/shard_map/ppermute | solution.py:260
  68.8 8.8 %all-to-all-start.1 = ((bf16[8,64,128]{2,1,0:T(8,128)(2,1)}), bf16[8,64,128]{2,1,0:T(8,128)(2,1)S(1)}, u32[]{:S(2)}, u32[]{:S(2)}) async-start(bf16[8,64,128]{2,1,0:T(8,128)(2,1)} %bitcast.27), calls=%async_computation.1 | async-start | bytes 262144 | tf_op jit(solution)/shard_map/all_to_all | solution.py:279

commit v3 on v2

v3 whole, which is shorter than its diff:
```python
import functools
import math

import jax
import jax.numpy as jnp
from jax import lax
from jax.experimental import pallas as pl
from jax.experimental.pallas import tpu as pltpu
from jax.sharding import Mesh, PartitionSpec as P

X = 4
Y = 4
GROUP = 8
HV = 32
EXTRA = 16
HIGH = lax.Precision.HIGHEST
MIB = 1024 * 1024
COLUMN = ("core", "rcv")
SLAB = ("x", "core", "rcv")


def pick_kernel(idx_ref, k_ref, first_ref, second_ref, sems):
    upper = idx_ref[0] // 2
    copies = [
        pltpu.make_async_copy(k_ref.at[upper], first_ref, sems.at[0]),
        pltpu.make_async_copy(k_ref.at[1 - upper], second_ref, sems.at[1]),
    ]
    for copy in copies:
        copy.start()
    for copy in copies:
        copy.wait()


def angles(fr_ref, samples):
    unit = 2.0 * math.pi / samples
    fr = jnp.concatenate([fr_ref[:, n : n + 1] for n in range(fr_ref.shape[1])], axis=0)
    lane = lax.broadcasted_iota(jnp.int32, (fr.shape[0], 128), 1)
    fine = (fr * lane & (samples - 1)).astype(jnp.float32) * unit
    coarse = (fr * (lane * 128) & (samples - 1)).astype(jnp.float32) * unit
    factor = 1.0 / math.sqrt(samples)
    return jnp.cos(fine), jnp.sin(fine), jnp.cos(coarse) * factor, jnp.sin(coarse) * factor


def table_kernel(p, fr_ref, hi_ref, lo_ref):
    samples = hi_ref.shape[1]
    cos_f, sin_f, cos_c, sin_c = angles(fr_ref, samples)
    for a in range(samples // 128):
        ca, sa = cos_c[:, a : a + 1], sin_c[:, a : a + 1]
        part = slice(a * 128, (a + 1) * 128)
        value = ca * cos_f - sa * sin_f if p == 0 else -(sa * cos_f + ca * sin_f)
        top = value.astype(jnp.bfloat16)
        hi_ref[:, part] = top
        lo_ref[:, part] = (value - top.astype(jnp.float32)).astype(jnp.bfloat16)


def dft_kernel(fr_ref, rec_ref, out_ref, norm_ref, table, rows):
    deep = fr_ref.shape[0]
    samples = rec_ref.shape[1]
    cos_f, sin_f, cos_c, sin_c = angles(fr_ref, samples)
    for a in range(samples // 128):
        ca, sa = cos_c[:, a : a + 1], sin_c[:, a : a + 1]
        part = slice(a * 128, (a + 1) * 128)
        table[0, :, part] = ca * cos_f - sa * sin_f
        table[1, :, part] = -(sa * cos_f + ca * sin_f)
    rec = rec_ref[...]
    norm_ref[...] = jnp.sum(rec * rec, axis=(0, 1), keepdims=True)
    spec = [
        lax.dot_general(table[p], rec, (((1,), (1,)), ((), ())), precision=HIGH, preferred_element_type=jnp.float32)
        for p in range(2)
    ]
    for c in range(2):
        parts = [spec[p][:, (2 * src + c) * HV : (2 * src + c + 1) * HV] for src in range(2) for p in range(2)]
        both = jnp.concatenate(parts, axis=1)
        for x in range(X):
            for phi in range(Y):
                n = x * Y + phi
                start = x * GROUP + c * Y + phi
                rows[pl.ds(start, deep, stride=X * GROUP), :] = both[n * deep : (n + 1) * deep]
    out_ref[...] = rows[...].astype(jnp.bfloat16)


def quarter_turn(x):
    width = x.shape[1]
    even = lax.broadcasted_iota(jnp.int32, x.shape, 1) % 2 == 0
    return jnp.where(even, pltpu.roll(x, width - 1, 1), -pltpu.roll(x, 1, 1))


def total(x):
    return jnp.sum(x, axis=(0, 1), keepdims=True)


def length_of(x):
    return jnp.sqrt(total(x * x))


def inverse_of(x):
    return jnp.where(x > 1e-30, 1.0 / jnp.maximum(x, 1e-30), 0.0)


def krylov_kernel(idx_ref, norm_ref, u_ref, *refs):
    k_refs, g_ref = refs[:4], refs[4]
    u_rows, q_rows = refs[5:]
    deep = u_ref.shape[1]
    share = k_refs[0].shape[1]
    y, core = idx_ref[0], idx_ref[1]
    near = lax.rem(y, 2) * 2
    quarters = [(near if j % 2 == 0 else 2 - near) + (core if j < 2 else 1 - core) for j in range(4)]

    for x in range(X):
        for c in range(2):
            fields = [u_ref[x * GROUP + c * Y + ys].astype(jnp.float32) for ys in range(Y)]
            for g in range(4):
                both = jnp.concatenate([block[:, g * HV : (g + 1) * HV] for block in fields], axis=1)
                u_rows[pl.ds(x * 8 + c * 4 + g, deep, stride=8 * X), :] = both
    turned = u_rows[...].T
    u = jnp.concatenate([turned[ys * HV : (ys + 1) * HV] for ys in range(Y)], axis=1)

    def adjoint(p):
        both = jnp.concatenate([p, quarter_turn(p)], axis=0).astype(jnp.bfloat16)
        parts = [jnp.dot(both, k_ref[...], preferred_element_type=jnp.float32) for k_ref in k_refs]
        return 0.5 * jnp.concatenate(parts, axis=1)

    def forward(q):
        q = q.astype(jnp.bfloat16)
        w = sum(
            lax.dot_general(
                q[:, j * share : (j + 1) * share],
                k_refs[j][...],
                (((1,), (1,)), ((), ())),
                preferred_element_type=jnp.float32,
            )
            for j in range(4)
        )
        return 0.5 * (w[:HV] - quarter_turn(w[HV:]))

    length = length_of(u)
    scale = inverse_of(length)
    g1 = adjoint(u) * scale
    a1 = length_of(g1)
    q1 = g1 * inverse_of(a1)
    h2 = forward(q1) - (a1 * scale) * u
    b2 = length_of(h2)
    p2 = h2 * inverse_of(b2)
    g2 = adjoint(p2) - b2 * q1
    a2 = length_of(g2)
    q2 = g2 * inverse_of(a2)
    h3 = forward(q2) - a2 * p2
    b3 = length_of(h3)
    p3 = h3 * inverse_of(b3)
    g3 = adjoint(p3) - b3 * q2
    a3 = length_of(g3)
    q3 = g3 * inverse_of(a3)

    lane = lax.broadcasted_iota(jnp.int32, (EXTRA, 128), 1)
    slot = lax.rem(lane, 64) // GROUP
    values = jnp.zeros((EXTRA, 128), jnp.float32)
    for n, value in enumerate((math.sqrt(2.0) * length, a1, b2, a2, b3, a3, norm_ref[...])):
        values = jnp.where(slot == n, value, values)
    hi = values.astype(jnp.bfloat16).astype(jnp.float32)
    scalars = jnp.where(lane < 64, hi, values - hi)
    scalars = jnp.where(lax.rem(lane, GROUP) == core * Y + y, scalars, 0.0).astype(jnp.bfloat16)

    for pair in range(2):
        first, second = ((q1, q2), (q3, q3))[pair]
        q_rows[...] = jnp.concatenate([first, second], axis=0).T
        for x in range(X):
            for c in range(2):
                for j in range(4):
                    base = j * share + x * 4 + c * 2
                    even = q_rows[pl.ds(base, deep, stride=4 * X), :]
                    odd = q_rows[pl.ds(base + 1, deep, stride=4 * X), :]
                    for inner in range(2 - pair):
                        lanes = slice(inner * 64, (inner + 1) * 64)
                        both = jnp.concatenate([even[:, lanes], odd[:, lanes]], axis=1)
                        row = (2 * pair + inner) * deep
                        g_ref[x * GROUP + c * Y + quarters[j], row : row + deep, :] = both.astype(jnp.bfloat16)
    for e in range(X * GROUP):
        g_ref[e, 3 * deep : 3 * deep + EXTRA, :] = scalars


def reduced_lsqr(s, a1, b2, a2, b3, a3, rec):
    def norm(*parts):
        return jnp.sqrt(total(sum(part * part for part in parts)))

    beta = jnp.sqrt(total(rec))
    y11 = s / beta
    w1 = jnp.sqrt(jnp.maximum(1.0 - total(y11 * y11), 0.0))
    x = a1 * y11
    alpha = norm(x)
    x11 = x / alpha
    res, diag = beta, alpha
    y21, y22, w2 = a1 * x11 - alpha * y11, b2 * x11, -alpha * w1
    beta = jnp.sqrt(total(y21 * y21 + y22 * y22) + w2 * w2)
    y21, y22, w2 = y21 / beta, y22 / beta, w2 / beta
    x21, x22 = a1 * y21 + b2 * y22 - beta * x11, a2 * y22
    alpha = norm(x21, x22)
    x21, x22 = x21 / alpha, x22 / alpha

    def rotate(res, diag, beta, alpha):
        rho = jnp.sqrt(diag * diag + beta * beta)
        c, sn = diag / rho, beta / rho
        return c * res / rho, sn * alpha / rho, sn * res, -c * alpha

    step, couple, res, diag = rotate(res, diag, beta, alpha)
    sol1 = step * x11
    dir1, dir2 = x21 - couple * x11, x22
    y31, y32, y33 = a1 * x21 - alpha * y21, b2 * x21 + a2 * x22 - alpha * y22, b3 * x22
    w3 = -alpha * w2
    beta = jnp.sqrt(total(y31 * y31 + y32 * y32 + y33 * y33) + w3 * w3)
    y31, y32, y33 = y31 / beta, y32 / beta, y33 / beta
    x31 = a1 * y31 + b2 * y32 - beta * x21
    x32 = a2 * y32 + b3 * y33 - beta * x22
    x33 = a3 * y33
    alpha = norm(x31, x32, x33)
    step, couple, res, diag = rotate(res, diag, beta, alpha)
    last = res * diag / alpha
    return (sol1 + step * dir1, step * dir2), (last * x31, last * x32, last * x33)


def traces_kernel(m_ref, hi0_ref, lo0_ref, hi1_ref, lo1_ref, sol_ref, res_ref):
    scal = [m_ref[3 * X * GROUP + x].astype(jnp.float32) for x in range(X)]
    parts = []
    for n in range(7):
        top, low = n * GROUP, 64 + n * GROUP
        parts.append(
            jnp.concatenate([sc[:, top : top + GROUP] + sc[:, low : low + GROUP] for sc in scal], axis=1)
        )
    sol_c, res_c = reduced_lsqr(*parts)
    root = math.sqrt(2.0)
    sol_c, res_c = [root * w for w in sol_c], [root * w for w in res_c]
    lines = []
    for weights in (sol_c, res_c):
        for c in range(2):
            blocks = []
            for x in range(X):
                for phi in range(Y):
                    e = x * GROUP + c * Y + phi
                    blocks.append(
                        sum(w[:, e : e + 1] * m_ref[3 * e + n].astype(jnp.float32) for n, w in enumerate(weights))
                    )
            turned = jnp.concatenate(blocks, axis=0).T
            for rr in range(2):
                lines.append(
                    jnp.concatenate([turned[(2 * rr + q) * HV : (2 * rr + q + 1) * HV] for q in range(2)], axis=1)
                )
    rows = jnp.concatenate(lines, axis=0)
    hi = rows.astype(jnp.bfloat16)
    lo = (rows - hi.astype(jnp.float32)).astype(jnp.bfloat16)
    thi = jnp.concatenate([hi0_ref[...], hi1_ref[...]], axis=0)
    tlo = jnp.concatenate([lo0_ref[...], lo1_ref[...]], axis=0)

    def dot(a, b):
        return jnp.dot(a, b, preferred_element_type=jnp.float32)

    out = dot(hi, thi) + (dot(hi, tlo) + dot(lo, thi))
    for n, ref in enumerate((sol_ref, res_ref)):
        for c in range(2):
            for rr in range(2):
                row = ((n * 2 + c) * 2 + rr) * HV
                ref[rr, c * HV : (c + 1) * HV, :] = out[row : row + HV]


def body(recorded, kernel, freq_index):
    share, virtual, samples = recorded.shape
    kept = freq_index.shape[0]
    deep = kept // (X * Y)
    sources, local = kernel.shape[1], kernel.shape[3]
    core = lax.axis_index("core")
    y = lax.axis_index("rcv")
    position = jnp.stack([y, core]).astype(jnp.int32)
    anywhere = pl.BlockSpec(memory_space=pl.ANY)
    vmem = pl.BlockSpec(memory_space=pltpu.VMEM)
    smem = pl.BlockSpec(memory_space=pltpu.SMEM)
    limit = pltpu.CompilerParams(vmem_limit_bytes=32 * MIB)

    def route(flip):
        def target(c, here):
            return (here % 2) * Y + 2 * c + (here // 2 ^ flip)

        return [(c * Y + here, target(c, here)) for c in range(2) for here in range(Y)]

    payload = jax.ShapeDtypeStruct((2 * sources, local), jnp.bfloat16)
    loads = pl.pallas_call(
        pick_kernel,
        out_shape=(payload, payload),
        in_specs=[smem, anywhere],
        out_specs=(anywhere, anywhere),
        scratch_shapes=[pltpu.SemaphoreType.DMA((2,))],
        compiler_params=limit,
        name="pick",
    )(position, kernel.reshape(2, 2 * sources, local))
    blocks = [lax.ppermute(load, COLUMN, route(n)) for n, load in enumerate(loads)]
    def table(p, freqs):
        half = jax.ShapeDtypeStruct((kept, samples), jnp.bfloat16)
        return pl.pallas_call(
            functools.partial(table_kernel, p), out_shape=(half, half), compiler_params=limit, name=f"table{p}"
        )(freqs)

    freqs = freq_index.reshape(deep, X * Y)
    spec, rec_norm = pl.pallas_call(
        dft_kernel,
        out_shape=(
            jax.ShapeDtypeStruct((GROUP * X * deep, 128), jnp.bfloat16),
            jax.ShapeDtypeStruct((1, 1), jnp.float32),
        ),
        scratch_shapes=[
            pltpu.VMEM((2, kept, samples), jnp.float32),
            pltpu.VMEM((GROUP * X * deep, 128), jnp.float32),
        ],
        compiler_params=limit,
        name="dft",
    )(freqs, recorded.reshape(share * virtual, samples))

    spec, freqs = lax.optimization_barrier((spec, freqs))
    hi0, lo0 = table(0, freqs)
    spec = spec.reshape(deep, X * GROUP, 128)
    spec = lax.all_to_all(spec, "z", split_axis=0, concat_axis=0, tiled=True)
    spec, freqs, *blocks = lax.optimization_barrier((spec, freqs, *blocks))
    hi1, lo1 = table(1, freqs)
    blocks = blocks + [lax.ppermute(b, "core", [(0, 1), (1, 0)]) for b in blocks]
    spec = lax.all_to_all(spec.transpose(1, 0, 2), SLAB, split_axis=0, concat_axis=0, tiled=True)

    lines = 3 * deep + EXTRA
    vectors = pl.pallas_call(
        krylov_kernel,
        out_shape=jax.ShapeDtypeStruct((X * GROUP, lines, 128), jnp.bfloat16),
        in_specs=[smem] + [vmem] * 6,
        out_specs=vmem,
        scratch_shapes=[
            pltpu.VMEM((8 * X * deep, 128), jnp.float32),
            pltpu.VMEM((4 * local, 128), jnp.float32),
        ],
        compiler_params=limit,
        name="krylov",
    )(position, rec_norm, spec, *blocks)
    back = lax.all_to_all(vectors, SLAB, split_axis=0, concat_axis=0, tiled=True)
    data = back[:, : 3 * deep].reshape(X * GROUP, 3, deep, 128).transpose(2, 0, 1, 3)
    data = data.reshape(deep, 3 * X * GROUP, 128)
    scal = back[:, 3 * deep].astype(jnp.float32).reshape(X, GROUP, 128)
    scal = jnp.sum(scal, axis=1).astype(jnp.bfloat16)
    scal = jnp.concatenate([scal, jnp.zeros_like(scal)], axis=0)
    send = jnp.concatenate([data, jnp.broadcast_to(scal, (deep, 2 * X, 128))], axis=1)
    got = lax.all_to_all(send, "z", split_axis=0, concat_axis=0, tiled=True).transpose(1, 0, 2)

    return pl.pallas_call(
        traces_kernel,
        out_shape=tuple(jax.ShapeDtypeStruct((share, virtual, samples), jnp.float32) for _ in range(2)),
        compiler_params=limit,
        name="traces",
    )(got, hi0, lo0, hi1, lo1)


def solution(mesh):
    devices = mesh.devices
    deep = devices.shape[0] // (2 * X)
    fine = Mesh(devices.reshape(deep, X, 2, devices.shape[1]), ("z", "x", "core", "rcv"))
    traces = P(("rcv", "z", "x", "core"), None, None)
    in_specs = (traces, P(("z", "x", "core"), None, None, "rcv"), P())
    return jax.shard_map(body, mesh=fine, in_specs=in_specs, out_specs=(traces, traces), check_vma=False)
```

time: 141 us -> 124 us (0.88)
  starting transfers between devices: 45.7 us -> 18 us
  blocking collectives: 47.3 us -> 57.7 us
  waiting for transfers between devices: 13.8 us -> 22.4 us
  other arithmetic: 6.76 us -> 0.14 us
  local copies, waits for them, and re-layouts: 7.14 us -> 3.89 us
  Pallas kernels: 18.3 us -> 20.6 us
    all_to_all x2 -> x1, starting transfers between devices: 22.2 us -> 6.5 us  [body(): lax.all_to_all(send, 'z', split_axis=0, concat_axis=0, tiled=True)]
    all_to_all x2 -> x3, blocking collectives: 47.3 us -> 57.7 us  [the longest x1 28.1 us: body(): spec = lax.all_to_all(spec, 'z', split_axis=0, concat_axis=0, tiled=True)]
    ppermute x4 -> x2, starting transfers between devices: 14.8 us -> 5.41 us  [body(): lax.ppermute(load, COLUMN, route(n))]
    all_to_all x2 -> x1, waiting for transfers between devices: 13.8 us -> 22.3 us  [body(): lax.all_to_all(send, 'z', split_axis=0, concat_axis=0, tiled=True)]
    select_n x4 -> x0, other arithmetic: 6.62 us -> none  [payload(): jnp.where(low, mine[..., :width], mine[..., width:])]
    squeeze x1 -> x0, local copies, waits for them, and re-layouts: 5.79 us -> none  [payload(): mine = lax.dynamic_index_in_dim(kernel, (y + o) % 2, 0, keepdims=False)]
    pallas_call x2 -> x5, Pallas kernels: 13.8 us -> 17.1 us  [the longest x1 8.38 us: body(): pl.pallas_call(krylov_kernel, out_shape=jax.ShapeDtypeStruct((X * GROUP,...]
    ppermute x4 -> x2, starting transfers between devices: 8.66 us -> 6.06 us  [body(): lax.ppermute(b, 'core', [(0, 1), (1, 0)])]
  transfers between devices with their start and end apart: 10 -> 5, of which waited for: 2 -> 1; matrix products, arithmetic and copies ran while one was open for 4% -> 0% of each run, Pallas kernels for 3% -> 6%
where the time goes in v3:
time: 124 us
  blocking collectives  57.7 us (47%)
  waiting for transfers between devices  22.4 us (18%)
  Pallas kernels  20.6 us (17%)
  starting transfers between devices  18 us (15%)
  local copies, waits for them, and re-layouts  3.89 us (3%)
    all_to_all x1, blocking collectives, body(): spec = lax.all_to_all(spec, 'z', split_axis=0, concat_axis=0, tiled=True)  28.1 us
    all_to_all x1, waiting for transfers between devices, body(): lax.all_to_all(send, 'z', split_axis=0, concat_axis=0, tiled=True)  22.3 us
    all_to_all x1, blocking collectives, body(): lax.all_to_all(vectors, SLAB, split_axis=0, concat_axis=0, tiled=True)  15.2 us
    all_to_all x1, blocking collectives, body(): lax.all_to_all(spec.transpose(1, 0, 2), SLAB, split_axis=0, concat_axis=0...  14.5 us
    pallas_call x1, Pallas kernels, body(): pl.pallas_call(krylov_kernel, out_shape=jax.ShapeDtypeStruct((X * GROUP,...  8.38 us
    all_to_all x1, starting transfers between devices, body(): lax.all_to_all(send, 'z', split_axis=0, concat_axis=0, tiled=True)  6.5 us
    ppermute x2, starting transfers between devices, body(): lax.ppermute(b, 'core', [(0, 1), (1, 0)])  6.06 us
    ppermute x2, starting transfers between devices, body(): lax.ppermute(load, COLUMN, route(n))  5.41 us
  transfers between devices with their start and end apart: 5, of which 1 were waited for; matrix products, arithmetic and copies ran while one was open for 0% of the time, Pallas kernels for 6%

profile of v3, /device:TPU:2, one launch (start us, length us, event | category | flops | bytes accessed | tf_op | source)
XLA Modules:
  0.0 123.5 jit_solution(16707497235805274006)
XLA Ops:
  0.6 2.7 %reshape.27.k_ref = bf16[2,2048,256]{2,1,0:T(8,128)(2,1)S(1)} reshape(bf16[2,1024,2,256]{3,2,1,0:T(2,128)(2,1)} %param.4) | data formatting | bytes 4194304 | tf_op jit(solution)/shard_map/reshape | solution.py:291
  3.4 0.0 copy-start.1
  3.4 0.0 copy-start
  3.4 0.1 pad_add_fusion.idx_ref
  3.5 1.9 %pick.1 = (bf16[2048,256]{1,0:T(8,128)(2,1)}, bf16[2048,256]{1,0:T(8,128)(2,1)}) custom-call(s32[2]{0:T(128)S(1)} %pad_add_fusion.idx_ref, bf16[2,2048,256]{2,1,0:T(8,128)(2,1)S(1)} %reshape.27.k_ref), custom_call_target="tpu_custom_call" | custom-call | tf_op jit(solution)/shard_map/pick/pallas_call | solution.py:283
  5.4 1.9 %collective-permute-start = (bf16[2048,256]{1,0:T(8,128)(2,1)}, bf16[2048,256]{1,0:T(8,128)(2,1)S(1)}, u32[]{:S(2)}, u32[]{:S(2)}) collective-permute-start(bf16[2048,256]{1,0:T(8,128)(2,1)} %get-tuple-element.20), channel_id=1, source_target_pairs={{0,0},{1,4},{2,1},{3,5},{4,2},{5,6},{6,3},{7,7},{8,8},{9,12},{10,9... | collective-permute-start | bytes 3145736 | tf_op jit(solution)/shard_map/ppermute | solution.py:292
  7.3 3.5 %collective-permute-start.1 = (bf16[2048,256]{1,0:T(8,128)(2,1)}, bf16[2048,256]{1,0:T(8,128)(2,1)S(1)}, u32[]{:S(2)}, u32[]{:S(2)}) collective-permute-start(bf16[2048,256]{1,0:T(8,128)(2,1)} %get-tuple-element.21), channel_id=1, source_target_pairs={{0,1},{1,5},{2,0},{3,4},{4,3},{5,7},{6,2},{7,6},{8,9},{9,13},{10,8... | collective-permute-start | bytes 3145736 | tf_op jit(solution)/shard_map/ppermute | solution.py:292
  10.8 0.0 copy-done.1
  10.8 0.1 reshape.24.fr_ref
  10.9 0.0 copy-done
  10.9 3.6 %dft.1 = (bf16[512,128]{1,0:T(8,128)(2,1)S(1)}, f32[1,1]{1,0:T(1,128)}) custom-call(s32[16,16]{1,0:T(8,128)S(1)} %reshape.24.fr_ref, f32[128,1024]{1,0:T(8,128)S(1)} %bitcast.18), custom_call_target="tpu_custom_call" | custom-call | tf_op jit(solution)/shard_map/dft/pallas_call | solution.py:300
  14.5 28.1 %all_to_all.20 = bf16[16,32,128]{2,1,0:T(8,128)(2,1)S(1)} all-to-all(bf16[16,32,128]{2,1,0:T(8,128)(2,1)S(1)} %bitcast.19), channel_id=1, replica_groups=mesh['z'=16,'x'=4,'core'=2,'rcv'=4] {'z'}, dimensions={0} | all-to-all | bytes 262144 | tf_op jit(solution)/shard_map/all_to_all | solution.py:317
  42.7 0.0 collective-permute-done.refs_0_
  42.7 0.0 collective-permute-done.1.refs_1_
  42.7 4.1 %collective-permute-start.2 = (bf16[2048,256]{1,0:T(8,128)(2,1)S(1)}, bf16[2048,256]{1,0:T(8,128)(2,1)S(1)}, u32[]{:S(2)}, u32[]{:S(2)}) collective-permute-start(bf16[2048,256]{1,0:T(8,128)(2,1)S(1)} %collective-permute-done.refs_0_), channel_id=1, source_target_pairs={{0,4},{4,0},{1,5},{5,1},{2,6},{6,2},{3,7},{7,3},{8,12},{12,8},{9,1... | collective-permute-start | bytes 3145736 | tf_op jit(solution)/shard_map/ppermute | solution.py:320
  46.8 1.9 %collective-permute-start.3 = (bf16[2048,256]{1,0:T(8,128)(2,1)S(1)}, bf16[2048,256]{1,0:T(8,128)(2,1)S(1)}, u32[]{:S(2)}, u32[]{:S(2)}) collective-permute-start(bf16[2048,256]{1,0:T(8,128)(2,1)S(1)} %collective-permute-done.1.refs_1_), channel_id=1, source_target_pairs={{0,4},{4,0},{1,5},{5,1},{2,6},{6,2},{3,7},{7,3},{8,12},{12,8},{9,1... | collective-permute-start | bytes 3145736 | tf_op jit(solution)/shard_map/ppermute | solution.py:320
  48.7 0.1 copy.17
  48.8 14.5 %all_to_all.21.u_ref = bf16[32,16,128]{2,1,0:T(8,128)(2,1)S(1)} all-to-all(bf16[32,16,128]{2,1,0:T(8,128)(2,1)S(1)} %bitcast.21), channel_id=1, replica_groups=mesh['z'=16,'x'=4,'core'=2,'rcv'=4] {'x','core','rcv'}, dimensions={0} | all-to-all | bytes 262144 | tf_op jit(solution)/shard_map/all_to_all | solution.py:321
  63.3 0.0 collective-permute-done.2.refs_2_
  63.3 0.0 collective-permute-done.3.refs_3_
  63.3 8.4 %krylov.1 = bf16[32,64,128]{2,1,0:T(8,128)(2,1)S(1)} custom-call(s32[2]{0:T(128)S(1)} %pad_add_fusion.idx_ref, f32[1,1]{1,0:T(1,128)} %get-tuple-element.16.norm_ref, bf16[32,16,128]{2,1,0:T(8,128)(2,1)S(1)} %all_to_all.21.u_ref, bf16[2048,256]{1,0:T(8,128)(2,1)S(1)} %collective-permute-done.refs_0_, bf16[2048,256]{1,0:T(8,128)(2,1)S(1)} %collective-permute-done.1.refs_1_, ...), custom_call_target="tpu_custom_call" | custom-call | tf_op jit(solution)/shard_map/krylov/pallas_call | solution.py:324
  71.7 15.2 %all_to_all.22 = bf16[32,64,128]{2,1,0:T(8,128)(2,1)S(1)} all-to-all(bf16[32,64,128]{2,1,0:T(8,128)(2,1)S(1)} %krylov.1), channel_id=1, replica_groups=mesh['z'=16,'x'=4,'core'=2,'rcv'=4] {'x','core','rcv'}, dimensions={0} | all-to-all | bytes 1048576 | tf_op jit(solution)/shard_map/all_to_all | solution.py:336
  87.0 0.9 copy.10
  87.9 6.5 %all-to-all-start.3 = ((bf16[16,104,128]{2,1,0:T(8,128)(2,1)}), bf16[16,104,128]{2,1,0:T(8,128)(2,1)S(1)}, u32[]{:S(2)}, u32[]{:S(2)}) async-start(bf16[16,104,128]{2,1,0:T(8,128)(2,1)} %copy.10), calls=%async_computation.3 | async-start | bytes 851968 | tf_op jit(solution)/shard_map/all_to_all | solution.py:343
  94.4 1.6 %table0.1 = (bf16[256,1024]{1,0:T(8,128)(2,1)S(1)}, bf16[256,1024]{1,0:T(8,128)(2,1)S(1)}) custom-call(s32[16,16]{1,0:T(8,128)S(1)} %reshape.24.fr_ref), custom_call_target="tpu_custom_call" | custom-call | tf_op jit(solution)/shard_map/table0/pallas_call | solution.py:295
  96.0 1.6 %table1.1 = (bf16[256,1024]{1,0:T(8,128)(2,1)S(1)}, bf16[256,1024]{1,0:T(8,128)(2,1)S(1)}) custom-call(s32[16,16]{1,0:T(8,128)S(1)} %reshape.24.fr_ref), custom_call_target="tpu_custom_call" | custom-call | tf_op jit(solution)/shard_map/table1/pallas_call | solution.py:295
  97.6 22.3 %all-to-all-done.3 = bf16[16,104,128]{2,1,0:T(8,128)(2,1)S(1)} async-done(((bf16[16,104,128]{2,1,0:T(8,128)(2,1)}), bf16[16,104,128]{2,1,0:T(8,128)(2,1)S(1)}, u32[]{:S(2)}, u32[]{:S(2)}) %all-to-all-start.3) | async-done | bytes 426016 | tf_op jit(solution)/shard_map/all_to_all | solution.py:343
  120.0 0.1 copy.16
  120.0 3.5 %traces.1 = (f32[2,64,1024]{2,1,0:T(8,128)}, f32[2,64,1024]{2,1,0:T(8,128)}) custom-call(bf16[104,16,128]{2,1,0:T(8,128)(2,1)S(1)} %bitcast.17, bf16[256,1024]{1,0:T(8,128)(2,1)S(1)} %get-tuple-element.25.hi0_ref, bf16[256,1024]{1,0:T(8,128)(2,1)S(1)} %get-tuple-element.26.lo0_ref, bf16[256,1024]{1,0:T(8,128)(2,1)S(1)} %get-tuple-element.28.hi1_ref, ...), custom_call_target="tpu_custom_call" | custom-call | tf_op jit(solution)/shard_map/traces/pallas_call | solution.py:345
  (6 shorter events, 0.1 us)
Async XLA Ops:
  3.4 7.4 %copy-start.1 = (s32[256]{0:T(256)S(1)}, s32[256]{0:T(256)}, u32[]{:S(2)}) copy-start(s32[256]{0:T(256)} %param.5) | copy-start | bytes 3076
  3.4 7.5 %copy-start = (f32[2,64,1024]{2,1,0:T(8,128)S(1)}, f32[2,64,1024]{2,1,0:T(8,128)}, u32[]{:S(2)}) copy-start(f32[2,64,1024]{2,1,0:T(8,128)} %param.3) | copy-start | bytes 1572868
  5.4 37.3 %collective-permute-start = (bf16[2048,256]{1,0:T(8,128)(2,1)}, bf16[2048,256]{1,0:T(8,128)(2,1)S(1)}, u32[]{:S(2)}, u32[]{:S(2)}) collective-permute-start(bf16[2048,256]{1,0:T(8,128)(2,1)} %get-tuple-element.20), channel_id=1, source_target_pairs={{0,0},{1,4},{2,1},{3,5},{4,2},{5,6},{6,3},{7,7},{8,8},{9,12},{10,9... | collective-permute-start | bytes 3145736 | tf_op jit(solution)/shard_map/ppermute | solution.py:292
  7.3 35.4 %collective-permute-start.1 = (bf16[2048,256]{1,0:T(8,128)(2,1)}, bf16[2048,256]{1,0:T(8,128)(2,1)S(1)}, u32[]{:S(2)}, u32[]{:S(2)}) collective-permute-start(bf16[2048,256]{1,0:T(8,128)(2,1)} %get-tuple-element.21), channel_id=1, source_target_pairs={{0,1},{1,5},{2,0},{3,4},{4,3},{5,7},{6,2},{7,6},{8,9},{9,13},{10,8... | collective-permute-start | bytes 3145736 | tf_op jit(solution)/shard_map/ppermute | solution.py:292
  42.7 20.6 %collective-permute-start.2 = (bf16[2048,256]{1,0:T(8,128)(2,1)S(1)}, bf16[2048,256]{1,0:T(8,128)(2,1)S(1)}, u32[]{:S(2)}, u32[]{:S(2)}) collective-permute-start(bf16[2048,256]{1,0:T(8,128)(2,1)S(1)} %collective-permute-done.refs_0_), channel_id=1, source_target_pairs={{0,4},{4,0},{1,5},{5,1},{2,6},{6,2},{3,7},{7,3},{8,12},{12,8},{9,1... | collective-permute-start | bytes 3145736 | tf_op jit(solution)/shard_map/ppermute | solution.py:320
  46.8 16.5 %collective-permute-start.3 = (bf16[2048,256]{1,0:T(8,128)(2,1)S(1)}, bf16[2048,256]{1,0:T(8,128)(2,1)S(1)}, u32[]{:S(2)}, u32[]{:S(2)}) collective-permute-start(bf16[2048,256]{1,0:T(8,128)(2,1)S(1)} %collective-permute-done.1.refs_1_), channel_id=1, source_target_pairs={{0,4},{4,0},{1,5},{5,1},{2,6},{6,2},{3,7},{7,3},{8,12},{12,8},{9,1... | collective-permute-start | bytes 3145736 | tf_op jit(solution)/shard_map/ppermute | solution.py:320
  87.9 32.1 %all-to-all-start.3 = ((bf16[16,104,128]{2,1,0:T(8,128)(2,1)}), bf16[16,104,128]{2,1,0:T(8,128)(2,1)S(1)}, u32[]{:S(2)}, u32[]{:S(2)}) async-start(bf16[16,104,128]{2,1,0:T(8,128)(2,1)} %copy.10), calls=%async_computation.3 | async-start | bytes 851968 | tf_op jit(solution)/shard_map/all_to_all | solution.py:343

commit v4 on v3

--- a/solution.py
+++ b/solution.py
@@ -97,15 +97,62 @@
     return jnp.where(x > 1e-30, 1.0 / jnp.maximum(x, 1e-30), 0.0)
 
 
-def krylov_kernel(idx_ref, norm_ref, u_ref, *refs):
-    k_refs, g_ref = refs[:4], refs[4]
-    u_rows, q_rows = refs[5:]
-    deep = u_ref.shape[1]
+def apply_adjoint(p, k_refs):
+    both = jnp.concatenate([p, quarter_turn(p)], axis=0).astype(jnp.bfloat16)
+    depth = both.shape[1] // 2
+    parts = [jnp.dot(both, k_ref[...], preferred_element_type=jnp.float32) for k_ref in k_refs[:2]]
+    for top, low in (k_refs[2:4], k_refs[4:6]):
+        parts.append(
+            jnp.dot(both[:, :depth], top[...], preferred_element_type=jnp.float32)
+            + jnp.dot(both[:, depth:], low[...], preferred_element_type=jnp.float32)
+        )
+    return 0.5 * jnp.concatenate(parts, axis=1)
+
+
+def apply_forward(q, k_refs):
+    q = q.astype(jnp.bfloat16)
     share = k_refs[0].shape[1]
+
+    def product(j, k_ref):
+        part = q[:, j * share : (j + 1) * share]
+        return lax.dot_general(part, k_ref[...], (((1,), (1,)), ((), ())), preferred_element_type=jnp.float32)
+
+    w = product(0, k_refs[0]) + product(1, k_refs[1])
+    tops = product(2, k_refs[2]) + product(3, k_refs[4])
+    lows = product(2, k_refs[3]) + product(3, k_refs[5])
+    w = w + jnp.concatenate([tops, lows], axis=1)
+    return 0.5 * (w[:HV] - quarter_turn(w[HV:]))
+
+
+def fill(row, entries):
+    slot = lax.rem(lax.broadcasted_iota(jnp.int32, row.shape, 1), 64) // GROUP
+    for n, value in entries:
+        row = jnp.where(slot == n, value, row)
+    return row
+
+
+def write_vectors(idx_ref, q_rows, first, second, count, g_ref, deep):
     y, core = idx_ref[0], idx_ref[1]
     near = lax.rem(y, 2) * 2
     quarters = [(near if j % 2 == 0 else 2 - near) + (core if j < 2 else 1 - core) for j in range(4)]
-
+    share = first.shape[1] // 4
+    q_rows[...] = jnp.concatenate([first, second], axis=0).T
+    for x in range(X):
+        for c in range(2):
+            for j in range(4):
+                base = j * share + x * 4 + c * 2
+                even = q_rows[pl.ds(base, deep, stride=4 * X), :]
+                odd = q_rows[pl.ds(base + 1, deep, stride=4 * X), :]
+                for n in range(count):
+                    lanes = slice(n * 64, (n + 1) * 64)
+                    both = jnp.concatenate([even[:, lanes], odd[:, lanes]], axis=1)
+                    g_ref[x * GROUP + c * Y + quarters[j], n * deep : (n + 1) * deep, :] = both.astype(jnp.bfloat16)
+
+
+def krylov_first_kernel(idx_ref, norm_ref, u_ref, *refs):
+    k_refs = refs[:6]
+    g_ref, p_ref, q_ref, a_ref, row_ref, u_rows, q_rows = refs[6:]
+    deep = u_ref.shape[1]
     for x in range(X):
         for c in range(2):
             fields = [u_ref[x * GROUP + c * Y + ys].astype(jnp.float32) for ys in range(Y)]
@@ -115,67 +162,45 @@
     turned = u_rows[...].T
     u = jnp.concatenate([turned[ys * HV : (ys + 1) * HV] for ys in range(Y)], axis=1)
 
-    def adjoint(p):
-        both = jnp.concatenate([p, quarter_turn(p)], axis=0).astype(jnp.bfloat16)
-        parts = [jnp.dot(both, k_ref[...], preferred_element_type=jnp.float32) for k_ref in k_refs]
-        return 0.5 * jnp.concatenate(parts, axis=1)
-
-    def forward(q):
-        q = q.astype(jnp.bfloat16)
-        w = sum(
-            lax.dot_general(
-                q[:, j * share : (j + 1) * share],
-                k_refs[j][...],
-                (((1,), (1,)), ((), ())),
-                preferred_element_type=jnp.float32,
-            )
-            for j in range(4)
-        )
-        return 0.5 * (w[:HV] - quarter_turn(w[HV:]))
-
     length = length_of(u)
     scale = inverse_of(length)
-    g1 = adjoint(u) * scale
+    g1 = apply_adjoint(u, k_refs) * scale
     a1 = length_of(g1)
     q1 = g1 * inverse_of(a1)
-    h2 = forward(q1) - (a1 * scale) * u
+    h2 = apply_forward(q1, k_refs) - (a1 * scale) * u
     b2 = length_of(h2)
     p2 = h2 * inverse_of(b2)
-    g2 = adjoint(p2) - b2 * q1
+    g2 = apply_adjoint(p2, k_refs) - b2 * q1
     a2 = length_of(g2)
     q2 = g2 * inverse_of(a2)
-    h3 = forward(q2) - a2 * p2
+    p_ref[...] = p2
+    q_ref[...] = q2
+    a_ref[...] = a2
+    entries = ((0, math.sqrt(2.0) * length), (1, a1), (2, b2), (3, a2), (6, norm_ref[...]))
+    row_ref[...] = fill(jnp.zeros((EXTRA, 128), jnp.float32), entries)
+    write_vectors(idx_ref, q_rows, q1, q2, 2, g_ref, deep)
+
+
+def krylov_second_kernel(idx_ref, p_ref, q_ref, a_ref, row_ref, *refs):
+    k_refs = refs[:6]
+    g_ref, q_rows = refs[6:]
+    deep = g_ref.shape[1] - EXTRA
+    q2 = q_ref[...]
+    h3 = apply_forward(q2, k_refs) - a_ref[...] * p_ref[...]
     b3 = length_of(h3)
     p3 = h3 * inverse_of(b3)
-    g3 = adjoint(p3) - b3 * q2
+    g3 = apply_adjoint(p3, k_refs) - b3 * q2
     a3 = length_of(g3)
     q3 = g3 * inverse_of(a3)
-
+    values = fill(row_ref[...], ((4, b3), (5, a3)))
     lane = lax.broadcasted_iota(jnp.int32, (EXTRA, 128), 1)
-    slot = lax.rem(lane, 64) // GROUP
-    values = jnp.zeros((EXTRA, 128), jnp.float32)
-    for n, value in enumerate((math.sqrt(2.0) * length, a1, b2, a2, b3, a3, norm_ref[...])):
-        values = jnp.where(slot == n, value, values)
     hi = values.astype(jnp.bfloat16).astype(jnp.float32)
     scalars = jnp.where(lane < 64, hi, values - hi)
-    scalars = jnp.where(lax.rem(lane, GROUP) == core * Y + y, scalars, 0.0).astype(jnp.bfloat16)
-
-    for pair in range(2):
-        first, second = ((q1, q2), (q3, q3))[pair]
-        q_rows[...] = jnp.concatenate([first, second], axis=0).T
-        for x in range(X):
-            for c in range(2):
-                for j in range(4):
-                    base = j * share + x * 4 + c * 2
-                    even = q_rows[pl.ds(base, deep, stride=4 * X), :]
-                    odd = q_rows[pl.ds(base + 1, deep, stride=4 * X), :]
-                    for inner in range(2 - pair):
-                        lanes = slice(inner * 64, (inner + 1) * 64)
-                        both = jnp.concatenate([even[:, lanes], odd[:, lanes]], axis=1)
-                        row = (2 * pair + inner) * deep
-                        g_ref[x * GROUP + c * Y + quarters[j], row : row + deep, :] = both.astype(jnp.bfloat16)
+    mine = idx_ref[1] * Y + idx_ref[0]
+    scalars = jnp.where(lax.rem(lane, GROUP) == mine, scalars, 0.0).astype(jnp.bfloat16)
+    write_vectors(idx_ref, q_rows, q3, q3, 1, g_ref, deep)
     for e in range(X * GROUP):
-        g_ref[e, 3 * deep : 3 * deep + EXTRA, :] = scalars
+        g_ref[e, deep : deep + EXTRA, :] = scalars
 
 
 def reduced_lsqr(s, a1, b2, a2, b3, a3, rec):
@@ -217,8 +242,8 @@
     return (sol1 + step * dir1, step * dir2), (last * x31, last * x32, last * x33)
 
 
-def traces_kernel(m_ref, hi0_ref, lo0_ref, hi1_ref, lo1_ref, sol_ref, res_ref):
-    scal = [m_ref[3 * X * GROUP + x].astype(jnp.float32) for x in range(X)]
+def traces_kernel(m_ref, last_ref, hi0_ref, lo0_ref, hi1_ref, lo1_ref, sol_ref, res_ref):
+    scal = [last_ref[X * GROUP + x].astype(jnp.float32) for x in range(X)]
     parts = []
     for n in range(7):
         top, low = n * GROUP, 64 + n * GROUP
@@ -235,9 +260,12 @@
             for x in range(X):
                 for phi in range(Y):
                     e = x * GROUP + c * Y + phi
-                    blocks.append(
-                        sum(w[:, e : e + 1] * m_ref[3 * e + n].astype(jnp.float32) for n, w in enumerate(weights))
+                    block = sum(
+                        w[:, e : e + 1] * m_ref[2 * e + n].astype(jnp.float32) for n, w in enumerate(weights[:2])
                     )
+                    for w in weights[2:]:
+                        block = block + w[:, e : e + 1] * last_ref[e].astype(jnp.float32)
+                    blocks.append(block)
             turned = jnp.concatenate(blocks, axis=0).T
             for rr in range(2):
                 lines.append(
@@ -311,43 +339,64 @@
         name="dft",
     )(freqs, recorded.reshape(share * virtual, samples))
 
-    spec, freqs = lax.optimization_barrier((spec, freqs))
+    spec, freqs, *blocks = lax.optimization_barrier((spec, freqs, *blocks))
     hi0, lo0 = table(0, freqs)
+    hi1, lo1 = table(1, freqs)
+    for b in blocks[:2]:
+        halves = b[:sources], b[sources:]
+        blocks = blocks + [lax.ppermute(half, "core", [(0, 1), (1, 0)]) for half in halves]
     spec = spec.reshape(deep, X * GROUP, 128)
     spec = lax.all_to_all(spec, "z", split_axis=0, concat_axis=0, tiled=True)
-    spec, freqs, *blocks = lax.optimization_barrier((spec, freqs, *blocks))
-    hi1, lo1 = table(1, freqs)
-    blocks = blocks + [lax.ppermute(b, "core", [(0, 1), (1, 0)]) for b in blocks]
     spec = lax.all_to_all(spec.transpose(1, 0, 2), SLAB, split_axis=0, concat_axis=0, tiled=True)
 
-    lines = 3 * deep + EXTRA
-    vectors = pl.pallas_call(
-        krylov_kernel,
-        out_shape=jax.ShapeDtypeStruct((X * GROUP, lines, 128), jnp.bfloat16),
-        in_specs=[smem] + [vmem] * 6,
+    slab = X * GROUP
+    q_rows = pltpu.VMEM((4 * local, 128), jnp.float32)
+    single = jax.ShapeDtypeStruct((1, 1), jnp.float32)
+    row = jax.ShapeDtypeStruct((EXTRA, 128), jnp.float32)
+    pair, *state = pl.pallas_call(
+        krylov_first_kernel,
+        out_shape=(
+            jax.ShapeDtypeStruct((slab, 2 * deep, 128), jnp.bfloat16),
+            jax.ShapeDtypeStruct((HV, 2 * sources), jnp.float32),
+            jax.ShapeDtypeStruct((2 * HV, 4 * local), jnp.float32),
+            single,
+            row,
+        ),
+        in_specs=[smem] + [vmem] * 8,
+        out_specs=(vmem,) * 5,
+        scratch_shapes=[pltpu.VMEM((8 * slab * deep // GROUP, 128), jnp.float32), q_rows],
+        compiler_params=limit,
+        name="krylov_first",
+    )(position, rec_norm, spec, *blocks)
+    pair = lax.all_to_all(pair, SLAB, split_axis=0, concat_axis=0, tiled=True)
+    pair = pair.reshape(slab, 2, deep, 128).transpose(2, 0, 1, 3).reshape(deep, 2 * slab, 128)
+
+    last = pl.pallas_call(
+        krylov_second_kernel,
+        out_shape=jax.ShapeDtypeStruct((slab, deep + EXTRA, 128), jnp.bfloat16),
+        in_specs=[smem] + [vmem] * 10,
         out_specs=vmem,
-        scratch_shapes=[
-            pltpu.VMEM((8 * X * deep, 128), jnp.float32),
-            pltpu.VMEM((4 * local, 128), jnp.float32),
-        ],
+        scratch_shapes=[q_rows],
         compiler_params=limit,
-        name="krylov",
-    )(position, rec_norm, spec, *blocks)
-    back = lax.all_to_all(vectors, SLAB, split_axis=0, concat_axis=0, tiled=True)
-    data = back[:, : 3 * deep].reshape(X * GROUP, 3, deep, 128).transpose(2, 0, 1, 3)
-    data = data.reshape(deep, 3 * X * GROUP, 128)
-    scal = back[:, 3 * deep].astype(jnp.float32).reshape(X, GROUP, 128)
+        cost_estimate=pl.CostEstimate(
+            flops=8 * HV * 2 * sources * 4 * local, bytes_accessed=16 * sources * local, transcendentals=0
+        ),
+        name="krylov_second",
+    )(position, *state, *blocks)
+    last = lax.all_to_all(last, SLAB, split_axis=0, concat_axis=0, tiled=True)
+    scal = last[:, deep].astype(jnp.float32).reshape(X, GROUP, 128)
     scal = jnp.sum(scal, axis=1).astype(jnp.bfloat16)
-    scal = jnp.concatenate([scal, jnp.zeros_like(scal)], axis=0)
-    send = jnp.concatenate([data, jnp.broadcast_to(scal, (deep, 2 * X, 128))], axis=1)
-    got = lax.all_to_all(send, "z", split_axis=0, concat_axis=0, tiled=True).transpose(1, 0, 2)
-
+    scal = jnp.concatenate([scal, jnp.zeros((8 - X, 128), jnp.bfloat16)], axis=0)
+    last = jnp.concatenate([last[:, :deep].transpose(1, 0, 2), jnp.broadcast_to(scal, (deep, 8, 128))], axis=1)
+
+    pair = lax.all_to_all(pair, "z", split_axis=0, concat_axis=0, tiled=True).transpose(1, 0, 2)
+    last = lax.all_to_all(last, "z", split_axis=0, concat_axis=0, tiled=True).transpose(1, 0, 2)
     return pl.pallas_call(
         traces_kernel,
         out_shape=tuple(jax.ShapeDtypeStruct((share, virtual, samples), jnp.float32) for _ in range(2)),
         compiler_params=limit,
         name="traces",
-    )(got, hi0, lo0, hi1, lo1)
+    )(pair, last, hi0, lo0, hi1, lo1)
 
 
 def solution(mesh):

time: 124 us -> 172 us (1.39)
  the two profiles are of different devices: /device:TPU:2 before, /device:TPU:32 now
where the time goes in v4:
time: 172 us; the launch traced here: 171 us
  waiting for transfers between devices  74.7 us (43%)
  starting transfers between devices  50.3 us (29%)
  Pallas kernels  24.6 us (14%)
  blocking collectives  12.7 us (7%)
  local copies, waits for them, and re-layouts  7.51 us (4%)
    ppermute x2, waiting for transfers between devices, body(): lax.ppermute(load, COLUMN, route(n))  20.6 us
    all_to_all x1, starting transfers between devices, body(): spec = lax.all_to_all(spec, 'z', split_axis=0, concat_axis=0, tiled=True)  15.2 us
    all_to_all x1, waiting for transfers between devices, body(): lax.all_to_all(pair, 'z', split_axis=0, concat_axis=0, tiled=True)  14.8 us
    all_to_all x1, waiting for transfers between devices, body(): lax.all_to_all(last, 'z', split_axis=0, concat_axis=0, tiled=True)  14.1 us
    all_to_all x1, blocking collectives, body(): last = lax.all_to_all(last, SLAB, split_axis=0, concat_axis=0, tiled=True)  12.7 us
    ppermute x4, starting transfers between devices, body(): lax.ppermute(half, 'core', [(0, 1), (1, 0)])  10.8 us
    all_to_all x1, waiting for transfers between devices, body(): spec = lax.all_to_all(spec, 'z', split_axis=0, concat_axis=0, tiled=True)  9.1 us
    all_to_all x1, waiting for transfers between devices, body(): pair = lax.all_to_all(pair, SLAB, split_axis=0, concat_axis=0, tiled=True)  8.32 us
  transfers between devices with their start and end apart: 11, of which 6 were waited for; matrix products, arithmetic and copies ran while one was open for 2% of the time, Pallas kernels for 4%

profile of v4, /device:TPU:32, one launch (start us, length us, event | category | flops | bytes accessed | tf_op | source)
XLA Modules:
  0.0 170.9 jit_solution(9238651540744668242)
XLA Ops:
  0.6 2.7 %reshape.26.k_ref = bf16[2,2048,256]{2,1,0:T(8,128)(2,1)S(1)} reshape(bf16[2,1024,2,256]{3,2,1,0:T(2,128)(2,1)} %param.4) | data formatting | bytes 4194304 | tf_op jit(solution)/shard_map/reshape | solution.py:319
  3.4 0.0 copy-start.1
  3.4 0.0 copy-start
  3.4 0.1 pad_add_fusion.idx_ref
  3.5 1.9 %pick.1 = (bf16[2048,256]{1,0:T(8,128)(2,1)}, bf16[2048,256]{1,0:T(8,128)(2,1)}) custom-call(s32[2]{0:T(128)S(1)} %pad_add_fusion.idx_ref, bf16[2,2048,256]{2,1,0:T(8,128)(2,1)S(1)} %reshape.26.k_ref), custom_call_target="tpu_custom_call" | custom-call | tf_op jit(solution)/shard_map/pick/pallas_call | solution.py:311
  5.4 1.9 %collective-permute-start = (bf16[2048,256]{1,0:T(8,128)(2,1)}, bf16[2048,256]{1,0:T(8,128)(2,1)S(1)}, u32[]{:S(2)}, u32[]{:S(2)}) collective-permute-start(bf16[2048,256]{1,0:T(8,128)(2,1)} %get-tuple-element.21), channel_id=1, source_target_pairs={{0,0},{1,4},{2,1},{3,5},{4,2},{5,6},{6,3},{7,7},{8,8},{9,12},{10,9... | collective-permute-start | bytes 3145736 | tf_op jit(solution)/shard_map/ppermute | solution.py:320
  7.3 3.5 %collective-permute-start.1 = (bf16[2048,256]{1,0:T(8,128)(2,1)}, bf16[2048,256]{1,0:T(8,128)(2,1)S(1)}, u32[]{:S(2)}, u32[]{:S(2)}) collective-permute-start(bf16[2048,256]{1,0:T(8,128)(2,1)} %get-tuple-element.22), channel_id=1, source_target_pairs={{0,1},{1,5},{2,0},{3,4},{4,3},{5,7},{6,2},{7,6},{8,9},{9,13},{10,8... | collective-permute-start | bytes 3145736 | tf_op jit(solution)/shard_map/ppermute | solution.py:320
  10.8 0.0 copy-done.1
  10.8 0.1 reshape.24.fr_ref
  10.9 0.0 copy-done
  10.9 4.0 %dft.1 = (bf16[512,128]{1,0:T(8,128)(2,1)}, f32[1,1]{1,0:T(1,128)}) custom-call(s32[16,16]{1,0:T(8,128)S(1)} %reshape.24.fr_ref, f32[128,1024]{1,0:T(8,128)S(1)} %bitcast.23), custom_call_target="tpu_custom_call" | custom-call | tf_op jit(solution)/shard_map/dft/pallas_call | solution.py:328
  14.9 0.0 collective-permute-done.refs_0_
  14.9 20.6 %collective-permute-done.1.refs_1_ = bf16[2048,256]{1,0:T(8,128)(2,1)S(1)} collective-permute-done((bf16[2048,256]{1,0:T(8,128)(2,1)}, bf16[2048,256]{1,0:T(8,128)(2,1)S(1)}, u32[]{:S(2)}, u32[]{:S(2)}) %collective-permute-start.1) | collective-permute-done | bytes 1048608 | tf_op jit(solution)/shard_map/ppermute | solution.py:320
  35.5 1.0 fusion.1
  36.6 4.6 %collective-permute-start.2 = (bf16[1024,256]{1,0:T(8,128)(2,1)}, bf16[1024,256]{1,0:T(8,128)(2,1)S(1)}, u32[]{:S(2)}, u32[]{:S(2)}) collective-permute-start(bf16[1024,256]{1,0:T(8,128)(2,1)} %get-tuple-element.39), channel_id=1, source_target_pairs={{0,4},{4,0},{1,5},{5,1},{2,6},{6,2},{3,7},{7,3},{8,12},{12,8},{9,1... | collective-permute-start | bytes 1572872 | tf_op jit(solution)/shard_map/ppermute | solution.py:347
  41.1 1.9 %collective-permute-start.3 = (bf16[1024,256]{1,0:T(8,128)(2,1)}, bf16[1024,256]{1,0:T(8,128)(2,1)S(1)}, u32[]{:S(2)}, u32[]{:S(2)}) collective-permute-start(bf16[1024,256]{1,0:T(8,128)(2,1)} %get-tuple-element.38), channel_id=1, source_target_pairs={{0,4},{4,0},{1,5},{5,1},{2,6},{6,2},{3,7},{7,3},{8,12},{12,8},{9,1... | collective-permute-start | bytes 1572872 | tf_op jit(solution)/shard_map/ppermute | solution.py:347
  43.0 15.2 %all-to-all-start = ((bf16[16,32,128]{2,1,0:T(8,128)(2,1)}), bf16[16,32,128]{2,1,0:T(8,128)(2,1)S(1)}, u32[]{:S(2)}, u32[]{:S(2)}) async-start(bf16[16,32,128]{2,1,0:T(8,128)(2,1)} %bitcast.3), calls=%async_computation | async-start | bytes 262144 | tf_op jit(solution)/shard_map/all_to_all | solution.py:349
  58.3 1.0 fusion
  59.3 1.9 %collective-permute-start.4 = (bf16[1024,256]{1,0:T(8,128)(2,1)}, bf16[1024,256]{1,0:T(8,128)(2,1)}, u32[]{:S(2)}, u32[]{:S(2)}) collective-permute-start(bf16[1024,256]{1,0:T(8,128)(2,1)} %get-tuple-element.37), channel_id=1, source_target_pairs={{0,4},{4,0},{1,5},{5,1},{2,6},{6,2},{3,7},{7,3},{8,12},{12,8},{9,1... | collective-permute-start | bytes 1572872 | tf_op jit(solution)/shard_map/ppermute | solution.py:347
  61.2 2.4 %collective-permute-start.5 = (bf16[1024,256]{1,0:T(8,128)(2,1)}, bf16[1024,256]{1,0:T(8,128)(2,1)}, u32[]{:S(2)}, u32[]{:S(2)}) collective-permute-start(bf16[1024,256]{1,0:T(8,128)(2,1)} %get-tuple-element.36), channel_id=1, source_target_pairs={{0,4},{4,0},{1,5},{5,1},{2,6},{6,2},{3,7},{7,3},{8,12},{12,8},{9,1... | collective-permute-start | bytes 1572872 | tf_op jit(solution)/shard_map/ppermute | solution.py:347
  63.6 9.1 %all-to-all-done = bf16[16,32,128]{2,1,0:T(8,128)(2,1)S(1)} async-done(((bf16[16,32,128]{2,1,0:T(8,128)(2,1)}), bf16[16,32,128]{2,1,0:T(8,128)(2,1)S(1)}, u32[]{:S(2)}, u32[]{:S(2)}) %all-to-all-start) | async-done | bytes 131104 | tf_op jit(solution)/shard_map/all_to_all | solution.py:349
  72.7 0.7 copy.18
  73.5 5.2 %all-to-all-start.1 = ((bf16[32,16,128]{2,1,0:T(8,128)(2,1)}), bf16[32,16,128]{2,1,0:T(8,128)(2,1)S(1)}, u32[]{:S(2)}, u32[]{:S(2)}) async-start(bf16[32,16,128]{2,1,0:T(8,128)(2,1)} %bitcast.20), calls=%async_computation.1 | async-start | bytes 262144 | tf_op jit(solution)/shard_map/all_to_all | solution.py:350
  78.7 0.0 collective-permute-done.2.refs_2_
  78.7 0.0 collective-permute-done.3.refs_3_
  78.7 0.0 collective-permute-done.4.refs_4_
  78.7 0.0 collective-permute-done.5.refs_5_
  78.7 7.8 %all-to-all-done.1.u_ref = bf16[32,16,128]{2,1,0:T(8,128)(2,1)S(1)} async-done(((bf16[32,16,128]{2,1,0:T(8,128)(2,1)}), bf16[32,16,128]{2,1,0:T(8,128)(2,1)S(1)}, u32[]{:S(2)}, u32[]{:S(2)}) %all-to-all-start.1) | async-done | bytes 131104 | tf_op jit(solution)/shard_map/all_to_all | solution.py:350
  86.5 7.1 %krylov_first.1 = (bf16[32,32,128]{2,1,0:T(8,128)(2,1)}, f32[32,2048]{1,0:T(8,128)S(1)}, f32[64,1024]{1,0:T(8,128)S(1)}, f32[1,1]{1,0:T(1,128)}, f32[16,128]{1,0:T(8,128)S(1)}) custom-call(s32[2]{0:T(128)S(1)} %pad_add_fusion.idx_ref, f32[1,1]{1,0:T(1,128)} %get-tuple-element.19.norm_ref, bf16[32,16,128]{2,1,0:T(8,128)(2,1)S(1)} %all-to-all-done.1.u_ref, ...), custom_call_target="tpu_custom_call" | custom-call | tf_op jit(solution)/shard_map/krylov_first/pallas_call | solution.py:356
  93.6 5.0 %krylov_second.1 = bf16[32,32,128]{2,1,0:T(8,128)(2,1)S(1)} custom-call(s32[2]{0:T(128)S(1)} %pad_add_fusion.idx_ref, f32[32,2048]{1,0:T(8,128)S(1)} %get-tuple-element.27.p_ref, f32[64,1024]{1,0:T(8,128)S(1)} %get-tuple-element.28.q_ref, f32[1,1]{1,0:T(1,128)} %get-tuple-element.29.a_ref, f32[16,128]{1,0:T(8,128)S(1)} %get-tuple-element.30.row_ref, ...), custom_call_target="tpu_custom_call" | custom-call | flops 536870912 | bytes 4194304 | tf_op jit(solution)/shard_map/krylov_second/pallas_call | solution.py:374
  98.6 12.7 %all_to_all.30 = bf16[32,32,128]{2,1,0:T(8,128)(2,1)S(1)} all-to-all(bf16[32,32,128]{2,1,0:T(8,128)(2,1)S(1)} %krylov_second.1), channel_id=1, replica_groups=mesh['z'=16,'x'=4,'core'=2,'rcv'=4] {'x','core','rcv'}, dimensions={0} | all-to-all | bytes 524288 | tf_op jit(solution)/shard_map/all_to_all | solution.py:386
  111.3 3.9 %all-to-all-start.2 = ((bf16[32,32,128]{2,1,0:T(8,128)(2,1)}), bf16[32,32,128]{2,1,0:T(8,128)(2,1)S(1)}, u32[]{:S(2)}, u32[]{:S(2)}) async-start(bf16[32,32,128]{2,1,0:T(8,128)(2,1)} %get-tuple-element.26), calls=%async_computation.2 | async-start | bytes 524288 | tf_op jit(solution)/shard_map/all_to_all | solution.py:371
  115.3 0.7 copy.9
  116.0 8.3 %all-to-all-done.2 = bf16[32,32,128]{2,1,0:T(8,128)(2,1)S(1)} async-done(((bf16[32,32,128]{2,1,0:T(8,128)(2,1)}), bf16[32,32,128]{2,1,0:T(8,128)(2,1)S(1)}, u32[]{:S(2)}, u32[]{:S(2)}) %all-to-all-start.2) | async-done | bytes 262176 | tf_op jit(solution)/shard_map/all_to_all | solution.py:371
  124.3 4.8 %all-to-all-start.5 = ((bf16[16,40,128]{2,1,0:T(8,128)(2,1)}), bf16[16,40,128]{2,1,0:T(8,128)(2,1)S(1)}, u32[]{:S(2)}, u32[]{:S(2)}) async-start(bf16[16,40,128]{2,1,0:T(8,128)(2,1)} %copy.9), calls=%async_computation.5 | async-start | bytes 327680 | tf_op jit(solution)/shard_map/all_to_all | solution.py:393
  129.1 0.9 copy.7
  130.1 14.1 %all-to-all-done.5 = bf16[16,40,128]{2,1,0:T(8,128)(2,1)S(1)} async-done(((bf16[16,40,128]{2,1,0:T(8,128)(2,1)}), bf16[16,40,128]{2,1,0:T(8,128)(2,1)S(1)}, u32[]{:S(2)}, u32[]{:S(2)}) %all-to-all-start.5) | async-done | bytes 163872 | tf_op jit(solution)/shard_map/all_to_all | solution.py:393
  144.2 5.0 %all-to-all-start.3 = ((bf16[16,64,128]{2,1,0:T(8,128)(2,1)}), bf16[16,64,128]{2,1,0:T(8,128)(2,1)S(1)}, u32[]{:S(2)}, u32[]{:S(2)}) async-start(bf16[16,64,128]{2,1,0:T(8,128)(2,1)} %bitcast.7), calls=%async_computation.3 | async-start | bytes 524288 | tf_op jit(solution)/shard_map/all_to_all | solution.py:392
  149.2 1.6 table0.1
  150.8 1.6 table1.1
  152.5 14.8 %all-to-all-done.3 = bf16[16,64,128]{2,1,0:T(8,128)(2,1)S(1)} async-done(((bf16[16,64,128]{2,1,0:T(8,128)(2,1)}), bf16[16,64,128]{2,1,0:T(8,128)(2,1)S(1)}, u32[]{:S(2)}, u32[]{:S(2)}) %all-to-all-start.3) | async-done | bytes 262176 | tf_op jit(solution)/shard_map/all_to_all | solution.py:392
  167.2 0.2 copy.16
  167.4 3.5 %traces.1 = (f32[2,64,1024]{2,1,0:T(8,128)}, f32[2,64,1024]{2,1,0:T(8,128)}) custom-call(bf16[64,16,128]{2,1,0:T(8,128)(2,1)S(1)} %bitcast.21, bf16[40,16,128]{2,1,0:T(8,128)(2,1)S(1)} %bitcast.22, bf16[256,1024]{1,0:T(8,128)(2,1)S(1)} %get-tuple-element.32.hi0_ref, bf16[256,1024]{1,0:T(8,128)(2,1)S(1)} %get-tuple-element.33.lo0_ref, ...), custom_call_target="tpu_custom_call" | custom-call | tf_op jit(solution)/shard_map/traces/pallas_call | solution.py:394
  (7 shorter events, 0.1 us)
Async XLA Ops:
  3.4 7.4 %copy-start.1 = (s32[256]{0:T(256)S(1)}, s32[256]{0:T(256)}, u32[]{:S(2)}) copy-start(s32[256]{0:T(256)} %param.5) | copy-start | bytes 3076
  3.4 7.5 %copy-start = (f32[2,64,1024]{2,1,0:T(8,128)S(1)}, f32[2,64,1024]{2,1,0:T(8,128)}, u32[]{:S(2)}) copy-start(f32[2,64,1024]{2,1,0:T(8,128)} %param.3) | copy-start | bytes 1572868
  5.4 9.5 %collective-permute-start = (bf16[2048,256]{1,0:T(8,128)(2,1)}, bf16[2048,256]{1,0:T(8,128)(2,1)S(1)}, u32[]{:S(2)}, u32[]{:S(2)}) collective-permute-start(bf16[2048,256]{1,0:T(8,128)(2,1)} %get-tuple-element.21), channel_id=1, source_target_pairs={{0,0},{1,4},{2,1},{3,5},{4,2},{5,6},{6,3},{7,7},{8,8},{9,12},{10,9... | collective-permute-start | bytes 3145736 | tf_op jit(solution)/shard_map/ppermute | solution.py:320
  7.3 28.2 %collective-permute-start.1 = (bf16[2048,256]{1,0:T(8,128)(2,1)}, bf16[2048,256]{1,0:T(8,128)(2,1)S(1)}, u32[]{:S(2)}, u32[]{:S(2)}) collective-permute-start(bf16[2048,256]{1,0:T(8,128)(2,1)} %get-tuple-element.22), channel_id=1, source_target_pairs={{0,1},{1,5},{2,0},{3,4},{4,3},{5,7},{6,2},{7,6},{8,9},{9,13},{10,8... | collective-permute-start | bytes 3145736 | tf_op jit(solution)/shard_map/ppermute | solution.py:320
  36.6 42.1 %collective-permute-start.2 = (bf16[1024,256]{1,0:T(8,128)(2,1)}, bf16[1024,256]{1,0:T(8,128)(2,1)S(1)}, u32[]{:S(2)}, u32[]{:S(2)}) collective-permute-start(bf16[1024,256]{1,0:T(8,128)(2,1)} %get-tuple-element.39), channel_id=1, source_target_pairs={{0,4},{4,0},{1,5},{5,1},{2,6},{6,2},{3,7},{7,3},{8,12},{12,8},{9,1... | collective-permute-start | bytes 1572872 | tf_op jit(solution)/shard_map/ppermute | solution.py:347
  41.1 37.6 %collective-permute-start.3 = (bf16[1024,256]{1,0:T(8,128)(2,1)}, bf16[1024,256]{1,0:T(8,128)(2,1)S(1)}, u32[]{:S(2)}, u32[]{:S(2)}) collective-permute-start(bf16[1024,256]{1,0:T(8,128)(2,1)} %get-tuple-element.38), channel_id=1, source_target_pairs={{0,4},{4,0},{1,5},{5,1},{2,6},{6,2},{3,7},{7,3},{8,12},{12,8},{9,1... | collective-permute-start | bytes 1572872 | tf_op jit(solution)/shard_map/ppermute | solution.py:347
  43.0 29.7 %all-to-all-start = ((bf16[16,32,128]{2,1,0:T(8,128)(2,1)}), bf16[16,32,128]{2,1,0:T(8,128)(2,1)S(1)}, u32[]{:S(2)}, u32[]{:S(2)}) async-start(bf16[16,32,128]{2,1,0:T(8,128)(2,1)} %bitcast.3), calls=%async_computation | async-start | bytes 262144 | tf_op jit(solution)/shard_map/all_to_all | solution.py:349
  59.3 19.4 %collective-permute-start.4 = (bf16[1024,256]{1,0:T(8,128)(2,1)}, bf16[1024,256]{1,0:T(8,128)(2,1)}, u32[]{:S(2)}, u32[]{:S(2)}) collective-permute-start(bf16[1024,256]{1,0:T(8,128)(2,1)} %get-tuple-element.37), channel_id=1, source_target_pairs={{0,4},{4,0},{1,5},{5,1},{2,6},{6,2},{3,7},{7,3},{8,12},{12,8},{9,1... | collective-permute-start | bytes 1572872 | tf_op jit(solution)/shard_map/ppermute | solution.py:347
  61.2 17.5 %collective-permute-start.5 = (bf16[1024,256]{1,0:T(8,128)(2,1)}, bf16[1024,256]{1,0:T(8,128)(2,1)}, u32[]{:S(2)}, u32[]{:S(2)}) collective-permute-start(bf16[1024,256]{1,0:T(8,128)(2,1)} %get-tuple-element.36), channel_id=1, source_target_pairs={{0,4},{4,0},{1,5},{5,1},{2,6},{6,2},{3,7},{7,3},{8,12},{12,8},{9,1... | collective-permute-start | bytes 1572872 | tf_op jit(solution)/shard_map/ppermute | solution.py:347
  73.5 13.1 %all-to-all-start.1 = ((bf16[32,16,128]{2,1,0:T(8,128)(2,1)}), bf16[32,16,128]{2,1,0:T(8,128)(2,1)S(1)}, u32[]{:S(2)}, u32[]{:S(2)}) async-start(bf16[32,16,128]{2,1,0:T(8,128)(2,1)} %bitcast.20), calls=%async_computation.1 | async-start | bytes 262144 | tf_op jit(solution)/shard_map/all_to_all | solution.py:350
  111.3 13.0 %all-to-all-start.2 = ((bf16[32,32,128]{2,1,0:T(8,128)(2,1)}), bf16[32,32,128]{2,1,0:T(8,128)(2,1)S(1)}, u32[]{:S(2)}, u32[]{:S(2)}) async-start(bf16[32,32,128]{2,1,0:T(8,128)(2,1)} %get-tuple-element.26), calls=%async_computation.2 | async-start | bytes 524288 | tf_op jit(solution)/shard_map/all_to_all | solution.py:371
  124.3 19.8 %all-to-all-start.5 = ((bf16[16,40,128]{2,1,0:T(8,128)(2,1)}), bf16[16,40,128]{2,1,0:T(8,128)(2,1)S(1)}, u32[]{:S(2)}, u32[]{:S(2)}) async-start(bf16[16,40,128]{2,1,0:T(8,128)(2,1)} %copy.9), calls=%async_computation.5 | async-start | bytes 327680 | tf_op jit(solution)/shard_map/all_to_all | solution.py:393
  144.2 23.0 %all-to-all-start.3 = ((bf16[16,64,128]{2,1,0:T(8,128)(2,1)}), bf16[16,64,128]{2,1,0:T(8,128)(2,1)S(1)}, u32[]{:S(2)}, u32[]{:S(2)}) async-start(bf16[16,64,128]{2,1,0:T(8,128)(2,1)} %bitcast.7), calls=%async_computation.3 | async-start | bytes 524288 | tf_op jit(solution)/shard_map/all_to_all | solution.py:392

commit v5 on v3

--- a/solution.py
+++ b/solution.py
@@ -97,15 +97,8 @@
     return jnp.where(x > 1e-30, 1.0 / jnp.maximum(x, 1e-30), 0.0)
 
 
-def krylov_kernel(idx_ref, norm_ref, u_ref, *refs):
-    k_refs, g_ref = refs[:4], refs[4]
-    u_rows, q_rows = refs[5:]
+def gather_kernel(u_ref, out_ref, u_rows):
     deep = u_ref.shape[1]
-    share = k_refs[0].shape[1]
-    y, core = idx_ref[0], idx_ref[1]
-    near = lax.rem(y, 2) * 2
-    quarters = [(near if j % 2 == 0 else 2 - near) + (core if j < 2 else 1 - core) for j in range(4)]
-
     for x in range(X):
         for c in range(2):
             fields = [u_ref[x * GROUP + c * Y + ys].astype(jnp.float32) for ys in range(Y)]
@@ -113,7 +106,19 @@
                 both = jnp.concatenate([block[:, g * HV : (g + 1) * HV] for block in fields], axis=1)
                 u_rows[pl.ds(x * 8 + c * 4 + g, deep, stride=8 * X), :] = both
     turned = u_rows[...].T
-    u = jnp.concatenate([turned[ys * HV : (ys + 1) * HV] for ys in range(Y)], axis=1)
+    out_ref[...] = jnp.concatenate([turned[ys * HV : (ys + 1) * HV] for ys in range(Y)], axis=1)
+
+
+def krylov_kernel(idx_ref, norm_ref, u_ref, *refs):
+    k_refs, g_ref = refs[:4], refs[4]
+    (q_rows,) = refs[5:]
+    deep = (g_ref.shape[1] - EXTRA) // 3
+    share = k_refs[0].shape[1]
+    y, core = idx_ref[0], idx_ref[1]
+    near = lax.rem(y, 2) * 2
+    quarters = [(near if j % 2 == 0 else 2 - near) + (core if j < 2 else 1 - core) for j in range(4)]
+
+    u = u_ref[...]
 
     def adjoint(p):
         both = jnp.concatenate([p, quarter_turn(p)], axis=0).astype(jnp.bfloat16)
@@ -311,14 +316,20 @@
         name="dft",
     )(freqs, recorded.reshape(share * virtual, samples))
 
-    spec, freqs = lax.optimization_barrier((spec, freqs))
-    hi0, lo0 = table(0, freqs)
     spec = spec.reshape(deep, X * GROUP, 128)
     spec = lax.all_to_all(spec, "z", split_axis=0, concat_axis=0, tiled=True)
-    spec, freqs, *blocks = lax.optimization_barrier((spec, freqs, *blocks))
-    hi1, lo1 = table(1, freqs)
+    spec, *blocks = lax.optimization_barrier((spec, *blocks))
     blocks = blocks + [lax.ppermute(b, "core", [(0, 1), (1, 0)]) for b in blocks]
     spec = lax.all_to_all(spec.transpose(1, 0, 2), SLAB, split_axis=0, concat_axis=0, tiled=True)
+
+    spec = pl.pallas_call(
+        gather_kernel,
+        out_shape=jax.ShapeDtypeStruct((HV, 2 * sources), jnp.float32),
+        scratch_shapes=[pltpu.VMEM((8 * X * deep, 128), jnp.float32)],
+        compiler_params=limit,
+        cost_estimate=pl.CostEstimate(flops=10**11, bytes_accessed=10**6, transcendentals=0),
+        name="gather",
+    )(spec)
 
     lines = 3 * deep + EXTRA
     vectors = pl.pallas_call(
@@ -326,13 +337,12 @@
         out_shape=jax.ShapeDtypeStruct((X * GROUP, lines, 128), jnp.bfloat16),
         in_specs=[smem] + [vmem] * 6,
         out_specs=vmem,
-        scratch_shapes=[
-            pltpu.VMEM((8 * X * deep, 128), jnp.float32),
-            pltpu.VMEM((4 * local, 128), jnp.float32),
-        ],
+        scratch_shapes=[pltpu.VMEM((4 * local, 128), jnp.float32)],
         compiler_params=limit,
         name="krylov",
     )(position, rec_norm, spec, *blocks)
+    vectors, freqs = lax.optimization_barrier((vectors, freqs))
+    (hi0, lo0), (hi1, lo1) = table(0, freqs), table(1, freqs)
     back = lax.all_to_all(vectors, SLAB, split_axis=0, concat_axis=0, tiled=True)
     data = back[:, : 3 * deep].reshape(X * GROUP, 3, deep, 128).transpose(2, 0, 1, 3)
     data = data.reshape(deep, 3 * X * GROUP, 128)

time: 124 us -> 123 us (level)
  blocking collectives: 57.7 us -> 45.4 us
  starting transfers between devices: 18 us -> 26 us
  waiting for transfers between devices: 22.4 us -> 24.6 us
    all_to_all x1 -> x0, blocking collectives: 14.5 us -> none  [body(): lax.all_to_all(spec.transpose(1, 0, 2), SLAB, split_axis=0, concat_axis=0...]
    all_to_all x0 -> x1, starting transfers between devices: none -> 9.8 us  [body(): lax.all_to_all(spec.transpose(1, 0, 2), SLAB, split_axis=0, concat_axis=0...]
    all_to_all x0 -> x1, waiting for transfers between devices: none -> 2.27 us  [body(): lax.all_to_all(spec.transpose(1, 0, 2), SLAB, split_axis=0, concat_axis=0...]
    all_to_all x1, blocking collectives: 15.2 us -> 17.3 us  [body(): lax.all_to_all(vectors, SLAB, split_axis=0, concat_axis=0, tiled=True)]
    ppermute x2, starting transfers between devices: 6.06 us -> 4.33 us  [body(): lax.ppermute(b, 'core', [(0, 1), (1, 0)])]
  transfers between devices with their start and end apart: 5 -> 6, of which waited for: 1 -> 2; matrix products, arithmetic and copies ran while one was open for 0% -> 0% of each run, Pallas kernels for 6% -> 6%
where the time goes in v5:
time: 123 us
  blocking collectives  45.4 us (37%)
  starting transfers between devices  26 us (21%)
  waiting for transfers between devices  24.6 us (20%)
  Pallas kernels  21.4 us (17%)
  local copies, waits for them, and re-layouts  4.55 us (4%)
    all_to_all x1, blocking collectives, body(): spec = lax.all_to_all(spec, 'z', split_axis=0, concat_axis=0, tiled=True)  28.1 us
    all_to_all x1, waiting for transfers between devices, body(): lax.all_to_all(send, 'z', split_axis=0, concat_axis=0, tiled=True)  22.3 us
    all_to_all x1, blocking collectives, body(): lax.all_to_all(vectors, SLAB, split_axis=0, concat_axis=0, tiled=True)  17.3 us
    all_to_all x1, starting transfers between devices, body(): lax.all_to_all(spec.transpose(1, 0, 2), SLAB, split_axis=0, concat_axis=0...  9.8 us
    pallas_call x1, Pallas kernels, body(): pl.pallas_call(krylov_kernel, out_shape=jax.ShapeDtypeStruct((X * GROUP,...  8.79 us
    all_to_all x1, starting transfers between devices, body(): lax.all_to_all(send, 'z', split_axis=0, concat_axis=0, tiled=True)  6.49 us
    ppermute x2, starting transfers between devices, body(): lax.ppermute(load, COLUMN, route(n))  5.41 us
    ppermute x2, starting transfers between devices, body(): lax.ppermute(b, 'core', [(0, 1), (1, 0)])  4.33 us
  transfers between devices with their start and end apart: 6, of which 2 were waited for; matrix products, arithmetic and copies ran while one was open for 0% of the time, Pallas kernels for 6%

profile of v5, /device:TPU:2, one launch (start us, length us, event | category | flops | bytes accessed | tf_op | source)
XLA Modules:
  0.0 122.9 jit_solution(3729310616603159846)
XLA Ops:
  0.6 2.7 %reshape.27.k_ref = bf16[2,2048,256]{2,1,0:T(8,128)(2,1)S(1)} reshape(bf16[2,1024,2,256]{3,2,1,0:T(2,128)(2,1)} %param.4) | data formatting | bytes 4194304 | tf_op jit(solution)/shard_map/reshape | solution.py:296
  3.4 0.0 copy-start.1
  3.4 0.0 copy-start
  3.4 0.1 pad_add_fusion.idx_ref
  3.5 1.9 %pick.1 = (bf16[2048,256]{1,0:T(8,128)(2,1)}, bf16[2048,256]{1,0:T(8,128)(2,1)}) custom-call(s32[2]{0:T(128)S(1)} %pad_add_fusion.idx_ref, bf16[2,2048,256]{2,1,0:T(8,128)(2,1)S(1)} %reshape.27.k_ref), custom_call_target="tpu_custom_call" | custom-call | tf_op jit(solution)/shard_map/pick/pallas_call | solution.py:288
  5.4 1.9 %collective-permute-start = (bf16[2048,256]{1,0:T(8,128)(2,1)}, bf16[2048,256]{1,0:T(8,128)(2,1)S(1)}, u32[]{:S(2)}, u32[]{:S(2)}) collective-permute-start(bf16[2048,256]{1,0:T(8,128)(2,1)} %get-tuple-element.17), channel_id=1, source_target_pairs={{0,0},{1,4},{2,1},{3,5},{4,2},{5,6},{6,3},{7,7},{8,8},{9,12},{10,9... | collective-permute-start | bytes 3145736 | tf_op jit(solution)/shard_map/ppermute | solution.py:297
  7.3 3.5 %collective-permute-start.1 = (bf16[2048,256]{1,0:T(8,128)(2,1)}, bf16[2048,256]{1,0:T(8,128)(2,1)S(1)}, u32[]{:S(2)}, u32[]{:S(2)}) collective-permute-start(bf16[2048,256]{1,0:T(8,128)(2,1)} %get-tuple-element.18), channel_id=1, source_target_pairs={{0,1},{1,5},{2,0},{3,4},{4,3},{5,7},{6,2},{7,6},{8,9},{9,13},{10,8... | collective-permute-start | bytes 3145736 | tf_op jit(solution)/shard_map/ppermute | solution.py:297
  10.8 0.0 copy-done.1
  10.8 0.1 reshape.24.fr_ref
  10.9 0.0 copy-done
  10.9 3.6 %dft.1 = (bf16[512,128]{1,0:T(8,128)(2,1)S(1)}, f32[1,1]{1,0:T(1,128)}) custom-call(s32[16,16]{1,0:T(8,128)S(1)} %reshape.24.fr_ref, f32[128,1024]{1,0:T(8,128)S(1)} %bitcast.18), custom_call_target="tpu_custom_call" | custom-call | tf_op jit(solution)/shard_map/dft/pallas_call | solution.py:305
  14.5 28.1 %all_to_all.20 = bf16[16,32,128]{2,1,0:T(8,128)(2,1)S(1)} all-to-all(bf16[16,32,128]{2,1,0:T(8,128)(2,1)S(1)} %bitcast.19), channel_id=1, replica_groups=mesh['z'=16,'x'=4,'core'=2,'rcv'=4] {'z'}, dimensions={0} | all-to-all | bytes 262144 | tf_op jit(solution)/shard_map/all_to_all | solution.py:320
  42.7 0.0 collective-permute-done.refs_0_
  42.7 0.0 collective-permute-done.1.refs_1_
  42.7 0.7 copy.17
  43.4 9.8 %all-to-all-start.1 = ((bf16[32,16,128]{2,1,0:T(8,128)(2,1)}), bf16[32,16,128]{2,1,0:T(8,128)(2,1)S(1)}, u32[]{:S(2)}, u32[]{:S(2)}) async-start(bf16[32,16,128]{2,1,0:T(8,128)(2,1)} %bitcast.16), calls=%async_computation.1 | async-start | bytes 262144 | tf_op jit(solution)/shard_map/all_to_all | solution.py:323
  53.2 2.1 %collective-permute-start.2 = (bf16[2048,256]{1,0:T(8,128)(2,1)S(1)}, bf16[2048,256]{1,0:T(8,128)(2,1)S(1)}, u32[]{:S(2)}, u32[]{:S(2)}) collective-permute-start(bf16[2048,256]{1,0:T(8,128)(2,1)S(1)} %collective-permute-done.refs_0_), channel_id=1, source_target_pairs={{0,4},{4,0},{1,5},{5,1},{2,6},{6,2},{3,7},{7,3},{8,12},{12,8},{9,1... | collective-permute-start | bytes 3145736 | tf_op jit(solution)/shard_map/ppermute | solution.py:322
  55.2 2.3 %collective-permute-start.3 = (bf16[2048,256]{1,0:T(8,128)(2,1)S(1)}, bf16[2048,256]{1,0:T(8,128)(2,1)}, u32[]{:S(2)}, u32[]{:S(2)}) collective-permute-start(bf16[2048,256]{1,0:T(8,128)(2,1)S(1)} %collective-permute-done.1.refs_1_), channel_id=1, source_target_pairs={{0,4},{4,0},{1,5},{5,1},{2,6},{6,2},{3,7},{7,3},{8,12},{12,8},{9,1... | collective-permute-start | bytes 3145736 | tf_op jit(solution)/shard_map/ppermute | solution.py:322
  57.5 2.3 %all-to-all-done.1.u_ref = bf16[32,16,128]{2,1,0:T(8,128)(2,1)S(1)} async-done(((bf16[32,16,128]{2,1,0:T(8,128)(2,1)}), bf16[32,16,128]{2,1,0:T(8,128)(2,1)S(1)}, u32[]{:S(2)}, u32[]{:S(2)}) %all-to-all-start.1) | async-done | bytes 131104 | tf_op jit(solution)/shard_map/all_to_all | solution.py:323
  59.8 0.4 gather.1.u_ref
  60.2 0.0 collective-permute-done.2.refs_2_
  60.2 0.0 collective-permute-done.3.refs_3_
  60.2 8.8 %krylov.1 = bf16[32,64,128]{2,1,0:T(8,128)(2,1)S(1)} custom-call(s32[2]{0:T(128)S(1)} %pad_add_fusion.idx_ref, f32[1,1]{1,0:T(1,128)} %get-tuple-element.15.norm_ref, f32[32,2048]{1,0:T(8,128)S(1)} %gather.1.u_ref, bf16[2048,256]{1,0:T(8,128)(2,1)S(1)} %collective-permute-done.refs_0_, bf16[2048,256]{1,0:T(8,128)(2,1)S(1)} %collective-permute-done.1.refs_1_, ...), custom_call_target="tpu_custom_call" | custom-call | tf_op jit(solution)/shard_map/krylov/pallas_call | solution.py:335
  69.0 17.3 %all_to_all.21 = bf16[32,64,128]{2,1,0:T(8,128)(2,1)S(1)} all-to-all(bf16[32,64,128]{2,1,0:T(8,128)(2,1)S(1)} %krylov.1), channel_id=1, replica_groups=mesh['z'=16,'x'=4,'core'=2,'rcv'=4] {'x','core','rcv'}, dimensions={0} | all-to-all | bytes 1048576 | tf_op jit(solution)/shard_map/all_to_all | solution.py:346
  86.4 0.9 copy.10
  87.3 6.5 %all-to-all-start.3 = ((bf16[16,104,128]{2,1,0:T(8,128)(2,1)}), bf16[16,104,128]{2,1,0:T(8,128)(2,1)S(1)}, u32[]{:S(2)}, u32[]{:S(2)}) async-start(bf16[16,104,128]{2,1,0:T(8,128)(2,1)} %copy.10), calls=%async_computation.3 | async-start | bytes 851968 | tf_op jit(solution)/shard_map/all_to_all | solution.py:353
  93.8 1.6 %table1.1 = (bf16[256,1024]{1,0:T(8,128)(2,1)S(1)}, bf16[256,1024]{1,0:T(8,128)(2,1)S(1)}) custom-call(s32[16,16]{1,0:T(8,128)S(1)} %reshape.24.fr_ref), custom_call_target="tpu_custom_call" | custom-call | tf_op jit(solution)/shard_map/table1/pallas_call | solution.py:300
  95.4 1.6 %table0.1 = (bf16[256,1024]{1,0:T(8,128)(2,1)S(1)}, bf16[256,1024]{1,0:T(8,128)(2,1)S(1)}) custom-call(s32[16,16]{1,0:T(8,128)S(1)} %reshape.24.fr_ref), custom_call_target="tpu_custom_call" | custom-call | tf_op jit(solution)/shard_map/table0/pallas_call | solution.py:300
  97.1 22.3 %all-to-all-done.3 = bf16[16,104,128]{2,1,0:T(8,128)(2,1)S(1)} async-done(((bf16[16,104,128]{2,1,0:T(8,128)(2,1)}), bf16[16,104,128]{2,1,0:T(8,128)(2,1)S(1)}, u32[]{:S(2)}, u32[]{:S(2)}) %all-to-all-start.3) | async-done | bytes 426016 | tf_op jit(solution)/shard_map/all_to_all | solution.py:353
  119.4 0.1 copy.16
  119.5 3.5 %traces.1 = (f32[2,64,1024]{2,1,0:T(8,128)}, f32[2,64,1024]{2,1,0:T(8,128)}) custom-call(bf16[104,16,128]{2,1,0:T(8,128)(2,1)S(1)} %bitcast.17, bf16[256,1024]{1,0:T(8,128)(2,1)S(1)} %get-tuple-element.24.hi0_ref, bf16[256,1024]{1,0:T(8,128)(2,1)S(1)} %get-tuple-element.25.lo0_ref, bf16[256,1024]{1,0:T(8,128)(2,1)S(1)} %get-tuple-element.26.hi1_ref, ...), custom_call_target="tpu_custom_call" | custom-call | tf_op jit(solution)/shard_map/traces/pallas_call | solution.py:355
  (6 shorter events, 0.1 us)
Async XLA Ops:
  3.4 7.4 %copy-start.1 = (s32[256]{0:T(256)S(1)}, s32[256]{0:T(256)}, u32[]{:S(2)}) copy-start(s32[256]{0:T(256)} %param.5) | copy-start | bytes 3076
  3.4 7.5 %copy-start = (f32[2,64,1024]{2,1,0:T(8,128)S(1)}, f32[2,64,1024]{2,1,0:T(8,128)}, u32[]{:S(2)}) copy-start(f32[2,64,1024]{2,1,0:T(8,128)} %param.3) | copy-start | bytes 1572868
  5.4 37.3 %collective-permute-start = (bf16[2048,256]{1,0:T(8,128)(2,1)}, bf16[2048,256]{1,0:T(8,128)(2,1)S(1)}, u32[]{:S(2)}, u32[]{:S(2)}) collective-permute-start(bf16[2048,256]{1,0:T(8,128)(2,1)} %get-tuple-element.17), channel_id=1, source_target_pairs={{0,0},{1,4},{2,1},{3,5},{4,2},{5,6},{6,3},{7,7},{8,8},{9,12},{10,9... | collective-permute-start | bytes 3145736 | tf_op jit(solution)/shard_map/ppermute | solution.py:297
  7.3 35.4 %collective-permute-start.1 = (bf16[2048,256]{1,0:T(8,128)(2,1)}, bf16[2048,256]{1,0:T(8,128)(2,1)S(1)}, u32[]{:S(2)}, u32[]{:S(2)}) collective-permute-start(bf16[2048,256]{1,0:T(8,128)(2,1)} %get-tuple-element.18), channel_id=1, source_target_pairs={{0,1},{1,5},{2,0},{3,4},{4,3},{5,7},{6,2},{7,6},{8,9},{9,13},{10,8... | collective-permute-start | bytes 3145736 | tf_op jit(solution)/shard_map/ppermute | solution.py:297
  43.4 16.4 %all-to-all-start.1 = ((bf16[32,16,128]{2,1,0:T(8,128)(2,1)}), bf16[32,16,128]{2,1,0:T(8,128)(2,1)S(1)}, u32[]{:S(2)}, u32[]{:S(2)}) async-start(bf16[32,16,128]{2,1,0:T(8,128)(2,1)} %bitcast.16), calls=%async_computation.1 | async-start | bytes 262144 | tf_op jit(solution)/shard_map/all_to_all | solution.py:323
  53.2 7.0 %collective-permute-start.2 = (bf16[2048,256]{1,0:T(8,128)(2,1)S(1)}, bf16[2048,256]{1,0:T(8,128)(2,1)S(1)}, u32[]{:S(2)}, u32[]{:S(2)}) collective-permute-start(bf16[2048,256]{1,0:T(8,128)(2,1)S(1)} %collective-permute-done.refs_0_), channel_id=1, source_target_pairs={{0,4},{4,0},{1,5},{5,1},{2,6},{6,2},{3,7},{7,3},{8,12},{12,8},{9,1... | collective-permute-start | bytes 3145736 | tf_op jit(solution)/shard_map/ppermute | solution.py:322
  55.2 4.9 %collective-permute-start.3 = (bf16[2048,256]{1,0:T(8,128)(2,1)S(1)}, bf16[2048,256]{1,0:T(8,128)(2,1)}, u32[]{:S(2)}, u32[]{:S(2)}) collective-permute-start(bf16[2048,256]{1,0:T(8,128)(2,1)S(1)} %collective-permute-done.1.refs_1_), channel_id=1, source_target_pairs={{0,4},{4,0},{1,5},{5,1},{2,6},{6,2},{3,7},{7,3},{8,12},{12,8},{9,1... | collective-permute-start | bytes 3145736 | tf_op jit(solution)/shard_map/ppermute | solution.py:322
  87.3 32.1 %all-to-all-start.3 = ((bf16[16,104,128]{2,1,0:T(8,128)(2,1)}), bf16[16,104,128]{2,1,0:T(8,128)(2,1)S(1)}, u32[]{:S(2)}, u32[]{:S(2)}) async-start(bf16[16,104,128]{2,1,0:T(8,128)(2,1)} %copy.10), calls=%async_computation.3 | async-start | bytes 851968 | tf_op jit(solution)/shard_map/all_to_all | solution.py:353

commit v6 on v5

--- a/solution.py
+++ b/solution.py
@@ -97,8 +97,13 @@
     return jnp.where(x > 1e-30, 1.0 / jnp.maximum(x, 1e-30), 0.0)
 
 
-def gather_kernel(u_ref, out_ref, u_rows):
+def both_turns(p):
+    return jnp.concatenate([p, quarter_turn(p)], axis=0).astype(jnp.bfloat16)
+
+
+def gather_kernel(u_ref, first_ref, second_ref, out_ref, part_ref, u_rows):
     deep = u_ref.shape[1]
+    share = first_ref.shape[1]
     for x in range(X):
         for c in range(2):
             fields = [u_ref[x * GROUP + c * Y + ys].astype(jnp.float32) for ys in range(Y)]
@@ -106,24 +111,26 @@
                 both = jnp.concatenate([block[:, g * HV : (g + 1) * HV] for block in fields], axis=1)
                 u_rows[pl.ds(x * 8 + c * 4 + g, deep, stride=8 * X), :] = both
     turned = u_rows[...].T
-    out_ref[...] = jnp.concatenate([turned[ys * HV : (ys + 1) * HV] for ys in range(Y)], axis=1)
-
-
-def krylov_kernel(idx_ref, norm_ref, u_ref, *refs):
-    k_refs, g_ref = refs[:4], refs[4]
-    (q_rows,) = refs[5:]
-    deep = (g_ref.shape[1] - EXTRA) // 3
+    u = jnp.concatenate([turned[ys * HV : (ys + 1) * HV] for ys in range(Y)], axis=1)
+    out_ref[...] = u
+    both = both_turns(u)
+    part_ref[:, :share] = jnp.dot(both, first_ref[...], preferred_element_type=jnp.float32)
+    part_ref[:, share:] = jnp.dot(both, second_ref[...], preferred_element_type=jnp.float32)
+
+
+def krylov_kernel(idx_ref, norm_ref, u_ref, part_ref, *refs):
+    k_refs, g_ref, q_rows = refs[:4], refs[4], refs[5]
     share = k_refs[0].shape[1]
+    columns = share // 4
     y, core = idx_ref[0], idx_ref[1]
     near = lax.rem(y, 2) * 2
     quarters = [(near if j % 2 == 0 else 2 - near) + (core if j < 2 else 1 - core) for j in range(4)]
 
-    u = u_ref[...]
+    def products(both, some):
+        return [jnp.dot(both, k_ref[...], preferred_element_type=jnp.float32) for k_ref in some]
 
     def adjoint(p):
-        both = jnp.concatenate([p, quarter_turn(p)], axis=0).astype(jnp.bfloat16)
-        parts = [jnp.dot(both, k_ref[...], preferred_element_type=jnp.float32) for k_ref in k_refs]
-        return 0.5 * jnp.concatenate(parts, axis=1)
+        return 0.5 * jnp.concatenate(products(both_turns(p), k_refs), axis=1)
 
     def forward(q):
         q = q.astype(jnp.bfloat16)
@@ -138,9 +145,23 @@
         )
         return 0.5 * (w[:HV] - quarter_turn(w[HV:]))
 
+    def write(first, second, start, count):
+        q_rows[...] = jnp.concatenate([first, second], axis=0).T
+        for c in range(2):
+            for j in range(4):
+                base = j * share + 2 * c
+                even = q_rows[pl.ds(base, columns, stride=4), :]
+                odd = q_rows[pl.ds(base + 1, columns, stride=4), :]
+                for n in range(count):
+                    lanes = slice(n * 64, (n + 1) * 64)
+                    both = jnp.concatenate([even[:, lanes], odd[:, lanes]], axis=1)
+                    row = (start + n) * columns
+                    g_ref[c * Y + quarters[j], row : row + columns, :] = both.astype(jnp.bfloat16)
+
+    u = u_ref[...]
     length = length_of(u)
     scale = inverse_of(length)
-    g1 = adjoint(u) * scale
+    g1 = jnp.concatenate([part_ref[...]] + products(both_turns(u), k_refs[2:]), axis=1) * (0.5 * scale)
     a1 = length_of(g1)
     q1 = g1 * inverse_of(a1)
     h2 = forward(q1) - (a1 * scale) * u
@@ -149,12 +170,14 @@
     g2 = adjoint(p2) - b2 * q1
     a2 = length_of(g2)
     q2 = g2 * inverse_of(a2)
+    write(q1, q2, 0, 2)
     h3 = forward(q2) - a2 * p2
     b3 = length_of(h3)
     p3 = h3 * inverse_of(b3)
     g3 = adjoint(p3) - b3 * q2
     a3 = length_of(g3)
     q3 = g3 * inverse_of(a3)
+    write(q3, q3, 2, 1)
 
     lane = lax.broadcasted_iota(jnp.int32, (EXTRA, 128), 1)
     slot = lax.rem(lane, 64) // GROUP
@@ -164,23 +187,8 @@
     hi = values.astype(jnp.bfloat16).astype(jnp.float32)
     scalars = jnp.where(lane < 64, hi, values - hi)
     scalars = jnp.where(lax.rem(lane, GROUP) == core * Y + y, scalars, 0.0).astype(jnp.bfloat16)
-
-    for pair in range(2):
-        first, second = ((q1, q2), (q3, q3))[pair]
-        q_rows[...] = jnp.concatenate([first, second], axis=0).T
-        for x in range(X):
-            for c in range(2):
-                for j in range(4):
-                    base = j * share + x * 4 + c * 2
-                    even = q_rows[pl.ds(base, deep, stride=4 * X), :]
-                    odd = q_rows[pl.ds(base + 1, deep, stride=4 * X), :]
-                    for inner in range(2 - pair):
-                        lanes = slice(inner * 64, (inner + 1) * 64)
-                        both = jnp.concatenate([even[:, lanes], odd[:, lanes]], axis=1)
-                        row = (2 * pair + inner) * deep
-                        g_ref[x * GROUP + c * Y + quarters[j], row : row + deep, :] = both.astype(jnp.bfloat16)
-    for e in range(X * GROUP):
-        g_ref[e, 3 * deep : 3 * deep + EXTRA, :] = scalars
+    for e in range(GROUP):
+        g_ref[e, 3 * columns : 3 * columns + EXTRA, :] = scalars
 
 
 def reduced_lsqr(s, a1, b2, a2, b3, a3, rec):
@@ -223,13 +231,10 @@
 
 
 def traces_kernel(m_ref, hi0_ref, lo0_ref, hi1_ref, lo1_ref, sol_ref, res_ref):
-    scal = [m_ref[3 * X * GROUP + x].astype(jnp.float32) for x in range(X)]
-    parts = []
-    for n in range(7):
-        top, low = n * GROUP, 64 + n * GROUP
-        parts.append(
-            jnp.concatenate([sc[:, top : top + GROUP] + sc[:, low : low + GROUP] for sc in scal], axis=1)
-        )
+    scal = m_ref[3 * GROUP].astype(jnp.float32)
+    parts = [
+        scal[:, n * GROUP : (n + 1) * GROUP] + scal[:, 64 + n * GROUP : 64 + (n + 1) * GROUP] for n in range(7)
+    ]
     sol_c, res_c = reduced_lsqr(*parts)
     root = math.sqrt(2.0)
     sol_c, res_c = [root * w for w in sol_c], [root * w for w in res_c]
@@ -237,12 +242,11 @@
     for weights in (sol_c, res_c):
         for c in range(2):
             blocks = []
-            for x in range(X):
-                for phi in range(Y):
-                    e = x * GROUP + c * Y + phi
-                    blocks.append(
-                        sum(w[:, e : e + 1] * m_ref[3 * e + n].astype(jnp.float32) for n, w in enumerate(weights))
-                    )
+            for phi in range(Y):
+                e = c * Y + phi
+                blocks.append(
+                    sum(w[:, e : e + 1] * m_ref[3 * e + n].astype(jnp.float32) for n, w in enumerate(weights))
+                )
             turned = jnp.concatenate(blocks, axis=0).T
             for rr in range(2):
                 lines.append(
@@ -322,35 +326,38 @@
     blocks = blocks + [lax.ppermute(b, "core", [(0, 1), (1, 0)]) for b in blocks]
     spec = lax.all_to_all(spec.transpose(1, 0, 2), SLAB, split_axis=0, concat_axis=0, tiled=True)
 
-    spec = pl.pallas_call(
+    field, part = pl.pallas_call(
         gather_kernel,
-        out_shape=jax.ShapeDtypeStruct((HV, 2 * sources), jnp.float32),
+        out_shape=(
+            jax.ShapeDtypeStruct((HV, 2 * sources), jnp.float32),
+            jax.ShapeDtypeStruct((2 * HV, 2 * local), jnp.float32),
+        ),
         scratch_shapes=[pltpu.VMEM((8 * X * deep, 128), jnp.float32)],
         compiler_params=limit,
         cost_estimate=pl.CostEstimate(flops=10**11, bytes_accessed=10**6, transcendentals=0),
         name="gather",
-    )(spec)
-
-    lines = 3 * deep + EXTRA
+    )(spec, *blocks[:2])
+
+    columns = X * deep
+    lines = 3 * columns + EXTRA
     vectors = pl.pallas_call(
         krylov_kernel,
-        out_shape=jax.ShapeDtypeStruct((X * GROUP, lines, 128), jnp.bfloat16),
-        in_specs=[smem] + [vmem] * 6,
+        out_shape=jax.ShapeDtypeStruct((GROUP, lines, 128), jnp.bfloat16),
+        in_specs=[smem] + [vmem] * 7,
         out_specs=vmem,
         scratch_shapes=[pltpu.VMEM((4 * local, 128), jnp.float32)],
         compiler_params=limit,
         name="krylov",
-    )(position, rec_norm, spec, *blocks)
-    vectors, freqs = lax.optimization_barrier((vectors, freqs))
+    )(position, rec_norm, field, part, *blocks)
+    vectors, freqs = lax.optimization_barrier((vectors, freq_index.reshape(columns, Y)))
     (hi0, lo0), (hi1, lo1) = table(0, freqs), table(1, freqs)
-    back = lax.all_to_all(vectors, SLAB, split_axis=0, concat_axis=0, tiled=True)
-    data = back[:, : 3 * deep].reshape(X * GROUP, 3, deep, 128).transpose(2, 0, 1, 3)
-    data = data.reshape(deep, 3 * X * GROUP, 128)
-    scal = back[:, 3 * deep].astype(jnp.float32).reshape(X, GROUP, 128)
-    scal = jnp.sum(scal, axis=1).astype(jnp.bfloat16)
-    scal = jnp.concatenate([scal, jnp.zeros_like(scal)], axis=0)
-    send = jnp.concatenate([data, jnp.broadcast_to(scal, (deep, 2 * X, 128))], axis=1)
-    got = lax.all_to_all(send, "z", split_axis=0, concat_axis=0, tiled=True).transpose(1, 0, 2)
+    back = lax.all_to_all(vectors, COLUMN, split_axis=0, concat_axis=0, tiled=True)
+    data = back[:, : 3 * columns].reshape(GROUP, 3, columns, 128).transpose(2, 0, 1, 3).reshape(columns, 24, 128)
+    scal = jnp.sum(back[:, 3 * columns].astype(jnp.float32), axis=0).astype(jnp.bfloat16)
+    scal = jnp.broadcast_to(scal, (columns, 2, 128))
+    send = jnp.concatenate([data, scal], axis=1).reshape(columns, 13, 2, 128)
+    got = lax.all_to_all(send, ("z", "x"), split_axis=0, concat_axis=0, tiled=True)
+    got = got.reshape(columns, 26, 128).transpose(1, 0, 2)
 
     return pl.pallas_call(
         traces_kernel,

time: 123 us -> 126 us (1.024)
  blocking collectives: 45.4 us -> 40.2 us
  starting transfers between devices: 26 us -> 29.5 us
  waiting for transfers between devices: 24.6 us -> 27.8 us
    all_to_all x1, blocking collectives: 17.3 us -> 12.1 us  [body(): lax.all_to_all(vectors, COLUMN, split_axis=0, concat_axis=0, tiled=True)]
    all_to_all x1, starting transfers between devices: 6.49 us -> 9.93 us  [body(): lax.all_to_all(send, ('z', 'x'), split_axis=0, concat_axis=0, tiled=True)]
    all_to_all x1, waiting for transfers between devices: 22.3 us -> 25.6 us  [body(): lax.all_to_all(send, ('z', 'x'), split_axis=0, concat_axis=0, tiled=True)]
    reshape x0 -> x2, local copies, waits for them, and re-layouts: none -> 1.3 us  [the longest x1 1.2 us: body(): send = jnp.concatenate([data, scal], axis=1).reshape(columns, 13, 2, 128)]
where the time goes in v6:
time: 126 us
  blocking collectives  40.2 us (32%)
  starting transfers between devices  29.5 us (23%)
  waiting for transfers between devices  27.8 us (22%)
  Pallas kernels  22.5 us (18%)
  local copies, waits for them, and re-layouts  4.97 us (4%)
    all_to_all x1, blocking collectives, body(): spec = lax.all_to_all(spec, 'z', split_axis=0, concat_axis=0, tiled=True)  28.1 us
    all_to_all x1, waiting for transfers between devices, body(): lax.all_to_all(send, ('z', 'x'), split_axis=0, concat_axis=0, tiled=True)  25.6 us
    all_to_all x1, blocking collectives, body(): lax.all_to_all(vectors, COLUMN, split_axis=0, concat_axis=0, tiled=True)  12.1 us
    all_to_all x1, starting transfers between devices, body(): lax.all_to_all(send, ('z', 'x'), split_axis=0, concat_axis=0, tiled=True)  9.93 us
    all_to_all x1, starting transfers between devices, body(): lax.all_to_all(spec.transpose(1, 0, 2), SLAB, split_axis=0, concat_axis=0...  9.8 us
    pallas_call x1, Pallas kernels, body(): pl.pallas_call(krylov_kernel, out_shape=jax.ShapeDtypeStruct((GROUP, line...  8.34 us
    ppermute x2, starting transfers between devices, body(): lax.ppermute(load, COLUMN, route(n))  5.41 us
    pallas_call x1, Pallas kernels, body(): pl.pallas_call(traces_kernel, out_shape=tuple((jax.ShapeDtypeStruct((shar...  4.54 us
  transfers between devices with their start and end apart: 6, of which 2 were waited for; matrix products, arithmetic and copies ran while one was open for 0% of the time, Pallas kernels for 6%

profile of v6, /device:TPU:2, one launch (start us, length us, event | category | flops | bytes accessed | tf_op | source)
XLA Modules:
  0.0 125.8 jit_solution(7236631584108822117)
XLA Ops:
  0.6 2.7 %reshape.34.k_ref = bf16[2,2048,256]{2,1,0:T(8,128)(2,1)S(1)} reshape(bf16[2,1024,2,256]{3,2,1,0:T(2,128)(2,1)} %param.4) | data formatting | bytes 4194304 | tf_op jit(solution)/shard_map/reshape | solution.py:300
  3.4 0.0 copy-start.1
  3.4 0.0 copy-start
  3.4 0.1 pad_add_fusion.idx_ref
  3.5 1.9 %pick.1 = (bf16[2048,256]{1,0:T(8,128)(2,1)}, bf16[2048,256]{1,0:T(8,128)(2,1)}) custom-call(s32[2]{0:T(128)S(1)} %pad_add_fusion.idx_ref, bf16[2,2048,256]{2,1,0:T(8,128)(2,1)S(1)} %reshape.34.k_ref), custom_call_target="tpu_custom_call" | custom-call | tf_op jit(solution)/shard_map/pick/pallas_call | solution.py:292
  5.4 1.9 %collective-permute-start = (bf16[2048,256]{1,0:T(8,128)(2,1)}, bf16[2048,256]{1,0:T(8,128)(2,1)S(1)}, u32[]{:S(2)}, u32[]{:S(2)}) collective-permute-start(bf16[2048,256]{1,0:T(8,128)(2,1)} %get-tuple-element.19), channel_id=1, source_target_pairs={{0,0},{1,4},{2,1},{3,5},{4,2},{5,6},{6,3},{7,7},{8,8},{9,12},{10,9... | collective-permute-start | bytes 3145736 | tf_op jit(solution)/shard_map/ppermute | solution.py:301
  7.3 3.5 %collective-permute-start.1 = (bf16[2048,256]{1,0:T(8,128)(2,1)}, bf16[2048,256]{1,0:T(8,128)(2,1)S(1)}, u32[]{:S(2)}, u32[]{:S(2)}) collective-permute-start(bf16[2048,256]{1,0:T(8,128)(2,1)} %get-tuple-element.20), channel_id=1, source_target_pairs={{0,1},{1,5},{2,0},{3,4},{4,3},{5,7},{6,2},{7,6},{8,9},{9,13},{10,8... | collective-permute-start | bytes 3145736 | tf_op jit(solution)/shard_map/ppermute | solution.py:301
  10.8 0.0 copy-done.1
  10.8 0.1 reshape.31.fr_ref
  10.9 0.0 copy-done
  10.9 3.6 %dft.1 = (bf16[512,128]{1,0:T(8,128)(2,1)S(1)}, f32[1,1]{1,0:T(1,128)}) custom-call(s32[16,16]{1,0:T(8,128)S(1)} %reshape.31.fr_ref, f32[128,1024]{1,0:T(8,128)S(1)} %bitcast.17), custom_call_target="tpu_custom_call" | custom-call | tf_op jit(solution)/shard_map/dft/pallas_call | solution.py:309
  14.5 28.1 %all_to_all.20 = bf16[16,32,128]{2,1,0:T(8,128)(2,1)S(1)} all-to-all(bf16[16,32,128]{2,1,0:T(8,128)(2,1)S(1)} %bitcast.18), channel_id=1, replica_groups=mesh['z'=16,'x'=4,'core'=2,'rcv'=4] {'z'}, dimensions={0} | all-to-all | bytes 262144 | tf_op jit(solution)/shard_map/all_to_all | solution.py:324
  42.6 0.0 collective-permute-done.first_ref.refs_0_
  42.6 0.0 collective-permute-done.1.second_ref.refs_1_
  42.7 0.7 copy.13
  43.4 9.8 %all-to-all-start.1 = ((bf16[32,16,128]{2,1,0:T(8,128)(2,1)}), bf16[32,16,128]{2,1,0:T(8,128)(2,1)S(1)}, u32[]{:S(2)}, u32[]{:S(2)}) async-start(bf16[32,16,128]{2,1,0:T(8,128)(2,1)} %bitcast.15), calls=%async_computation.1 | async-start | bytes 262144 | tf_op jit(solution)/shard_map/all_to_all | solution.py:327
  53.2 0.1 reshape.35.fr_ref
  53.3 2.1 %collective-permute-start.2 = (bf16[2048,256]{1,0:T(8,128)(2,1)S(1)}, bf16[2048,256]{1,0:T(8,128)(2,1)S(1)}, u32[]{:S(2)}, u32[]{:S(2)}) collective-permute-start(bf16[2048,256]{1,0:T(8,128)(2,1)S(1)} %collective-permute-done.first_ref.refs_0_), channel_id=1, source_target_pairs={{0,4},{4,0},{1,5},{5,1},{2,6},{6,2},{3,7},{7,3},{8,12},{12,8},{9,1... | collective-permute-start | bytes 3145736 | tf_op jit(solution)/shard_map/ppermute | solution.py:326
  55.3 2.3 %collective-permute-start.3 = (bf16[2048,256]{1,0:T(8,128)(2,1)S(1)}, bf16[2048,256]{1,0:T(8,128)(2,1)}, u32[]{:S(2)}, u32[]{:S(2)}) collective-permute-start(bf16[2048,256]{1,0:T(8,128)(2,1)S(1)} %collective-permute-done.1.second_ref.refs_1_), channel_id=1, source_target_pairs={{0,4},{4,0},{1,5},{5,1},{2,6},{6,2},{3,7},{7,3},{8,12},{12,8},{9,1... | collective-permute-start | bytes 3145736 | tf_op jit(solution)/shard_map/ppermute | solution.py:326
  57.6 2.2 %all-to-all-done.1.u_ref = bf16[32,16,128]{2,1,0:T(8,128)(2,1)S(1)} async-done(((bf16[32,16,128]{2,1,0:T(8,128)(2,1)}), bf16[32,16,128]{2,1,0:T(8,128)(2,1)S(1)}, u32[]{:S(2)}, u32[]{:S(2)}) %all-to-all-start.1) | async-done | bytes 131104 | tf_op jit(solution)/shard_map/all_to_all | solution.py:327
  59.8 0.9 gather.1
  60.6 0.0 collective-permute-done.2.refs_2_
  60.6 0.0 collective-permute-done.3.refs_3_
  60.7 8.3 %krylov.1 = bf16[8,208,128]{2,1,0:T(8,128)(2,1)S(1)} custom-call(s32[2]{0:T(128)S(1)} %pad_add_fusion.idx_ref, f32[1,1]{1,0:T(1,128)} %get-tuple-element.17.norm_ref, f32[32,2048]{1,0:T(8,128)S(1)} %get-tuple-element.24.u_ref, f32[64,512]{1,0:T(8,128)S(1)} %get-tuple-element.25.part_ref, bf16[2048,256]{1,0:T(8,128)(2,1)S(1)} %collective-permute-done.first_ref.refs_0_, ...), custom_call_target="tpu_custom_call" | custom-call | tf_op jit(solution)/shard_map/krylov/pallas_call | solution.py:343
  69.0 12.1 %all_to_all.21 = bf16[8,208,128]{2,1,0:T(8,128)(2,1)S(1)} all-to-all(bf16[8,208,128]{2,1,0:T(8,128)(2,1)S(1)} %krylov.1), channel_id=1, replica_groups=mesh['z'=16,'x'=4,'core'=2,'rcv'=4] {'core','rcv'}, dimensions={0} | all-to-all | bytes 851968 | tf_op jit(solution)/shard_map/all_to_all | solution.py:354
  81.2 1.2 copy.10
  82.4 9.9 %all-to-all-start.3 = ((bf16[64,13,2,128]{3,2,1,0:T(2,128)(2,1)}), bf16[64,13,2,128]{3,2,1,0:T(2,128)(2,1)S(1)}, u32[]{:S(2)}, u32[]{:S(2)}) async-start(bf16[64,13,2,128]{3,2,1,0:T(2,128)(2,1)} %copy.10), calls=%async_computation.3 | async-start | bytes 851968 | tf_op jit(solution)/shard_map/all_to_all | solution.py:359
  92.3 1.6 %table0.1 = (bf16[256,1024]{1,0:T(8,128)(2,1)S(1)}, bf16[256,1024]{1,0:T(8,128)(2,1)S(1)}) custom-call(s32[64,4]{1,0:T(8,128)S(1)} %reshape.35.fr_ref), custom_call_target="tpu_custom_call" | custom-call | tf_op jit(solution)/shard_map/table0/pallas_call | solution.py:304
  94.0 1.6 %table1.1 = (bf16[256,1024]{1,0:T(8,128)(2,1)S(1)}, bf16[256,1024]{1,0:T(8,128)(2,1)S(1)}) custom-call(s32[64,4]{1,0:T(8,128)S(1)} %reshape.35.fr_ref), custom_call_target="tpu_custom_call" | custom-call | tf_op jit(solution)/shard_map/table1/pallas_call | solution.py:304
  95.6 25.6 %all-to-all-done.3 = bf16[64,13,2,128]{3,2,1,0:T(2,128)(2,1)S(1)} async-done(((bf16[64,13,2,128]{3,2,1,0:T(2,128)(2,1)}), bf16[64,13,2,128]{3,2,1,0:T(2,128)(2,1)S(1)}, u32[]{:S(2)}, u32[]{:S(2)}) %all-to-all-start.3) | async-done | bytes 426016 | tf_op jit(solution)/shard_map/all_to_all | solution.py:359
  121.2 0.1 copy.11
  121.3 4.5 %traces.1 = (f32[2,64,1024]{2,1,0:T(8,128)}, f32[2,64,1024]{2,1,0:T(8,128)}) custom-call(bf16[26,64,128]{2,1,0:T(8,128)(2,1)S(1)} %bitcast.16, bf16[256,1024]{1,0:T(8,128)(2,1)S(1)} %get-tuple-element.28.hi0_ref, bf16[256,1024]{1,0:T(8,128)(2,1)S(1)} %get-tuple-element.29.lo0_ref, bf16[256,1024]{1,0:T(8,128)(2,1)S(1)} %get-tuple-element.30.hi1_ref, ...), custom_call_target="tpu_custom_call" | custom-call | tf_op jit(solution)/shard_map/traces/pallas_call | solution.py:362
  (4 shorter events, 0.1 us)
Async XLA Ops:
  3.4 7.4 %copy-start.1 = (s32[256]{0:T(256)S(1)}, s32[256]{0:T(256)}, u32[]{:S(2)}) copy-start(s32[256]{0:T(256)} %param.5) | copy-start | bytes 3076
  3.4 7.5 %copy-start = (f32[2,64,1024]{2,1,0:T(8,128)S(1)}, f32[2,64,1024]{2,1,0:T(8,128)}, u32[]{:S(2)}) copy-start(f32[2,64,1024]{2,1,0:T(8,128)} %param.3) | copy-start | bytes 1572868
  5.4 37.2 %collective-permute-start = (bf16[2048,256]{1,0:T(8,128)(2,1)}, bf16[2048,256]{1,0:T(8,128)(2,1)S(1)}, u32[]{:S(2)}, u32[]{:S(2)}) collective-permute-start(bf16[2048,256]{1,0:T(8,128)(2,1)} %get-tuple-element.19), channel_id=1, source_target_pairs={{0,0},{1,4},{2,1},{3,5},{4,2},{5,6},{6,3},{7,7},{8,8},{9,12},{10,9... | collective-permute-start | bytes 3145736 | tf_op jit(solution)/shard_map/ppermute | solution.py:301
  7.3 35.4 %collective-permute-start.1 = (bf16[2048,256]{1,0:T(8,128)(2,1)}, bf16[2048,256]{1,0:T(8,128)(2,1)S(1)}, u32[]{:S(2)}, u32[]{:S(2)}) collective-permute-start(bf16[2048,256]{1,0:T(8,128)(2,1)} %get-tuple-element.20), channel_id=1, source_target_pairs={{0,1},{1,5},{2,0},{3,4},{4,3},{5,7},{6,2},{7,6},{8,9},{9,13},{10,8... | collective-permute-start | bytes 3145736 | tf_op jit(solution)/shard_map/ppermute | solution.py:301
  43.4 16.4 %all-to-all-start.1 = ((bf16[32,16,128]{2,1,0:T(8,128)(2,1)}), bf16[32,16,128]{2,1,0:T(8,128)(2,1)S(1)}, u32[]{:S(2)}, u32[]{:S(2)}) async-start(bf16[32,16,128]{2,1,0:T(8,128)(2,1)} %bitcast.15), calls=%async_computation.1 | async-start | bytes 262144 | tf_op jit(solution)/shard_map/all_to_all | solution.py:327
  53.3 7.4 %collective-permute-start.2 = (bf16[2048,256]{1,0:T(8,128)(2,1)S(1)}, bf16[2048,256]{1,0:T(8,128)(2,1)S(1)}, u32[]{:S(2)}, u32[]{:S(2)}) collective-permute-start(bf16[2048,256]{1,0:T(8,128)(2,1)S(1)} %collective-permute-done.first_ref.refs_0_), channel_id=1, source_target_pairs={{0,4},{4,0},{1,5},{5,1},{2,6},{6,2},{3,7},{7,3},{8,12},{12,8},{9,1... | collective-permute-start | bytes 3145736 | tf_op jit(solution)/shard_map/ppermute | solution.py:326
  55.3 5.3 %collective-permute-start.3 = (bf16[2048,256]{1,0:T(8,128)(2,1)S(1)}, bf16[2048,256]{1,0:T(8,128)(2,1)}, u32[]{:S(2)}, u32[]{:S(2)}) collective-permute-start(bf16[2048,256]{1,0:T(8,128)(2,1)S(1)} %collective-permute-done.1.second_ref.refs_1_), channel_id=1, source_target_pairs={{0,4},{4,0},{1,5},{5,1},{2,6},{6,2},{3,7},{7,3},{8,12},{12,8},{9,1... | collective-permute-start | bytes 3145736 | tf_op jit(solution)/shard_map/ppermute | solution.py:326
  82.4 38.8 %all-to-all-start.3 = ((bf16[64,13,2,128]{3,2,1,0:T(2,128)(2,1)}), bf16[64,13,2,128]{3,2,1,0:T(2,128)(2,1)S(1)}, u32[]{:S(2)}, u32[]{:S(2)}) async-start(bf16[64,13,2,128]{3,2,1,0:T(2,128)(2,1)} %copy.10), calls=%async_computation.3 | async-start | bytes 851968 | tf_op jit(solution)/shard_map/all_to_all | solution.py:359

commit v7 on v5

--- a/solution.py
+++ b/solution.py
@@ -12,7 +12,7 @@
 Y = 4
 GROUP = 8
 HV = 32
-EXTRA = 16
+EXTRA = 8
 HIGH = lax.Precision.HIGHEST
 MIB = 1024 * 1024
 COLUMN = ("core", "rcv")
@@ -33,19 +33,29 @@
 
 def angles(fr_ref, samples):
     unit = 2.0 * math.pi / samples
-    fr = jnp.concatenate([fr_ref[:, n : n + 1] for n in range(fr_ref.shape[1])], axis=0)
-    lane = lax.broadcasted_iota(jnp.int32, (fr.shape[0], 128), 1)
+    chunks = samples // 128
+    deep, groups = fr_ref.shape
+    fr = jnp.concatenate([fr_ref[:, n : n + 1] for n in range(groups)], axis=0)
+    lane = lax.broadcasted_iota(jnp.int32, (deep * groups, 128), 1)
     fine = (fr * lane & (samples - 1)).astype(jnp.float32) * unit
-    coarse = (fr * (lane * 128) & (samples - 1)).astype(jnp.float32) * unit
+    wide = [jnp.broadcast_to(fr_ref[:, n : n + 1], (deep, chunks)) for n in range(groups)]
+    wide = jnp.concatenate(wide, axis=1)
+    step = lax.rem(lax.broadcasted_iota(jnp.int32, wide.shape, 1), chunks) * 128
+    coarse = (wide * step & (samples - 1)).astype(jnp.float32) * unit
     factor = 1.0 / math.sqrt(samples)
-    return jnp.cos(fine), jnp.sin(fine), jnp.cos(coarse) * factor, jnp.sin(coarse) * factor
+    cos_c, sin_c = jnp.cos(coarse) * factor, jnp.sin(coarse) * factor
+
+    def column(values, a):
+        return jnp.concatenate([values[:, n * chunks + a : n * chunks + a + 1] for n in range(groups)], axis=0)
+
+    pairs = [(column(cos_c, a), column(sin_c, a)) for a in range(chunks)]
+    return jnp.cos(fine), jnp.sin(fine), pairs
 
 
 def table_kernel(p, fr_ref, hi_ref, lo_ref):
     samples = hi_ref.shape[1]
-    cos_f, sin_f, cos_c, sin_c = angles(fr_ref, samples)
-    for a in range(samples // 128):
-        ca, sa = cos_c[:, a : a + 1], sin_c[:, a : a + 1]
+    cos_f, sin_f, pairs = angles(fr_ref, samples)
+    for a, (ca, sa) in enumerate(pairs):
         part = slice(a * 128, (a + 1) * 128)
         value = ca * cos_f - sa * sin_f if p == 0 else -(sa * cos_f + ca * sin_f)
         top = value.astype(jnp.bfloat16)
@@ -56,9 +66,8 @@
 def dft_kernel(fr_ref, rec_ref, out_ref, norm_ref, table, rows):
     deep = fr_ref.shape[0]
     samples = rec_ref.shape[1]
-    cos_f, sin_f, cos_c, sin_c = angles(fr_ref, samples)
-    for a in range(samples // 128):
-        ca, sa = cos_c[:, a : a + 1], sin_c[:, a : a + 1]
+    cos_f, sin_f, pairs = angles(fr_ref, samples)
+    for a, (ca, sa) in enumerate(pairs):
         part = slice(a * 128, (a + 1) * 128)
         table[0, :, part] = ca * cos_f - sa * sin_f
         table[1, :, part] = -(sa * cos_f + ca * sin_f)

time: 123 us -> 123 us (level)
  transfers between devices with their start and end apart: 6 -> 6, of which waited for: 2 -> 2; matrix products, arithmetic and copies ran while one was open for 0% -> 0% of each run, Pallas kernels for 6% -> 5%
where the time goes in v7:
time: 123 us; the launch traced here: 122 us
  blocking collectives  44.8 us (36%)
  starting transfers between devices  26.4 us (21%)
  waiting for transfers between devices  25.5 us (21%)
  Pallas kernels  20.2 us (16%)
  local copies, waits for them, and re-layouts  4.53 us (4%)
    all_to_all x1, blocking collectives, body(): spec = lax.all_to_all(spec, 'z', split_axis=0, concat_axis=0, tiled=True)  28.1 us
    all_to_all x1, waiting for transfers between devices, body(): lax.all_to_all(send, 'z', split_axis=0, concat_axis=0, tiled=True)  23.2 us
    all_to_all x1, blocking collectives, body(): lax.all_to_all(vectors, SLAB, split_axis=0, concat_axis=0, tiled=True)  16.7 us
    all_to_all x1, starting transfers between devices, body(): lax.all_to_all(spec.transpose(1, 0, 2), SLAB, split_axis=0, concat_axis=0...  9.8 us
    pallas_call x1, Pallas kernels, body(): pl.pallas_call(krylov_kernel, out_shape=jax.ShapeDtypeStruct((X * GROUP,...  8.79 us
    all_to_all x1, starting transfers between devices, body(): lax.all_to_all(send, 'z', split_axis=0, concat_axis=0, tiled=True)  6.86 us
    ppermute x2, starting transfers between devices, body(): lax.ppermute(load, COLUMN, route(n))  5.41 us
    ppermute x2, starting transfers between devices, body(): lax.ppermute(b, 'core', [(0, 1), (1, 0)])  4.33 us
  transfers between devices with their start and end apart: 6, of which 2 were waited for; matrix products, arithmetic and copies ran while one was open for 0% of the time, Pallas kernels for 5%

profile of v7, /device:TPU:2, one launch (start us, length us, event | category | flops | bytes accessed | tf_op | source)
XLA Modules:
  0.0 122.4 jit_solution(1283955541852152804)
XLA Ops:
  0.6 2.7 %reshape.27.k_ref = bf16[2,2048,256]{2,1,0:T(8,128)(2,1)S(1)} reshape(bf16[2,1024,2,256]{3,2,1,0:T(2,128)(2,1)} %param.4) | data formatting | bytes 4194304 | tf_op jit(solution)/shard_map/reshape | solution.py:305
  3.4 0.0 copy-start.1
  3.4 0.0 copy-start
  3.4 0.1 pad_add_fusion.idx_ref
  3.5 1.9 %pick.1 = (bf16[2048,256]{1,0:T(8,128)(2,1)}, bf16[2048,256]{1,0:T(8,128)(2,1)}) custom-call(s32[2]{0:T(128)S(1)} %pad_add_fusion.idx_ref, bf16[2,2048,256]{2,1,0:T(8,128)(2,1)S(1)} %reshape.27.k_ref), custom_call_target="tpu_custom_call" | custom-call | tf_op jit(solution)/shard_map/pick/pallas_call | solution.py:297
  5.4 1.9 %collective-permute-start = (bf16[2048,256]{1,0:T(8,128)(2,1)}, bf16[2048,256]{1,0:T(8,128)(2,1)S(1)}, u32[]{:S(2)}, u32[]{:S(2)}) collective-permute-start(bf16[2048,256]{1,0:T(8,128)(2,1)} %get-tuple-element.17), channel_id=1, source_target_pairs={{0,0},{1,4},{2,1},{3,5},{4,2},{5,6},{6,3},{7,7},{8,8},{9,12},{10,9... | collective-permute-start | bytes 3145736 | tf_op jit(solution)/shard_map/ppermute | solution.py:306
  7.3 3.5 %collective-permute-start.1 = (bf16[2048,256]{1,0:T(8,128)(2,1)}, bf16[2048,256]{1,0:T(8,128)(2,1)S(1)}, u32[]{:S(2)}, u32[]{:S(2)}) collective-permute-start(bf16[2048,256]{1,0:T(8,128)(2,1)} %get-tuple-element.18), channel_id=1, source_target_pairs={{0,1},{1,5},{2,0},{3,4},{4,3},{5,7},{6,2},{7,6},{8,9},{9,13},{10,8... | collective-permute-start | bytes 3145736 | tf_op jit(solution)/shard_map/ppermute | solution.py:306
  10.8 0.0 copy-done.1
  10.8 0.1 reshape.24.fr_ref
  10.9 0.0 copy-done
  10.9 3.3 %dft.1 = (bf16[512,128]{1,0:T(8,128)(2,1)S(1)}, f32[1,1]{1,0:T(1,128)}) custom-call(s32[16,16]{1,0:T(8,128)S(1)} %reshape.24.fr_ref, f32[128,1024]{1,0:T(8,128)S(1)} %bitcast.18), custom_call_target="tpu_custom_call" | custom-call | tf_op jit(solution)/shard_map/dft/pallas_call | solution.py:314
  14.2 28.1 %all_to_all.20 = bf16[16,32,128]{2,1,0:T(8,128)(2,1)S(1)} all-to-all(bf16[16,32,128]{2,1,0:T(8,128)(2,1)S(1)} %bitcast.19), channel_id=1, replica_groups=mesh['z'=16,'x'=4,'core'=2,'rcv'=4] {'z'}, dimensions={0} | all-to-all | bytes 262144 | tf_op jit(solution)/shard_map/all_to_all | solution.py:329
  42.3 0.0 collective-permute-done.refs_0_
  42.3 0.0 collective-permute-done.1.refs_1_
  42.3 0.7 copy.17
  43.0 9.8 %all-to-all-start.1 = ((bf16[32,16,128]{2,1,0:T(8,128)(2,1)}), bf16[32,16,128]{2,1,0:T(8,128)(2,1)S(1)}, u32[]{:S(2)}, u32[]{:S(2)}) async-start(bf16[32,16,128]{2,1,0:T(8,128)(2,1)} %bitcast.16), calls=%async_computation.1 | async-start | bytes 262144 | tf_op jit(solution)/shard_map/all_to_all | solution.py:332
  52.8 2.1 %collective-permute-start.2 = (bf16[2048,256]{1,0:T(8,128)(2,1)S(1)}, bf16[2048,256]{1,0:T(8,128)(2,1)S(1)}, u32[]{:S(2)}, u32[]{:S(2)}) collective-permute-start(bf16[2048,256]{1,0:T(8,128)(2,1)S(1)} %collective-permute-done.refs_0_), channel_id=1, source_target_pairs={{0,4},{4,0},{1,5},{5,1},{2,6},{6,2},{3,7},{7,3},{8,12},{12,8},{9,1... | collective-permute-start | bytes 3145736 | tf_op jit(solution)/shard_map/ppermute | solution.py:331
  54.9 2.3 %collective-permute-start.3 = (bf16[2048,256]{1,0:T(8,128)(2,1)S(1)}, bf16[2048,256]{1,0:T(8,128)(2,1)}, u32[]{:S(2)}, u32[]{:S(2)}) collective-permute-start(bf16[2048,256]{1,0:T(8,128)(2,1)S(1)} %collective-permute-done.1.refs_1_), channel_id=1, source_target_pairs={{0,4},{4,0},{1,5},{5,1},{2,6},{6,2},{3,7},{7,3},{8,12},{12,8},{9,1... | collective-permute-start | bytes 3145736 | tf_op jit(solution)/shard_map/ppermute | solution.py:331
  57.1 2.3 %all-to-all-done.1.u_ref = bf16[32,16,128]{2,1,0:T(8,128)(2,1)S(1)} async-done(((bf16[32,16,128]{2,1,0:T(8,128)(2,1)}), bf16[32,16,128]{2,1,0:T(8,128)(2,1)S(1)}, u32[]{:S(2)}, u32[]{:S(2)}) %all-to-all-start.1) | async-done | bytes 131104 | tf_op jit(solution)/shard_map/all_to_all | solution.py:332
  59.4 0.4 gather.1.u_ref
  59.8 0.0 collective-permute-done.2.refs_2_
  59.8 0.0 collective-permute-done.3.refs_3_
  59.8 8.8 %krylov.1 = bf16[32,56,128]{2,1,0:T(8,128)(2,1)S(1)} custom-call(s32[2]{0:T(128)S(1)} %pad_add_fusion.idx_ref, f32[1,1]{1,0:T(1,128)} %get-tuple-element.15.norm_ref, f32[32,2048]{1,0:T(8,128)S(1)} %gather.1.u_ref, bf16[2048,256]{1,0:T(8,128)(2,1)S(1)} %collective-permute-done.refs_0_, bf16[2048,256]{1,0:T(8,128)(2,1)S(1)} %collective-permute-done.1.refs_1_, ...), custom_call_target="tpu_custom_call" | custom-call | tf_op jit(solution)/shard_map/krylov/pallas_call | solution.py:344
  68.6 16.7 %all_to_all.21 = bf16[32,56,128]{2,1,0:T(8,128)(2,1)S(1)} all-to-all(bf16[32,56,128]{2,1,0:T(8,128)(2,1)S(1)} %krylov.1), channel_id=1, replica_groups=mesh['z'=16,'x'=4,'core'=2,'rcv'=4] {'x','core','rcv'}, dimensions={0} | all-to-all | bytes 917504 | tf_op jit(solution)/shard_map/all_to_all | solution.py:355
  85.5 0.9 copy.10
  86.4 6.9 %all-to-all-start.3 = ((bf16[16,104,128]{2,1,0:T(8,128)(2,1)}), bf16[16,104,128]{2,1,0:T(8,128)(2,1)S(1)}, u32[]{:S(2)}, u32[]{:S(2)}) async-start(bf16[16,104,128]{2,1,0:T(8,128)(2,1)} %copy.10), calls=%async_computation.3 | async-start | bytes 851968 | tf_op jit(solution)/shard_map/all_to_all | solution.py:362
  93.2 1.2 table1.1
  94.4 1.2 table0.1
  95.7 23.2 %all-to-all-done.3 = bf16[16,104,128]{2,1,0:T(8,128)(2,1)S(1)} async-done(((bf16[16,104,128]{2,1,0:T(8,128)(2,1)}), bf16[16,104,128]{2,1,0:T(8,128)(2,1)S(1)}, u32[]{:S(2)}, u32[]{:S(2)}) %all-to-all-start.3) | async-done | bytes 426016 | tf_op jit(solution)/shard_map/all_to_all | solution.py:362
  118.8 0.1 copy.16
  118.9 3.5 %traces.1 = (f32[2,64,1024]{2,1,0:T(8,128)}, f32[2,64,1024]{2,1,0:T(8,128)}) custom-call(bf16[104,16,128]{2,1,0:T(8,128)(2,1)S(1)} %bitcast.17, bf16[256,1024]{1,0:T(8,128)(2,1)S(1)} %get-tuple-element.24.hi0_ref, bf16[256,1024]{1,0:T(8,128)(2,1)S(1)} %get-tuple-element.25.lo0_ref, bf16[256,1024]{1,0:T(8,128)(2,1)S(1)} %get-tuple-element.26.hi1_ref, ...), custom_call_target="tpu_custom_call" | custom-call | tf_op jit(solution)/shard_map/traces/pallas_call | solution.py:364
  (6 shorter events, 0.1 us)
Async XLA Ops:
  3.4 7.4 %copy-start.1 = (s32[256]{0:T(256)S(1)}, s32[256]{0:T(256)}, u32[]{:S(2)}) copy-start(s32[256]{0:T(256)} %param.5) | copy-start | bytes 3076
  3.4 7.5 %copy-start = (f32[2,64,1024]{2,1,0:T(8,128)S(1)}, f32[2,64,1024]{2,1,0:T(8,128)}, u32[]{:S(2)}) copy-start(f32[2,64,1024]{2,1,0:T(8,128)} %param.3) | copy-start | bytes 1572868
  5.4 36.9 %collective-permute-start = (bf16[2048,256]{1,0:T(8,128)(2,1)}, bf16[2048,256]{1,0:T(8,128)(2,1)S(1)}, u32[]{:S(2)}, u32[]{:S(2)}) collective-permute-start(bf16[2048,256]{1,0:T(8,128)(2,1)} %get-tuple-element.17), channel_id=1, source_target_pairs={{0,0},{1,4},{2,1},{3,5},{4,2},{5,6},{6,3},{7,7},{8,8},{9,12},{10,9... | collective-permute-start | bytes 3145736 | tf_op jit(solution)/shard_map/ppermute | solution.py:306
  7.3 35.0 %collective-permute-start.1 = (bf16[2048,256]{1,0:T(8,128)(2,1)}, bf16[2048,256]{1,0:T(8,128)(2,1)S(1)}, u32[]{:S(2)}, u32[]{:S(2)}) collective-permute-start(bf16[2048,256]{1,0:T(8,128)(2,1)} %get-tuple-element.18), channel_id=1, source_target_pairs={{0,1},{1,5},{2,0},{3,4},{4,3},{5,7},{6,2},{7,6},{8,9},{9,13},{10,8... | collective-permute-start | bytes 3145736 | tf_op jit(solution)/shard_map/ppermute | solution.py:306
  43.0 16.4 %all-to-all-start.1 = ((bf16[32,16,128]{2,1,0:T(8,128)(2,1)}), bf16[32,16,128]{2,1,0:T(8,128)(2,1)S(1)}, u32[]{:S(2)}, u32[]{:S(2)}) async-start(bf16[32,16,128]{2,1,0:T(8,128)(2,1)} %bitcast.16), calls=%async_computation.1 | async-start | bytes 262144 | tf_op jit(solution)/shard_map/all_to_all | solution.py:332
  52.8 7.0 %collective-permute-start.2 = (bf16[2048,256]{1,0:T(8,128)(2,1)S(1)}, bf16[2048,256]{1,0:T(8,128)(2,1)S(1)}, u32[]{:S(2)}, u32[]{:S(2)}) collective-permute-start(bf16[2048,256]{1,0:T(8,128)(2,1)S(1)} %collective-permute-done.refs_0_), channel_id=1, source_target_pairs={{0,4},{4,0},{1,5},{5,1},{2,6},{6,2},{3,7},{7,3},{8,12},{12,8},{9,1... | collective-permute-start | bytes 3145736 | tf_op jit(solution)/shard_map/ppermute | solution.py:331
  54.9 4.9 %collective-permute-start.3 = (bf16[2048,256]{1,0:T(8,128)(2,1)S(1)}, bf16[2048,256]{1,0:T(8,128)(2,1)}, u32[]{:S(2)}, u32[]{:S(2)}) collective-permute-start(bf16[2048,256]{1,0:T(8,128)(2,1)S(1)} %collective-permute-done.1.refs_1_), channel_id=1, source_target_pairs={{0,4},{4,0},{1,5},{5,1},{2,6},{6,2},{3,7},{7,3},{8,12},{12,8},{9,1... | collective-permute-start | bytes 3145736 | tf_op jit(solution)/shard_map/ppermute | solution.py:331
  86.4 32.5 %all-to-all-start.3 = ((bf16[16,104,128]{2,1,0:T(8,128)(2,1)}), bf16[16,104,128]{2,1,0:T(8,128)(2,1)S(1)}, u32[]{:S(2)}, u32[]{:S(2)}) async-start(bf16[16,104,128]{2,1,0:T(8,128)(2,1)} %copy.10), calls=%async_computation.3 | async-start | bytes 851968 | tf_op jit(solution)/shard_map/all_to_all | solution.py:362

commit v8 on v7

--- a/solution.py
+++ b/solution.py
@@ -12,7 +12,7 @@
 Y = 4
 GROUP = 8
 HV = 32
-EXTRA = 8
+EXTRA = 16
 HIGH = lax.Precision.HIGHEST
 MIB = 1024 * 1024
 COLUMN = ("core", "rcv")

time: 123 us -> 123 us (level)
  no operation moved by 1% of the time
where the time goes in v8:
time: 123 us
  blocking collectives  45.4 us (37%)
  starting transfers between devices  26.4 us (21%)
  waiting for transfers between devices  25.4 us (21%)
  Pallas kernels  20.2 us (16%)
  local copies, waits for them, and re-layouts  4.55 us (4%)
    all_to_all x1, blocking collectives, body(): spec = lax.all_to_all(spec, 'z', split_axis=0, concat_axis=0, tiled=True)  28.1 us
    all_to_all x1, waiting for transfers between devices, body(): lax.all_to_all(send, 'z', split_axis=0, concat_axis=0, tiled=True)  23.2 us
    all_to_all x1, blocking collectives, body(): lax.all_to_all(vectors, SLAB, split_axis=0, concat_axis=0, tiled=True)  17.3 us
    all_to_all x1, starting transfers between devices, body(): lax.all_to_all(spec.transpose(1, 0, 2), SLAB, split_axis=0, concat_axis=0...  9.8 us
    pallas_call x1, Pallas kernels, body(): pl.pallas_call(krylov_kernel, out_shape=jax.ShapeDtypeStruct((X * GROUP,...  8.78 us
    all_to_all x1, starting transfers between devices, body(): lax.all_to_all(send, 'z', split_axis=0, concat_axis=0, tiled=True)  6.86 us
    ppermute x2, starting transfers between devices, body(): lax.ppermute(load, COLUMN, route(n))  5.41 us
    ppermute x2, starting transfers between devices, body(): lax.ppermute(b, 'core', [(0, 1), (1, 0)])  4.33 us
  transfers between devices with their start and end apart: 6, of which 2 were waited for; matrix products, arithmetic and copies ran while one was open for 0% of the time, Pallas kernels for 5%

profile of v8, /device:TPU:2, one launch (start us, length us, event | category | flops | bytes accessed | tf_op | source)
XLA Modules:
  0.0 122.9 jit_solution(8474605898410958111)
XLA Ops:
  0.6 2.7 %reshape.27.k_ref = bf16[2,2048,256]{2,1,0:T(8,128)(2,1)S(1)} reshape(bf16[2,1024,2,256]{3,2,1,0:T(2,128)(2,1)} %param.4) | data formatting | bytes 4194304 | tf_op jit(solution)/shard_map/reshape | solution.py:305
  3.4 0.0 copy-start.1
  3.4 0.0 copy-start
  3.4 0.1 pad_add_fusion.idx_ref
  3.5 1.9 %pick.1 = (bf16[2048,256]{1,0:T(8,128)(2,1)}, bf16[2048,256]{1,0:T(8,128)(2,1)}) custom-call(s32[2]{0:T(128)S(1)} %pad_add_fusion.idx_ref, bf16[2,2048,256]{2,1,0:T(8,128)(2,1)S(1)} %reshape.27.k_ref), custom_call_target="tpu_custom_call" | custom-call | tf_op jit(solution)/shard_map/pick/pallas_call | solution.py:297
  5.4 1.9 %collective-permute-start = (bf16[2048,256]{1,0:T(8,128)(2,1)}, bf16[2048,256]{1,0:T(8,128)(2,1)S(1)}, u32[]{:S(2)}, u32[]{:S(2)}) collective-permute-start(bf16[2048,256]{1,0:T(8,128)(2,1)} %get-tuple-element.17), channel_id=1, source_target_pairs={{0,0},{1,4},{2,1},{3,5},{4,2},{5,6},{6,3},{7,7},{8,8},{9,12},{10,9... | collective-permute-start | bytes 3145736 | tf_op jit(solution)/shard_map/ppermute | solution.py:306
  7.3 3.5 %collective-permute-start.1 = (bf16[2048,256]{1,0:T(8,128)(2,1)}, bf16[2048,256]{1,0:T(8,128)(2,1)S(1)}, u32[]{:S(2)}, u32[]{:S(2)}) collective-permute-start(bf16[2048,256]{1,0:T(8,128)(2,1)} %get-tuple-element.18), channel_id=1, source_target_pairs={{0,1},{1,5},{2,0},{3,4},{4,3},{5,7},{6,2},{7,6},{8,9},{9,13},{10,8... | collective-permute-start | bytes 3145736 | tf_op jit(solution)/shard_map/ppermute | solution.py:306
  10.8 0.0 copy-done.1
  10.8 0.1 reshape.24.fr_ref
  10.9 0.0 copy-done
  10.9 3.3 %dft.1 = (bf16[512,128]{1,0:T(8,128)(2,1)S(1)}, f32[1,1]{1,0:T(1,128)}) custom-call(s32[16,16]{1,0:T(8,128)S(1)} %reshape.24.fr_ref, f32[128,1024]{1,0:T(8,128)S(1)} %bitcast.18), custom_call_target="tpu_custom_call" | custom-call | tf_op jit(solution)/shard_map/dft/pallas_call | solution.py:314
  14.2 28.1 %all_to_all.20 = bf16[16,32,128]{2,1,0:T(8,128)(2,1)S(1)} all-to-all(bf16[16,32,128]{2,1,0:T(8,128)(2,1)S(1)} %bitcast.19), channel_id=1, replica_groups=mesh['z'=16,'x'=4,'core'=2,'rcv'=4] {'z'}, dimensions={0} | all-to-all | bytes 262144 | tf_op jit(solution)/shard_map/all_to_all | solution.py:329
  42.3 0.0 collective-permute-done.refs_0_
  42.3 0.0 collective-permute-done.1.refs_1_
  42.3 0.7 copy.17
  43.0 9.8 %all-to-all-start.1 = ((bf16[32,16,128]{2,1,0:T(8,128)(2,1)}), bf16[32,16,128]{2,1,0:T(8,128)(2,1)S(1)}, u32[]{:S(2)}, u32[]{:S(2)}) async-start(bf16[32,16,128]{2,1,0:T(8,128)(2,1)} %bitcast.16), calls=%async_computation.1 | async-start | bytes 262144 | tf_op jit(solution)/shard_map/all_to_all | solution.py:332
  52.8 2.1 %collective-permute-start.2 = (bf16[2048,256]{1,0:T(8,128)(2,1)S(1)}, bf16[2048,256]{1,0:T(8,128)(2,1)S(1)}, u32[]{:S(2)}, u32[]{:S(2)}) collective-permute-start(bf16[2048,256]{1,0:T(8,128)(2,1)S(1)} %collective-permute-done.refs_0_), channel_id=1, source_target_pairs={{0,4},{4,0},{1,5},{5,1},{2,6},{6,2},{3,7},{7,3},{8,12},{12,8},{9,1... | collective-permute-start | bytes 3145736 | tf_op jit(solution)/shard_map/ppermute | solution.py:331
  54.9 2.3 %collective-permute-start.3 = (bf16[2048,256]{1,0:T(8,128)(2,1)S(1)}, bf16[2048,256]{1,0:T(8,128)(2,1)}, u32[]{:S(2)}, u32[]{:S(2)}) collective-permute-start(bf16[2048,256]{1,0:T(8,128)(2,1)S(1)} %collective-permute-done.1.refs_1_), channel_id=1, source_target_pairs={{0,4},{4,0},{1,5},{5,1},{2,6},{6,2},{3,7},{7,3},{8,12},{12,8},{9,1... | collective-permute-start | bytes 3145736 | tf_op jit(solution)/shard_map/ppermute | solution.py:331
  57.1 2.3 %all-to-all-done.1.u_ref = bf16[32,16,128]{2,1,0:T(8,128)(2,1)S(1)} async-done(((bf16[32,16,128]{2,1,0:T(8,128)(2,1)}), bf16[32,16,128]{2,1,0:T(8,128)(2,1)S(1)}, u32[]{:S(2)}, u32[]{:S(2)}) %all-to-all-start.1) | async-done | bytes 131104 | tf_op jit(solution)/shard_map/all_to_all | solution.py:332
  59.4 0.4 gather.1.u_ref
  59.8 0.0 collective-permute-done.2.refs_2_
  59.8 0.0 collective-permute-done.3.refs_3_
  59.8 8.8 %krylov.1 = bf16[32,64,128]{2,1,0:T(8,128)(2,1)S(1)} custom-call(s32[2]{0:T(128)S(1)} %pad_add_fusion.idx_ref, f32[1,1]{1,0:T(1,128)} %get-tuple-element.15.norm_ref, f32[32,2048]{1,0:T(8,128)S(1)} %gather.1.u_ref, bf16[2048,256]{1,0:T(8,128)(2,1)S(1)} %collective-permute-done.refs_0_, bf16[2048,256]{1,0:T(8,128)(2,1)S(1)} %collective-permute-done.1.refs_1_, ...), custom_call_target="tpu_custom_call" | custom-call | tf_op jit(solution)/shard_map/krylov/pallas_call | solution.py:344
  68.6 17.3 %all_to_all.21 = bf16[32,64,128]{2,1,0:T(8,128)(2,1)S(1)} all-to-all(bf16[32,64,128]{2,1,0:T(8,128)(2,1)S(1)} %krylov.1), channel_id=1, replica_groups=mesh['z'=16,'x'=4,'core'=2,'rcv'=4] {'x','core','rcv'}, dimensions={0} | all-to-all | bytes 1048576 | tf_op jit(solution)/shard_map/all_to_all | solution.py:355
  86.1 0.9 copy.10
  86.9 6.9 %all-to-all-start.3 = ((bf16[16,104,128]{2,1,0:T(8,128)(2,1)}), bf16[16,104,128]{2,1,0:T(8,128)(2,1)S(1)}, u32[]{:S(2)}, u32[]{:S(2)}) async-start(bf16[16,104,128]{2,1,0:T(8,128)(2,1)} %copy.10), calls=%async_computation.3 | async-start | bytes 851968 | tf_op jit(solution)/shard_map/all_to_all | solution.py:362
  93.8 1.2 table1.1
  95.0 1.2 table0.1
  96.2 23.2 %all-to-all-done.3 = bf16[16,104,128]{2,1,0:T(8,128)(2,1)S(1)} async-done(((bf16[16,104,128]{2,1,0:T(8,128)(2,1)}), bf16[16,104,128]{2,1,0:T(8,128)(2,1)S(1)}, u32[]{:S(2)}, u32[]{:S(2)}) %all-to-all-start.3) | async-done | bytes 426016 | tf_op jit(solution)/shard_map/all_to_all | solution.py:362
  119.4 0.1 copy.16
  119.5 3.5 %traces.1 = (f32[2,64,1024]{2,1,0:T(8,128)}, f32[2,64,1024]{2,1,0:T(8,128)}) custom-call(bf16[104,16,128]{2,1,0:T(8,128)(2,1)S(1)} %bitcast.17, bf16[256,1024]{1,0:T(8,128)(2,1)S(1)} %get-tuple-element.24.hi0_ref, bf16[256,1024]{1,0:T(8,128)(2,1)S(1)} %get-tuple-element.25.lo0_ref, bf16[256,1024]{1,0:T(8,128)(2,1)S(1)} %get-tuple-element.26.hi1_ref, ...), custom_call_target="tpu_custom_call" | custom-call | tf_op jit(solution)/shard_map/traces/pallas_call | solution.py:364
  (6 shorter events, 0.1 us)
Async XLA Ops:
  3.4 7.4 %copy-start.1 = (s32[256]{0:T(256)S(1)}, s32[256]{0:T(256)}, u32[]{:S(2)}) copy-start(s32[256]{0:T(256)} %param.5) | copy-start | bytes 3076
  3.4 7.5 %copy-start = (f32[2,64,1024]{2,1,0:T(8,128)S(1)}, f32[2,64,1024]{2,1,0:T(8,128)}, u32[]{:S(2)}) copy-start(f32[2,64,1024]{2,1,0:T(8,128)} %param.3) | copy-start | bytes 1572868
  5.4 36.9 %collective-permute-start = (bf16[2048,256]{1,0:T(8,128)(2,1)}, bf16[2048,256]{1,0:T(8,128)(2,1)S(1)}, u32[]{:S(2)}, u32[]{:S(2)}) collective-permute-start(bf16[2048,256]{1,0:T(8,128)(2,1)} %get-tuple-element.17), channel_id=1, source_target_pairs={{0,0},{1,4},{2,1},{3,5},{4,2},{5,6},{6,3},{7,7},{8,8},{9,12},{10,9... | collective-permute-start | bytes 3145736 | tf_op jit(solution)/shard_map/ppermute | solution.py:306
  7.3 35.0 %collective-permute-start.1 = (bf16[2048,256]{1,0:T(8,128)(2,1)}, bf16[2048,256]{1,0:T(8,128)(2,1)S(1)}, u32[]{:S(2)}, u32[]{:S(2)}) collective-permute-start(bf16[2048,256]{1,0:T(8,128)(2,1)} %get-tuple-element.18), channel_id=1, source_target_pairs={{0,1},{1,5},{2,0},{3,4},{4,3},{5,7},{6,2},{7,6},{8,9},{9,13},{10,8... | collective-permute-start | bytes 3145736 | tf_op jit(solution)/shard_map/ppermute | solution.py:306
  43.0 16.4 %all-to-all-start.1 = ((bf16[32,16,128]{2,1,0:T(8,128)(2,1)}), bf16[32,16,128]{2,1,0:T(8,128)(2,1)S(1)}, u32[]{:S(2)}, u32[]{:S(2)}) async-start(bf16[32,16,128]{2,1,0:T(8,128)(2,1)} %bitcast.16), calls=%async_computation.1 | async-start | bytes 262144 | tf_op jit(solution)/shard_map/all_to_all | solution.py:332
  52.8 7.0 %collective-permute-start.2 = (bf16[2048,256]{1,0:T(8,128)(2,1)S(1)}, bf16[2048,256]{1,0:T(8,128)(2,1)S(1)}, u32[]{:S(2)}, u32[]{:S(2)}) collective-permute-start(bf16[2048,256]{1,0:T(8,128)(2,1)S(1)} %collective-permute-done.refs_0_), channel_id=1, source_target_pairs={{0,4},{4,0},{1,5},{5,1},{2,6},{6,2},{3,7},{7,3},{8,12},{12,8},{9,1... | collective-permute-start | bytes 3145736 | tf_op jit(solution)/shard_map/ppermute | solution.py:331
  54.9 4.9 %collective-permute-start.3 = (bf16[2048,256]{1,0:T(8,128)(2,1)S(1)}, bf16[2048,256]{1,0:T(8,128)(2,1)}, u32[]{:S(2)}, u32[]{:S(2)}) collective-permute-start(bf16[2048,256]{1,0:T(8,128)(2,1)S(1)} %collective-permute-done.1.refs_1_), channel_id=1, source_target_pairs={{0,4},{4,0},{1,5},{5,1},{2,6},{6,2},{3,7},{7,3},{8,12},{12,8},{9,1... | collective-permute-start | bytes 3145736 | tf_op jit(solution)/shard_map/ppermute | solution.py:331
  86.9 32.5 %all-to-all-start.3 = ((bf16[16,104,128]{2,1,0:T(8,128)(2,1)}), bf16[16,104,128]{2,1,0:T(8,128)(2,1)S(1)}, u32[]{:S(2)}, u32[]{:S(2)}) async-start(bf16[16,104,128]{2,1,0:T(8,128)(2,1)} %copy.10), calls=%async_computation.3 | async-start | bytes 851968 | tf_op jit(solution)/shard_map/all_to_all | solution.py:362
